TPU v7x, 128 devices: a whole 4x4x4 slice. The times are simulated.
128 devices in a mesh: wide: 16 (over z, y_lo, core), narrow: 8 (over x, y_hi).
Axes of the slice: x: 4, y: 4 (y_hi: 2, y_lo: 2; y = y_hi * 2 + y_lo), z: 4, core: 2. Of those that a mesh axis runs over, the one named last changes fastest.
Arguments:
- inputs: bfloat16 [2, 16, 1024, 768], P(None, 'wide', 'narrow'), may hold values from -9 to 9
- lengths: int32 [2, 16], P(None, 'wide'), may hold values from 102 to 1024, as said below
- norm_params: bfloat16 [2, 4, 768], P(None, None, ('wide', 'narrow')), may hold values from -2 to 2.203125, as said below
- attn_in: bfloat16 [2, 768, 2304], P(None, ('wide', 'narrow')), may hold values from -0.21875 to 0.21875
- attn_out: bfloat16 [2, 768, 768], P(None, ('wide', 'narrow')), may hold values from -1.25 to 1.25
- mlp_in: bfloat16 [2, 768, 3072], P(None, 'narrow', 'wide'), may hold values from -0.21875 to 0.21875
- mlp_out: bfloat16 [2, 3072, 768], P(None, 'wide', 'narrow'), may hold values from -0.21875 to 0.21875
- cotangent: bfloat16 [2, 16, 1024, 768], P(None, 'wide', 'narrow'), may hold values from -6 to 6
Outputs:
- outputs: float32 [2, 16, 1024, 768], P(None, 'wide', 'narrow')
- grad_inputs: float32 [2, 16, 1024, 768], P(None, 'wide', 'narrow')
- grad_norm_params: float32 [2, 4, 768], P(None, None, ('wide', 'narrow'))
- grad_attn_in: float32 [2, 768, 2304], P(None, ('wide', 'narrow'))
- grad_attn_out: float32 [2, 768, 768], P(None, ('wide', 'narrow'))
- grad_mlp_in: float32 [2, 768, 3072], P(None, 'narrow', 'wide')
- grad_mlp_out: float32 [2, 3072, 768], P(None, 'wide', 'narrow')
Inputs may be any that keep to these rules, and one draw needn't show every extreme that they name: `lengths`: among the 2 clips that share an index of wide, one has 1024 patches; one clip has 102. `norm_params`: rows 0 and 2 of each layer are gains, rows 1 and 3 biases.
All inputs are finite; a program needn't handle non-finite values.
Results may differ from a plain program's by a relative error of at most 0.02.
Values may be sent and summed in bfloat16 or wider, within the bound.
No kernel may reach another device: no remote copies, remote signals or barrier semaphores. Data moves between devices by JAX's collectives and lax.ppermute only.
A program may use at most 256 MiB of HBM per device.

v0:
```python
import jax
import jax.numpy as jnp
from jax import lax
from jax.sharding import PartitionSpec as P

HEADS = 12
HEAD_DIM = 64


EPS = 1e-06
ROOT_HALF = 0.7071067811865476


def in_one_piece(arrays, axis, dim, along):
    widths = [a.shape[along] for a in arrays]
    both = jnp.concatenate(arrays, axis=along)
    out = lax.all_gather(both, axis, axis=dim, tiled=True)
    return tuple(jnp.split(out, [sum(widths[:k]) for k in range(1, len(widths))], axis=along))


def in_one_piece_2(arrays, axis, dim, along):
    widths = [a.shape[along] for a in arrays]
    both = jnp.concatenate(arrays, axis=along)
    out = lax.psum_scatter(both, axis, scatter_dimension=dim, tiled=True)
    return tuple(jnp.split(out, [sum(widths[:k]) for k in range(1, len(widths))], axis=along))


def norm_rows(values, gain_row, offset_row):
    average = jnp.mean(values, -1, keepdims=True)
    centred = values - average
    spread = jnp.mean(centred * centred, -1, keepdims=True)
    return centred * lax.rsqrt(spread + EPS) * gain_row + offset_row


def gelu_exact(values):
    return 0.5 * values * (1.0 + jax.scipy.special.erf(values * ROOT_HALF))


def matmul(left_mat, right_mat):
    return jnp.dot(left_mat, right_mat, preferred_element_type=jnp.float32)


def left_trans(left_mat, right_mat):
    return lax.dot_general(
        left_mat, right_mat, (((0,), (0,)), ((), ())), preferred_element_type=jnp.float32
    )


def right_trans(left_mat, right_mat):
    return lax.dot_general(
        left_mat, right_mat, (((1,), (1,)), ((), ())), preferred_element_type=jnp.float32
    )


def head_group():
    return 4


def group_scores(query_part, key_part, key_valid):
    scores = jnp.einsum("cqhe,ckhe->chqk", query_part, key_part, preferred_element_type=jnp.float32)
    scores = scores * HEAD_DIM ** (-0.5)
    return jnp.where(key_valid[:, None, None, :], scores, -1e30)


def attend_forward(queries, keys_all, values_all, key_valid):
    group_size = head_group()
    outputs = []
    sums_log = []
    for first_head in range(0, HEADS, group_size):
        head_range = slice(first_head, first_head + group_size)
        scores = group_scores(queries[:, :, head_range], keys_all[:, :, head_range], key_valid)
        row_peak = jnp.max(scores, -1, keepdims=True)
        expont = jnp.exp(scores - row_peak)
        row_total = jnp.sum(expont, -1, keepdims=True)
        attn_probs = (expont / row_total).astype(jnp.bfloat16)
        outputs.append(
            jnp.einsum(
                "chqk,ckhe->cqhe",
                attn_probs,
                values_all[:, :, head_range],
                preferred_element_type=jnp.float32,
            )
        )
        sums_log.append(row_peak + jnp.log(row_total))
    return (jnp.concatenate(outputs, 2), jnp.concatenate(sums_log, 1))


def attend_backward(queries, keys_all, values_all, key_valid, sums_log, grad_attended):
    group_size = head_group()
    score_scale = HEAD_DIM ** (-0.5)
    grad_query_parts = []
    grad_key_parts = []
    grad_value_parts = []
    for first_head in range(0, HEADS, group_size):
        head_range = slice(first_head, first_head + group_size)
        query_part = queries[:, :, head_range]
        key_part = keys_all[:, :, head_range]
        value_part = values_all[:, :, head_range]
        grad_part = grad_attended[:, :, head_range]
        scores = group_scores(query_part, key_part, key_valid)
        attn_probs = jnp.where(
            key_valid[:, None, None, :], jnp.exp(scores - sums_log[:, head_range]), 0.0
        )
        probs_low = attn_probs.astype(jnp.bfloat16)
        grad_value_parts.append(
            jnp.einsum("chqk,cqhe->ckhe", probs_low, grad_part, preferred_element_type=jnp.float32)
        )
        grad_probs = jnp.einsum(
            "cqhe,ckhe->chqk", grad_part, value_part, preferred_element_type=jnp.float32
        )
        grad_scores = attn_probs * (
            grad_probs - jnp.sum(grad_probs * attn_probs, -1, keepdims=True)
        )
        grad_scores = grad_scores.astype(jnp.bfloat16)
        grad_query_parts.append(
            jnp.einsum("chqk,ckhe->cqhe", grad_scores, key_part, preferred_element_type=jnp.float32)
            * score_scale
        )
        grad_key_parts.append(
            jnp.einsum(
                "chqk,cqhe->ckhe", grad_scores, query_part, preferred_element_type=jnp.float32
            )
            * score_scale
        )
    return (
        jnp.concatenate(grad_query_parts, 2),
        jnp.concatenate(grad_key_parts, 2),
        jnp.concatenate(grad_value_parts, 2),
    )


def body(inputs, lengths, norm_params, attn_in, attn_out, mlp_in, mlp_out, cotangent):
    micro_count, clip_count, row_count, width_all = inputs.shape
    layer_count = attn_in.shape[0]
    token_rows = clip_count * row_count
    narrow_count = lax.axis_size("narrow")
    whole_len = row_count * narrow_count
    key_slots = jnp.arange(whole_len, dtype=jnp.int32)
    head_shape = (clip_count, row_count, HEADS, HEAD_DIM)
    full_shape = (clip_count, whole_len, HEADS, HEAD_DIM)
    norm_table, qkv_weight, proj_weight = (
        lax.all_gather(norm_params, ("wide", "narrow"), axis=2, tiled=True),
        lax.all_gather(attn_in, ("wide", "narrow"), axis=1, tiled=True),
        lax.all_gather(attn_out, ("wide", "narrow"), axis=1, tiled=True),
    )
    norm_gains = norm_table.astype(jnp.float32)
    first_weight, second_weight = (
        lax.all_gather(mlp_in, "narrow", axis=1, tiled=True),
        lax.all_gather(mlp_out, "narrow", axis=2, tiled=True),
    )
    first_weight, second_weight = (
        lax.all_gather(first_weight, "wide", axis=2, tiled=True),
        lax.all_gather(second_weight, "wide", axis=1, tiled=True),
    )
    grad_norms = jnp.zeros(norm_gains.shape, jnp.float32)
    grad_qkv = jnp.zeros(qkv_weight.shape, jnp.float32)
    grad_proj = jnp.zeros(proj_weight.shape, jnp.float32)
    grad_first = jnp.zeros(first_weight.shape, jnp.float32)
    grad_second = jnp.zeros(second_weight.shape, jnp.float32)
    outputs_all = []
    grads_all = []
    for micro_index in range(micro_count):
        key_valid = key_slots[None, :] < lengths[micro_index][:, None]
        hidden = inputs[micro_index].reshape(token_rows, width_all).astype(jnp.float32)
        records = []
        for layer_index in range(layer_count):
            normed_one = norm_rows(hidden, norm_gains[layer_index, 0], norm_gains[layer_index, 1])
            normed_one = normed_one.astype(jnp.bfloat16)
            projected = matmul(normed_one, qkv_weight[layer_index]).astype(jnp.bfloat16)
            queries = projected[:, :width_all].reshape(head_shape)
            key_local = projected[:, width_all : 2 * width_all].reshape(
                clip_count, row_count, width_all
            )
            value_local = projected[:, 2 * width_all :].reshape(clip_count, row_count, width_all)
            keys_all, values_all = in_one_piece((key_local, value_local), "narrow", 1, 0)
            keys_all = keys_all.reshape(full_shape)
            values_all = values_all.reshape(full_shape)
            attended, sums_log = attend_forward(queries, keys_all, values_all, key_valid)
            attended = attended.reshape(token_rows, width_all).astype(jnp.bfloat16)
            after_attn = hidden + matmul(attended, proj_weight[layer_index])
            normed_two = norm_rows(
                after_attn, norm_gains[layer_index, 2], norm_gains[layer_index, 3]
            )
            normed_two = normed_two.astype(jnp.bfloat16)
            rows_mlp = normed_two
            before_act = matmul(rows_mlp, first_weight[layer_index])
            activated = gelu_exact(before_act).astype(jnp.bfloat16)
            branch_out = matmul(activated, second_weight[layer_index])
            records.append(
                (
                    hidden,
                    normed_one,
                    queries,
                    keys_all,
                    values_all,
                    sums_log,
                    attended,
                    after_attn,
                    rows_mlp,
                    before_act,
                    activated,
                )
            )
            hidden = after_attn + branch_out
        outputs_all.append(hidden.reshape(clip_count, row_count, width_all))
        grad_stream = cotangent[micro_index].reshape(token_rows, width_all).astype(jnp.float32)
        for layer_index in reversed(range(layer_count)):
            (
                layer_input,
                normed_one,
                queries,
                keys_all,
                values_all,
                sums_log,
                attended,
                after_attn,
                rows_mlp,
                before_act,
                activated,
            ) = records[layer_index]
            grad_low = grad_stream.astype(jnp.bfloat16)
            grad_second = grad_second.at[layer_index].add(left_trans(activated, grad_low))
            grad_act = right_trans(grad_low, second_weight[layer_index])
            grad_before = jax.vjp(gelu_exact, before_act)[1](grad_act)[0].astype(jnp.bfloat16)
            grad_first = grad_first.at[layer_index].add(left_trans(rows_mlp, grad_before))
            grad_normed = right_trans(grad_before, first_weight[layer_index])
            norm_pull = jax.vjp(
                norm_rows, after_attn, norm_gains[layer_index, 2], norm_gains[layer_index, 3]
            )[1]
            grad_after, grad_gain, grad_offset = norm_pull(grad_normed)
            grad_norms = (
                grad_norms.at[layer_index, 2].add(grad_gain).at[layer_index, 3].add(grad_offset)
            )
            grad_mid = grad_stream + grad_after
            grad_mid_low = grad_mid.astype(jnp.bfloat16)
            grad_proj = grad_proj.at[layer_index].add(left_trans(attended, grad_mid_low))
            grad_attended = right_trans(grad_mid_low, proj_weight[layer_index]).astype(jnp.bfloat16)
            grad_queries, grad_keys_all, grad_values_all = attend_backward(
                queries,
                keys_all,
                values_all,
                key_valid,
                sums_log,
                grad_attended.reshape(head_shape),
            )
            grad_keys, grad_values = tuple(
                (
                    part.astype(jnp.float32)
                    for part in in_one_piece_2(
                        (
                            grad_keys_all.reshape(clip_count, whole_len, width_all).astype(
                                jnp.bfloat16
                            ),
                            grad_values_all.reshape(clip_count, whole_len, width_all).astype(
                                jnp.bfloat16
                            ),
                        ),
                        "narrow",
                        1,
                        0,
                    )
                )
            )
            grad_projected = jnp.concatenate(
                [
                    grad_queries.reshape(token_rows, width_all).astype(jnp.bfloat16),
                    grad_keys.reshape(token_rows, width_all).astype(jnp.bfloat16),
                    grad_values.reshape(token_rows, width_all).astype(jnp.bfloat16),
                ],
                1,
            )
            grad_qkv = grad_qkv.at[layer_index].add(left_trans(normed_one, grad_projected))
            grad_normed_one = right_trans(grad_projected, qkv_weight[layer_index])
            norm_pull = jax.vjp(
                norm_rows, layer_input, norm_gains[layer_index, 0], norm_gains[layer_index, 1]
            )[1]
            grad_input, grad_gain, grad_offset = norm_pull(grad_normed_one)
            grad_norms = (
                grad_norms.at[layer_index, 0].add(grad_gain).at[layer_index, 1].add(grad_offset)
            )
            grad_stream = grad_mid + grad_input
        grads_all.append(grad_stream.reshape(clip_count, row_count, width_all))
    grad_norms, grad_qkv, grad_proj = (
        lax.psum_scatter(grad_norms, ("wide", "narrow"), scatter_dimension=2, tiled=True),
        lax.psum_scatter(grad_qkv, ("wide", "narrow"), scatter_dimension=1, tiled=True),
        lax.psum_scatter(grad_proj, ("wide", "narrow"), scatter_dimension=1, tiled=True),
    )
    grad_first, grad_second = (
        lax.psum_scatter(
            grad_first.astype(jnp.bfloat16), "wide", scatter_dimension=2, tiled=True
        ).astype(jnp.float32),
        lax.psum_scatter(
            grad_second.astype(jnp.bfloat16), "wide", scatter_dimension=1, tiled=True
        ).astype(jnp.float32),
    )
    grad_first, grad_second = (
        lax.psum_scatter(
            grad_first.astype(jnp.bfloat16), "narrow", scatter_dimension=1, tiled=True
        ).astype(jnp.float32),
        lax.psum_scatter(
            grad_second.astype(jnp.bfloat16), "narrow", scatter_dimension=2, tiled=True
        ).astype(jnp.float32),
    )
    return (
        jnp.stack(outputs_all),
        jnp.stack(grads_all),
        grad_norms,
        grad_qkv,
        grad_proj,
        grad_first,
        grad_second,
    )


def solution(mesh):
    in_specs = (
        P(None, "wide", "narrow", None),
        P(None, "wide"),
        P(None, None, ("wide", "narrow")),
        P(None, ("wide", "narrow"), None),
        P(None, ("wide", "narrow"), None),
        P(None, "narrow", "wide"),
        P(None, "wide", "narrow"),
        P(None, "wide", "narrow", None),
    )
    out_specs = (
        P(None, "wide", "narrow", None),
        P(None, "wide", "narrow", None),
        P(None, None, ("wide", "narrow")),
        P(None, ("wide", "narrow"), None),
        P(None, ("wide", "narrow"), None),
        P(None, "narrow", "wide"),
        P(None, "wide", "narrow"),
    )
    return jax.shard_map(body, mesh=mesh, in_specs=in_specs, out_specs=out_specs, check_vma=False)
```

profile of v0, /device:TPU:0, one launch (start us, length us, event | category | flops | bytes accessed | tf_op | source)
XLA Modules:
  0.0 2180.1 jit_solution(4594474166655497744)
XLA Ops:
  9.7 35.7 %all_gather.37 = bf16[2,768,192]{2,0,1:T(2,128)(2,1)S(1)} all-gather(bf16[2,96,192]{2,0,1:T(2,128)(2,1)S(1)} %copy.148), channel_id=1, replica_groups=mesh['wide'=16,'narrow'=8] {'narrow'}, dimensions={1}, use_global_device_ids=true | all-gather | bytes 663552 | tf_op jit(solution)/shard_map/all_gather | solution.py:148
  47.9 315.5 %all_gather.33 = bf16[2,4,768]{1,0,2:T(2,128)(2,1)S(1)} all-gather(bf16[2,4,6]{1,0,2:T(2,128)(2,1)S(1)} %copy.142), channel_id=1, replica_groups=mesh['wide'=16,'narrow'=8] {'wide','narrow'}, dimensions={2}, use_global_device_ids=true | all-gather | bytes 12384 | tf_op jit(solution)/shard_map/all_gather | solution.py:142
  365.8 20.9 slice_reduce_fusion.1
  406.6 37.8 %all_gather.39 = bf16[2,192,768]{1,0,2:T(2,128)(2,1)} all-gather(bf16[2,192,96]{1,0,2:T(2,128)(2,1)} %copy.151), channel_id=1, replica_groups=mesh['wide'=16,'narrow'=8] {'narrow'}, dimensions={2}, use_global_device_ids=true | all-gather | bytes 663552 | tf_op jit(solution)/shard_map/all_gather | solution.py:149
  452.2 175.1 %all-gather.13.cloned.1.call-done = bf16[2,768,768]{2,0,1:T(2,128)(2,1)} async-done(((bf16[2,6,768]{2,0,1:T(2,128)(2,1)}), bf16[2,768,768]{2,0,1:T(2,128)(2,1)}) %all-gather.13.cloned.1.call-update) | async-done | bytes 2359312 | tf_op jit(solution)/shard_map/all_gather | solution.py:144
  646.0 42.4 %all-gather.15.cloned.1.call-done = bf16[2,768,3072]{1,0,2:T(2,128)(2,1)} async-done(((bf16[2,768,192]{1,0,2:T(2,128)(2,1)}), bf16[2,768,3072]{1,0,2:T(2,128)(2,1)}) %all-gather.15.cloned.1.call-update) | async-done | bytes 9437200 | tf_op jit(solution)/shard_map/all_gather | solution.py:152
  688.4 19.2 fusion.299
  707.6 19.9 copy.189
  727.4 27.1 %all-gather.21.cloned.1.call-done = bf16[2,1024,768]{2,1,0:T(8,128)(2,1)} async-done(((bf16[2,128,768]{2,1,0:T(8,128)(2,1)}), bf16[2,1024,768]{2,1,0:T(8,128)(2,1)}) %all-gather.21.cloned.1.call-update) | async-done | bytes 3145744 | tf_op jit(solution)/shard_map/all_gather | solution.py:17
  773.5 38.8 %all-gather.17.cloned.1.call-done = bf16[2,3072,768]{2,1,0:T(8,128)(2,1)} async-done(((bf16[2,192,768]{2,1,0:T(8,128)(2,1)}), bf16[2,3072,768]{2,1,0:T(8,128)(2,1)}) %all-gather.17.cloned.1.call-update) | async-done | bytes 9437200 | tf_op jit(solution)/shard_map/all_gather | solution.py:153
  819.0 59.4 %all-gather.11.cloned.1.call-done = bf16[2,1024,768]{2,1,0:T(8,128)(2,1)} async-done(((bf16[2,128,768]{2,1,0:T(8,128)(2,1)}), bf16[2,1024,768]{2,1,0:T(8,128)(2,1)}) %all-gather.11.cloned.1.call-update) | async-done | bytes 3145744 | tf_op jit(solution)/shard_map/all_gather | solution.py:17
  907.7 19.9 copy.192
  955.7 51.5 %all-gather.19.cloned.1.call-done = bf16[2,1024,768]{2,1,0:T(8,128)(2,1)} async-done(((bf16[2,128,768]{2,1,0:T(8,128)(2,1)}), bf16[2,1024,768]{2,1,0:T(8,128)(2,1)}) %all-gather.19.cloned.1.call-update) | async-done | bytes 3145744 | tf_op jit(solution)/shard_map/all_gather | solution.py:17
  1130.4 38.6 %reduce-scatter.27.cloned.1.call-done = bf16[128,1536]{1,0:T(8,128)(2,1)} async-done(((bf16[1024,1536]{1,0:T(8,128)(2,1)}), bf16[128,1536]{1,0:T(8,128)(2,1)}) %reduce-scatter.27.cloned.1.call-update) | async-done | bytes 393232
  1177.2 74.8 %reduce-scatter.23.cloned.1.call-done = bf16[128,1536]{1,0:T(8,128)(2,1)} async-done(((bf16[1024,1536]{1,0:T(8,128)(2,1)}), bf16[128,1536]{1,0:T(8,128)(2,1)}) %reduce-scatter.23.cloned.1.call-update) | async-done | bytes 393232
  1354.3 23.9 %copy.171 = bf16[2,768,3072]{1,0,2:T(2,128)(2,1)} copy(bf16[2,768,3072]{2,1,0:T(8,128)(2,1)} %convert_element_type.618) | data formatting | bytes 18874368 | tf_op jit(solution)/shard_map/convert_element_type | solution.py:290
  1424.2 46.6 %reduce-scatter.25.cloned.1.call-done = bf16[128,1536]{1,0:T(8,128)(2,1)} async-done(((bf16[1024,1536]{1,0:T(8,128)(2,1)}), bf16[128,1536]{1,0:T(8,128)(2,1)}) %reduce-scatter.25.cloned.1.call-update) | async-done | bytes 393232
  1489.9 198.4 %all-reduce.9.cloned.1.call-done = bf16[2,768,3072]{1,0,2:T(2,128)(2,1)} async-done(((bf16[2,768,3072]{1,0,2:T(2,128)(2,1)}), bf16[2,768,3072]{1,0,2:T(2,128)(2,1)}) %all-reduce.9.cloned.1.call-update) | async-done | bytes 9437200
  1689.8 27.8 %copy.183 = bf16[2,768,192]{0,2,1:T(8,128)(2,1)} copy(bf16[2,768,192]{1,0,2:T(2,128)(2,1)S(1)} %constant_dynamic-slice_fusion.6) | data formatting | bytes 1179648
  1717.6 54.7 %reshape.2716 = bf16[768,384]{1,0:T(8,128)(2,1)} reshape(bf16[768,192,2]{2,1,0:T(8,128)(2,1)} %bitcast.796) | data formatting | bytes 1179648
  1786.8 26.7 %copy.169 = f32[2,768,2304]{2,0,1:T(2,128)} copy(f32[2,768,2304]{2,1,0:T(8,128)} %fusion.2) | data formatting | bytes 28311552 | tf_op jit(solution)/shard_map/scatter-add | solution.py:272
  1878.1 65.3 %all-reduce.1 = f32[2,4,768]{2,1,0:T(4,128)S(1)} all-reduce(f32[2,4,768]{2,1,0:T(4,128)} %scatter-add.119), channel_id=6, replica_groups=mesh['wide'=16,'narrow'=8] {'wide','narrow'}, use_global_device_ids=true, to_apply=%region_90.91.clone | all-reduce | flops 6144 | bytes 49152
  1967.0 131.0 %all-reduce.11.cloned.1.call-done = (f32[2,768,2304]{2,0,1:T(2,128)}, f32[2,768,768]{2,0,1:T(2,128)}) async-done(((f32[2,768,2304]{2,0,1:T(2,128)}, f32[2,768,768]{2,0,1:T(2,128)}), (f32[2,768,2304]{2,0,1:T(2,128)}, f32[2,768,768]{2,0,1:T(2,128)})) %all-reduce.11.cloned.1.call-update) | async-done | bytes 18874384
  2100.9 70.4 %reduce-scatter.33.cloned.1.call-done = bf16[96,384]{1,0:T(8,128)(2,1)} async-done(((bf16[768,384]{1,0:T(8,128)(2,1)}), bf16[96,384]{1,0:T(8,128)(2,1)}) %reduce-scatter.33.cloned.1.call-update) | async-done | bytes 73744
  (957 shorter events, 539.6 us)
Async XLA Ops:
  7.2 379.5 %all-gather.9.cloned.1.call-start = ((), (), s32[]{:S(2)}) async-start(), calls=%async_computation.7 | async-start | bytes 7133184 | tf_op jit(solution)/shard_map/all_gather | solution.py:143
  7.9 619.4 %all-gather.13.cloned.1.call-start = ((), (), s32[]{:S(2)}) async-start(), calls=%async_computation.9 | async-start | bytes 2377728 | tf_op jit(solution)/shard_map/all_gather | solution.py:144
  8.7 679.7 %all-gather.15.cloned.1.call-start = ((), (), s32[]{:S(2)}) async-start(), calls=%async_computation.10 | async-start | bytes 10027008 | tf_op jit(solution)/shard_map/all_gather | solution.py:152
  9.7 354.0 %copy-start.30 = (bf16[2,1,128,768]{3,2,1,0:T(8,128)(2,1)S(1)}, bf16[2,1,128,768]{3,2,1,0:T(8,128)(2,1)}, u32[]{:S(2)}) copy-start(bf16[2,1,128,768]{3,2,1,0:T(8,128)(2,1)} %param.72) | copy-start | bytes 1179652
  47.7 706.8 %all-gather.21.cloned.1.call-start = ((), (), s32[]{:S(2)}) async-start(), calls=%async_computation.13 | async-start | bytes 3538944 | tf_op jit(solution)/shard_map/all_gather | solution.py:17
  386.7 257.2 %copy-start.171 = (f32[768]{0:T(1024)}, f32[768]{0:T(1024)S(1)}, u32[]{:S(2)}) copy-start(f32[768]{0:T(1024)S(1)} %get-tuple-element.449) | copy-start | bytes 9220
  386.7 880.5 %copy-start.174 = (f32[768]{0:T(1024)}, f32[768]{0:T(1024)S(1)}, u32[]{:S(2)}) copy-start(f32[768]{0:T(1024)S(1)} %get-tuple-element.445) | copy-start | bytes 9220
  402.2 241.7 %copy-start.22 = (bf16[1,768,2304]{2,1,0:T(8,128)(2,1)}, bf16[1,768,2304]{2,1,0:T(8,128)(2,1)S(1)}, u32[]{:S(2)}) copy-start(bf16[1,768,2304]{2,1,0:T(8,128)(2,1)S(1)} %copy.210) | copy-start | bytes 10616836
  404.9 407.3 %all-gather.17.cloned.1.call-start = ((), (), s32[]{:S(2)}) async-start(), calls=%async_computation.11 | async-start | bytes 10027008 | tf_op jit(solution)/shard_map/all_gather | solution.py:153
  447.3 431.1 %all-gather.11.cloned.1.call-start = ((), (), s32[]{:S(2)}) async-start(), calls=%async_computation.8 | async-start | bytes 3538944 | tf_op jit(solution)/shard_map/all_gather | solution.py:17
  644.8 246.0 %copy-start.134 = (bf16[128,768]{0,1:T(8,128)(2,1)}, bf16[128,768]{0,1:T(8,128)(2,1)S(1)}, u32[]{:S(2)}) copy-start(bf16[128,768]{0,1:T(8,128)(2,1)S(1)} %copy.145) | copy-start | bytes 589828
  645.7 297.1 %all-gather.23.cloned.1.call-start = ((), (), s32[]{:S(2)}) async-start(), calls=%async_computation.14 | async-start | bytes 3538944 | tf_op jit(solution)/shard_map/all_gather | solution.py:17
  818.7 188.5 %all-gather.19.cloned.1.call-start = ((), (), s32[]{:S(2)}) async-start(), calls=%async_computation.12 | async-start | bytes 3538944 | tf_op jit(solution)/shard_map/all_gather | solution.py:17
  904.3 264.7 %reduce-scatter.27.cloned.1.call-start = ((), (), s32[]{:S(2)}) async-start(), calls=%async_computation.18 | async-start | bytes 3538944
  1090.5 161.5 %reduce-scatter.23.cloned.1.call-start = ((), (), s32[]{:S(2)}) async-start(), calls=%async_computation.16 | async-start | bytes 3538944
  1121.6 298.7 %reduce-scatter.29.cloned.1.call-start = ((), (), s32[]{:S(2)}) async-start(), calls=%async_computation.19 | async-start | bytes 3538944
  1128.0 132.2 %copy-start.153 = (bf16[1,128,12,64]{1,3,2,0:T(8,128)(2,1)}, bf16[1,128,12,64]{1,3,2,0:T(8,128)(2,1)S(1)}, u32[]{:S(2)}) copy-start(bf16[1,128,12,64]{1,3,2,0:T(8,128)(2,1)S(1)} %pad_maximum_fusion.36) | copy-start | bytes 589828
  1309.1 161.7 %reduce-scatter.25.cloned.1.call-start = ((), (), s32[]{:S(2)}) async-start(), calls=%async_computation.17 | async-start | bytes 3538944
  1332.8 355.5 %all-reduce.9.cloned.1.call-start = ((), (), s32[]{:S(2)}) async-start(), calls=%async_computation.22 | async-start | bytes 18874368
  1378.2 565.2 %reduce-scatter.21.cloned.1.call-start = ((), (), s32[]{:S(2)}) async-start(), calls=%async_computation.15 | async-start | bytes 10027008 | tf_op jit(solution)/shard_map/reduce_scatter | solution.py:292
  1400.3 548.6 %reduce-scatter.31.cloned.1.call-start = ((), (), s32[]{:S(2)}) async-start(), calls=%async_computation.20 | async-start | bytes 663552
  1772.4 325.6 %all-reduce.11.cloned.1.call-start = ((), (), s32[]{:S(2)}) async-start(), calls=%async_computation.23 | async-start | bytes 37748736
  1813.6 357.7 %reduce-scatter.33.cloned.1.call-start = ((), (), s32[]{:S(2)}) async-start(), calls=%async_computation.21 | async-start | bytes 663552
  1845.5 102.1 %copy-start.212 = (f32[128]{0:T(128)S(1)}, f32[128]{0:T(128)}, u32[]{:S(2)}) copy-start(f32[128]{0:T(128)} %fusion.262) | copy-start | bytes 1540
  (277 other events, 1836.1 us)
Sparse Core Ops, SparseCore 0:
  9.7 314.0 all-gather.8
  325.5 301.7 all-gather.12
  629.5 58.7 all-gather.14
  690.5 63.9 all-gather.20
  756.6 55.5 all-gather.16
  814.4 63.9 all-gather.10
  881.3 61.4 all-gather.22
  945.7 61.4 all-gather.18
  1090.6 78.3 reduce-scatter.26
  1173.3 78.6 reduce-scatter.22
  1309.2 78.6 reduce-scatter.28
  1392.1 78.6 reduce-scatter.24
  1473.3 214.9 all-reduce.8
  1690.5 107.1 reduce-scatter.20
  1801.2 70.0 reduce-scatter.30
  1876.8 221.1 all-reduce.10
  2101.8 69.3 reduce-scatter.32
where the time goes:
time: 2200 us; the launch traced here: 2180 us
  waiting for transfers between devices  969 us (44%)
  local copies, waits for them, and re-layouts  466 us (21%)
  blocking collectives  454 us (21%)
  matrix products  172 us (8%)
  other arithmetic  95.7 us (4%)
    unnamed x25, waiting for transfers between devices  561 us
    all_gather x1, blocking collectives, body(): lax.all_gather(norm_params, ('wide', 'narrow'), axis=2, tiled=True)  316 us
    unnamed x611, local copies, waits for them, and re-layouts  261 us
    all_gather x1, waiting for transfers between devices, body(): lax.all_gather(attn_out, ('wide', 'narrow'), axis=1, tiled=True)  175 us
    all_gather x4, waiting for transfers between devices, in_one_piece(): out = lax.all_gather(both, axis, axis=dim, tiled=True)  151 us
    unnamed x1, blocking collectives  65.3 us
    dot_general x16, matrix products, left_trans(): lax.dot_general(left_mat, right_mat, (((0,), (0,)), ((), ())), preferred_...  46.7 us
  transfers between devices with their start and end apart: 17, of which 13 were waited for; matrix products, arithmetic and copies ran while one was open for 26% of the time, Pallas kernels for 0%

commit v1 on v0

v1 whole, which is shorter than its diff:
```python
import functools

import jax
import jax.numpy as jnp
from jax import lax
from jax.experimental import pallas as pl
from jax.experimental.pallas import tpu as pltpu
from jax.sharding import PartitionSpec as P

D = 768
FF = 3072
HEAD_DIM = 64
GROUP = 192
TOKENS = 256
EPS = 1e-06
ROOT_HALF = 0.7071067811865476
INV_ROOT_TWO_PI = 0.3989422804014327
ROW_A = 3200
BF = jnp.bfloat16
F32 = jnp.float32
AXES = ("wide", "narrow")
VMEM_LIMIT = 56 * 1024 * 1024


def index_of(z, y, c, x):
    return ((z * 2 + y % 2) * 2 + c) * 8 + x * 2 + y // 2


def fetch(value, z=0, y=0, c=0, x=0):
    pairs = []
    for tz in range(4):
        for ty in range(4):
            for tc in range(2):
                for tx in range(4):
                    source = index_of((tz + z) % 4, (ty + y) % 4, (tc + c) % 2, (tx + x) % 4)
                    pairs.append((source, index_of(tz, ty, tc, tx)))
    return lax.ppermute(value, AXES, pairs)


def gather_four(value, axis):
    return [value] + [fetch(value, **{axis: k}) for k in (1, 2, 3)]


def reduce_four(blocks, axis):
    total = blocks[0].astype(F32)
    for k in (1, 2, 3):
        total = total + fetch(blocks[k], **{axis: 4 - k}).astype(F32)
    return total


def exchange_four(pieces):
    return [pieces[0]] + [fetch(pieces[4 - k], x=k) for k in (1, 2, 3)]


def dot(left, right, over_left=1, over_right=0):
    return lax.dot_general(
        left, right, (((over_left,), (over_right,)), ((), ())), preferred_element_type=F32
    )


def dot_two(left, right, over_left=1, over_right=0):
    high = left.astype(BF)
    low = (left - high.astype(F32)).astype(BF)
    return dot(high, right, over_left, over_right) + dot(low, right, over_left, over_right)


def normed(values):
    average = jnp.mean(values, -1, keepdims=True)
    centred = values - average
    spread = jnp.mean(centred * centred, -1, keepdims=True)
    scale = lax.rsqrt(spread + EPS)
    return centred * scale, scale


def norm_back(grad, values, gain_row):
    z, scale = normed(values)
    dz = grad * gain_row
    out = (
        dz - jnp.mean(dz, -1, keepdims=True) - z * jnp.mean(dz * z, -1, keepdims=True)
    ) * scale
    gain_grad = jnp.sum(grad * z, 0, keepdims=True)
    offset_grad = jnp.sum(grad, 0, keepdims=True)
    return out, gain_grad, offset_grad


def two_rows(first, second):
    return jnp.concatenate([first, second, jnp.zeros((6, D), F32)], 0)


def group_start(x, k, base=0):
    return pl.multiple_of(base + lax.rem(x + k, 4) * GROUP, GROUP)


def start_copies(pairs, sems):
    copies = [
        pltpu.make_async_copy(source, target, sems.at[i])
        for i, (source, target) in enumerate(pairs)
    ]
    for copy in copies:
        copy.start()
    return copies


def wait_copies(copies):
    for copy in copies:
        copy.wait()


def qkv_kernel(layer, place_ref, h_ref, pa_ref, *refs):
    blocks, refs = refs[:8], refs[8:]
    a1p_ref, gains_ref, out_refs = refs[0], refs[1], refs[2:6]
    win, table, turned, sems = refs[6:]
    rows = [pl.ds(96 * i, 96) for i in range(8)]
    norm_copies = start_copies(
        [(b.at[layer, :, pl.ds(FF, 128)], table.at[r]) for b, r in zip(blocks, rows)],
        sems.at[pl.ds(0, 8)],
    )
    win_copies = start_copies(
        [(b.at[layer, :, pl.ds(0, 3 * D)], win.at[r]) for b, r in zip(blocks, rows)],
        sems.at[pl.ds(8, 8)],
    )
    z, _ = normed(h_ref[...])
    wait_copies(norm_copies)
    gains = dot(table[...], pa_ref[...], 0, 1)[0:8]
    gains_ref[...] = gains
    a1 = (z * gains[0:1] + gains[1:2]).astype(BF)
    a1p = dot(a1, pa_ref[...]).astype(BF)
    a1p_ref[...] = a1p
    wait_copies(win_copies)
    for c in range(3):
        part = dot(a1p, win[:, c * D : (c + 1) * D])
        if c == 0:
            part = part * HEAD_DIM ** (-0.5)
        turned[c * D : (c + 1) * D, :] = part.astype(BF).T
    x = place_ref[0]
    for k in range(4):
        for c in range(3):
            out_refs[k][c * GROUP : (c + 1) * GROUP, :] = turned[
                pl.ds(group_start(x, k, c * D), GROUP), :
            ]


def key_bias(place_ref, bias):
    x, yh, length = place_ref[0], place_ref[1], place_ref[2]
    for k in range(4):
        for half in range(2):
            start = lax.rem(x + k, 4) * 256 + lax.rem(yh + half, 2) * 128
            slot = start + lax.broadcasted_iota(jnp.int32, (128, TOKENS), 0)
            bias[pl.ds(k * 256 + half * 128, 128), :] = jnp.where(slot < length, 0.0, -1e30)


def side_by_side(refs, start):
    return jnp.concatenate([r[start : start + HEAD_DIM, :] for r in refs], 1)


def attend_kernel(place_ref, t0, t1, t2, t3, u0, u1, u2, u3, sums_ref, bias):
    t_refs, u_refs = (t0, t1, t2, t3), (u0, u1, u2, u3)
    key_bias(place_ref, bias)
    for j in range(3):
        keys = side_by_side(t_refs, GROUP + j * HEAD_DIM).T
        values_t = side_by_side(t_refs, 2 * GROUP + j * HEAD_DIM)
        for b in range(4):
            query_t = t_refs[b][j * HEAD_DIM : (j + 1) * HEAD_DIM, :]
            scores = dot(keys, query_t) + bias[...]
            peak = jnp.max(scores, 0, keepdims=True)
            expont = jnp.exp(scores - peak)
            total = jnp.sum(expont, 0, keepdims=True)
            mixed = dot(values_t, expont.astype(BF)) / total
            u_refs[b][j * HEAD_DIM : (j + 1) * HEAD_DIM, :] = mixed.astype(BF)
            sums_ref[j : j + 1, b * TOKENS : (b + 1) * TOKENS] = peak + jnp.log(total)


def attend_back_kernel(place_ref, *refs):
    t_refs, g_refs, u_refs = refs[0:4], refs[4:8], refs[8:12]
    sums_ref = refs[12]
    out_refs = refs[13:17]
    bias = refs[17]
    key_bias(place_ref, bias)
    for j in range(3):
        keys_t = side_by_side(t_refs, GROUP + j * HEAD_DIM)
        keys = keys_t.T
        values = side_by_side(t_refs, 2 * GROUP + j * HEAD_DIM).T
        grad_keys = jnp.zeros((4 * TOKENS, HEAD_DIM), F32)
        grad_values = jnp.zeros((4 * TOKENS, HEAD_DIM), F32)
        rows = slice(j * HEAD_DIM, (j + 1) * HEAD_DIM)
        for b in range(4):
            query_t = t_refs[b][rows, :]
            grad_t = g_refs[b][rows, :]
            scores = dot(keys, query_t) + bias[...]
            probs = jnp.exp(scores - sums_ref[j : j + 1, b * TOKENS : (b + 1) * TOKENS])
            grad_probs = dot(values, grad_t)
            delta = jnp.sum(
                grad_t.astype(F32) * u_refs[b][rows, :].astype(F32), 0, keepdims=True
            )
            grad_scores = (probs * (grad_probs - delta)).astype(BF)
            grad_values = grad_values + dot(probs.astype(BF), grad_t, 1, 1)
            grad_keys = grad_keys + dot(grad_scores, query_t, 1, 1)
            grad_query = dot(keys_t, grad_scores) * HEAD_DIM ** (-0.5)
            out_refs[b][rows, :] = grad_query.astype(BF)
        grad_keys = grad_keys.astype(BF).T
        grad_values = grad_values.astype(BF).T
        for b in range(4):
            columns = slice(b * TOKENS, (b + 1) * TOKENS)
            start = GROUP + j * HEAD_DIM
            out_refs[b][start : start + HEAD_DIM, :] = grad_keys[:, columns]
            start = 2 * GROUP + j * HEAD_DIM
            out_refs[b][start : start + HEAD_DIM, :] = grad_values[:, columns]


def mlp_copies(layer, a_blocks, b_blocks, c_blocks, wout, w1, w2, sems):
    out_copies = start_copies(
        [
            (b.at[layer, :, pl.ds(3 * D, D)], wout.at[pl.ds(96 * i, 96)])
            for i, b in enumerate(a_blocks)
        ],
        sems.at[pl.ds(0, 8)],
    )
    first_copies = start_copies(
        [
            (b.at[layer], w1.at[i // 4, pl.ds(192 * (i % 4), 192)])
            for i, b in enumerate(b_blocks)
        ],
        sems.at[pl.ds(8, 8)],
    )
    second_copies = start_copies(
        [
            (b.at[layer], w2.at[i // 4, pl.ds(384 * (i % 4), 384)])
            for i, b in enumerate(c_blocks)
        ],
        sems.at[pl.ds(16, 8)],
    )
    return out_copies, first_copies, second_copies


def mlp_kernel(layer, place_ref, h_ref, *refs):
    u_refs, refs = refs[:4], refs[4:]
    po_ref, p2_ref, gains_ref = refs[:3]
    a_blocks, b_blocks, c_blocks = refs[3:11], refs[11:19], refs[19:27]
    h1_ref, next_ref, a2_ref, op_ref, act_ref, slope_ref = refs[27:33]
    turned, wout, w1, w2, sems = refs[33:]
    out_copies, first_copies, second_copies = mlp_copies(
        layer, a_blocks, b_blocks, c_blocks, wout, w1, w2, sems
    )
    x = place_ref[0]
    for k in range(4):
        turned[pl.ds(group_start(x, k), GROUP), :] = u_refs[k][...]
    op = dot(turned[...], po_ref[...], 0, 0).astype(BF)
    op_ref[...] = op
    wait_copies(out_copies)
    h1 = h_ref[...] + dot_two(dot(op, wout[...]), p2_ref[...])
    h1_ref[...] = h1
    z, _ = normed(h1)
    a2 = (z * gains_ref[2:3] + gains_ref[3:4]).astype(BF)
    a2_ref[...] = a2
    wait_copies(first_copies)
    total = h1
    for half in range(2):
        pre = dot(a2, w1[half])
        below = 0.5 * (1.0 + lax.erf(pre * ROOT_HALF))
        act = (pre * below).astype(BF)
        slope = below + pre * (jnp.exp(-0.5 * pre * pre) * INV_ROOT_TWO_PI)
        columns = slice(half * 1536, (half + 1) * 1536)
        act_ref[:, columns] = act
        slope_ref[:, columns] = slope.astype(BF)
        if half == 0:
            wait_copies(second_copies)
        total = total + dot(act, w2[half])
    next_ref[...] = total


def mlp_back_kernel(layer, place_ref, g_ref, slope_ref, h1_ref, gains_ref, p2_ref, po_ref, *refs):
    a_blocks, b_blocks, c_blocks = refs[0:8], refs[8:16], refs[16:24]
    dpre_ref, g1_ref, g1b_ref, norm_ref = refs[24:28]
    out_refs = refs[28:32]
    turned, wout, w1, w2, sems = refs[32:]
    out_copies, first_copies, second_copies = mlp_copies(
        layer, a_blocks, b_blocks, c_blocks, wout, w1, w2, sems
    )
    grad = g_ref[...]
    grad_low = grad.astype(BF)
    wait_copies(second_copies)
    grad_a2 = jnp.zeros((TOKENS, D), F32)
    for half in range(2):
        columns = slice(half * 1536, (half + 1) * 1536)
        grad_act = dot(grad_low, w2[half], 1, 1)
        dpre = (grad_act * slope_ref[:, columns].astype(F32)).astype(BF)
        dpre_ref[:, columns] = dpre
        if half == 0:
            wait_copies(first_copies)
        grad_a2 = grad_a2 + dot(dpre, w1[half], 1, 1)
    dv, gain_grad, offset_grad = norm_back(grad_a2, h1_ref[...], gains_ref[2:3])
    norm_ref[...] = two_rows(gain_grad, offset_grad)
    g1 = grad + dv
    g1_ref[...] = g1
    g1b = dot(g1.astype(BF), p2_ref[...], 1, 1).astype(BF)
    g1b_ref[...] = g1b
    wait_copies(out_copies)
    grad_op = dot(g1b, wout[...], 1, 1).astype(BF)
    turned[...] = dot(po_ref[...], grad_op, 1, 1).astype(BF)
    x = place_ref[0]
    for k in range(4):
        out_refs[k][...] = turned[pl.ds(group_start(x, k), GROUP), :]


def mlp_grad_kernel(g_ref, act_ref, a2_ref, dpre_ref, first_keep, first_send, second_keep, second_send):
    grad_low = g_ref[...].astype(BF)
    a2 = a2_ref[...]
    for half, (first, second) in enumerate(((first_keep, second_keep), (first_send, second_send))):
        for part in range(2):
            start = half * 1536 + part * 768
            columns = slice(start, start + 768)
            inner = slice(part * 768, part * 768 + 768)
            first[:, inner] = dot(a2, dpre_ref[:, columns], 0, 0).astype(BF)
            second[inner, :] = dot(act_ref[:, columns], grad_low, 0, 0).astype(BF)


def qkv_back_kernel(layer, place_ref, d0, d1, d2, d3, h_ref, g1_ref, gains_ref, pa_ref, *refs):
    blocks, refs = refs[:8], refs[8:]
    next_ref, dqkv_ref, norm_ref, win, sems = refs
    win_copies = start_copies(
        [
            (b.at[layer, :, pl.ds(0, 3 * D)], win.at[pl.ds(96 * i, 96)])
            for i, b in enumerate(blocks)
        ],
        sems,
    )
    x = place_ref[0]
    for k, piece in enumerate((d0, d1, d2, d3)):
        for c in range(3):
            dqkv_ref[pl.ds(group_start(x, k, c * D), GROUP), :] = piece[
                c * GROUP : (c + 1) * GROUP, :
            ]
    wait_copies(win_copies)
    turned = dot(win[...], dqkv_ref[...])
    grad_a1 = dot_two(turned, pa_ref[...], 0, 1)
    dv, gain_grad, offset_grad = norm_back(grad_a1, h_ref[...], gains_ref[0:1])
    norm_ref[...] = two_rows(gain_grad, offset_grad)
    next_ref[...] = g1_ref[...] + dv


def attn_grad_kernel(a1p_ref, dqkv_ref, op_ref, g1b_ref, norm1_ref, norm2_ref, pa_ref, keep_ref, send_ref):
    norms = jnp.concatenate(
        [norm1_ref[0:2], norm2_ref[0:2], jnp.zeros((124, D), F32)], 0
    )
    norms = dot_two(norms, pa_ref[...]).T
    for half, out in enumerate((keep_ref, send_ref)):
        rows = slice(half * 384, half * 384 + 384)
        for c in range(3):
            out[:, c * D : (c + 1) * D] = dot(
                a1p_ref[:, rows], dqkv_ref[c * D : (c + 1) * D, :], 0, 1
            ).astype(BF)
        out[:, 3 * D : 4 * D] = dot(op_ref[:, rows], g1b_ref[...], 0, 0).astype(BF)
        out[:, 4 * D :] = norms[rows].astype(BF)


def shaped(*shape, dtype=BF):
    return jax.ShapeDtypeStruct(shape, dtype)


def run_kernel(kernel, inputs, outs, scratch=(), flops=0, any_count=0, scalars=True):
    specs = []
    for i in range(len(inputs)):
        if scalars and i == 0:
            specs.append(pl.BlockSpec(memory_space=pltpu.SMEM))
        elif i >= len(inputs) - any_count:
            specs.append(pl.BlockSpec(memory_space=pl.ANY))
        else:
            specs.append(pl.BlockSpec(memory_space=pltpu.VMEM))
    moved = sum(v.size * v.dtype.itemsize for v in inputs) + sum(
        v.size * v.dtype.itemsize for v in outs
    )
    return pl.pallas_call(
        kernel,
        out_shape=tuple(outs),
        in_specs=specs,
        out_specs=tuple(pl.BlockSpec(memory_space=pltpu.VMEM) for _ in outs),
        scratch_shapes=list(scratch),
        compiler_params=pltpu.CompilerParams(vmem_limit_bytes=VMEM_LIMIT),
        cost_estimate=pl.CostEstimate(flops=flops, bytes_accessed=moved, transcendentals=0),
    )(*inputs)


MLP_SCRATCH = (
    pltpu.VMEM((D, TOKENS), BF),
    pltpu.VMEM((D, D), BF),
    pltpu.VMEM((2, D, 1536), BF),
    pltpu.VMEM((2, 1536, D), BF),
    pltpu.SemaphoreType.DMA((24,)),
)
UNIT = 2 * TOKENS * D * D
ATTEND = 2 * 3 * 1024 * 1024 * HEAD_DIM * 4


def by_y(quads, low):
    one = jnp.where(low == 0, quads[1], quads[3])
    three = jnp.where(low == 0, quads[3], quads[1])
    return jnp.stack([jnp.stack([quads[0], one]), jnp.stack([quads[2], three])])


def from_y(table, low):
    one = jnp.where(low == 0, table[0, 1], table[1, 1])
    three = jnp.where(low == 0, table[1, 1], table[0, 1])
    return [table[0, 0], one, table[1, 0], three]


def weights_everywhere(norm_params, attn_in, attn_out, mlp_in, mlp_out, low):
    norm_part = jnp.pad(jnp.swapaxes(norm_params, 1, 2), ((0, 0), (0, 0), (0, 124)))
    a = jnp.concatenate([attn_in, attn_out, norm_part], -1).reshape(300, 128)
    b = mlp_in.reshape(288, 128)
    c = mlp_out.reshape(288, 128)
    a, b, c = (
        jnp.stack(gather_four(a, "z")),
        jnp.stack(gather_four(b, "y")),
        jnp.stack(gather_four(c, "x")),
    )
    a, b, c = gather_four(a, "x"), gather_four(b, "z"), gather_four(c, "y")
    a = jnp.stack(a).reshape(4, 4, 2, 6, ROW_A)
    a = a.transpose(2, 1, 0, 3, 4).reshape(2, 96, ROW_A)
    b = jnp.stack(b).reshape(4, 4, 2, 96, 192)
    b = by_y([b[:, k] for k in range(4)], low)
    b = b.transpose(3, 0, 4, 2, 1, 5).reshape(2, 192, 1536)
    c = by_y([v.reshape(4, 2, 192, 96) for v in c], low)
    c = c.transpose(3, 1, 4, 2, 0, 5).reshape(2, 384, 768)
    a, b, c = gather_four(a, "y"), gather_four(b, "x"), gather_four(c, "z")
    return tuple(part + [fetch(v, c=1) for v in part] for part in (a, b, c))


def gradients_home(keeps, sends, low):
    halves = [
        [
            (k.astype(F32) + fetch(s, c=1).astype(F32)).astype(BF)
            for k, s in zip(keep, send)
        ]
        for keep, send in zip(keeps, sends)
    ]

    def parts(which, rows):
        return [
            jnp.stack([halves[l][which][k * rows : (k + 1) * rows] for l in range(2)])
            for k in range(4)
        ]

    a, b, c = (
        reduce_four(parts(0, 96), "y").astype(BF),
        reduce_four(parts(1, 192), "x").astype(BF),
        reduce_four(parts(2, 384), "z").astype(BF),
    )
    a = a.reshape(2, 4, 4, 6, ROW_A).transpose(2, 1, 0, 3, 4).reshape(4, 4, 300, 128)
    b = b.reshape(2, 2, 96, 4, 2, 192).transpose(1, 4, 3, 0, 2, 5)
    b = jnp.stack(from_y(b, low)).transpose(1, 0, 2, 3, 4).reshape(4, 4, 288, 128)
    c = c.reshape(2, 2, 192, 4, 2, 96).transpose(4, 1, 3, 0, 2, 5)
    c = jnp.stack(from_y(c, low)).reshape(4, 4, 288, 128)
    a, b, c = (
        reduce_four([a[k] for k in range(4)], "x").astype(BF),
        reduce_four([b[k] for k in range(4)], "z").astype(BF),
        reduce_four([c[k] for k in range(4)], "y").astype(BF),
    )
    a, b, c = (
        reduce_four([a[k] for k in range(4)], "z"),
        reduce_four([b[k] for k in range(4)], "y"),
        reduce_four([c[k] for k in range(4)], "x"),
    )
    a = a.reshape(2, 6, ROW_A)
    return (
        jnp.swapaxes(a[:, :, 4 * D : 4 * D + 4], 1, 2),
        a[:, :, : 3 * D],
        a[:, :, 3 * D : 4 * D],
        b.reshape(2, 96, 192),
        c.reshape(2, 192, 96),
    )


def body(inputs, lengths, norm_params, attn_in, attn_out, mlp_in, mlp_out, cotangent):
    wide = lax.axis_index("wide")
    narrow = lax.axis_index("narrow")
    core, low, z = wide % 2, (wide // 2) % 2, wide // 4
    x, high = narrow // 2, narrow % 2
    y = high * 2 + low

    a_blocks, b_blocks, c_blocks = weights_everywhere(
        norm_params, attn_in, attn_out, mlp_in, mlp_out, low
    )

    slot = jnp.arange(D, dtype=jnp.int32)
    own_order = ((x + slot // 192) % 4) * 192 + ((high + (slot // 96) % 2) % 2) * 96 + slot % 96
    row_core = (core + slot // 384) % 2
    row_y = (y + (slot // 96) % 4) % 4
    row_z = (z + (slot // 24) % 4) % 4
    row_x = (x + (slot // 6) % 4) % 4
    row_order = 6 * index_of(row_z, row_y, row_core, row_x) + slot % 6
    pa = (own_order[:, None] == row_order[None, :]).astype(BF)
    po = (slot[:, None] == row_order[None, :]).astype(BF)
    p2 = (slot[:, None] == own_order[None, :]).astype(BF)

    both = jnp.stack([inputs, cotangent])[:, :, 0]
    mine = lax.dynamic_index_in_dim(both, high, 1, keepdims=False)
    other = lax.dynamic_index_in_dim(both, 1 - high, 1, keepdims=False)
    rows = jnp.concatenate([mine, fetch(other, y=2)], 1)
    rows = jnp.einsum("ntd,dr->ntr", rows, p2, preferred_element_type=F32)
    hidden, grad = rows[0], rows[1]
    length = lax.dynamic_index_in_dim(lengths[:, 0], high, 0, keepdims=False)
    place = jnp.stack([x, high, length, z]).astype(jnp.int32)

    records = []
    for layer in range(2):
        a1p, gains, *pieces = run_kernel(
            functools.partial(qkv_kernel, layer),
            [place, hidden, pa] + a_blocks,
            [shaped(TOKENS, D), shaped(8, D, dtype=F32)] + [shaped(576, TOKENS)] * 4,
            (
                pltpu.VMEM((D, 3 * D), BF),
                pltpu.VMEM((D, 128), BF),
                pltpu.VMEM((3 * D, TOKENS), BF),
                pltpu.SemaphoreType.DMA((16,)),
            ),
            flops=4 * UNIT,
            any_count=8,
        )
        turned = exchange_four(pieces)
        *mixed, sums = run_kernel(
            attend_kernel,
            [place] + turned,
            [shaped(GROUP, TOKENS)] * 4 + [shaped(3, 1024, dtype=F32)],
            (pltpu.VMEM((1024, TOKENS), F32),),
            flops=ATTEND,
        )
        back = exchange_four(mixed)
        h1, following, a2, op, act, slope = run_kernel(
            functools.partial(mlp_kernel, layer),
            [place, hidden] + back + [po, p2, gains] + a_blocks + b_blocks + c_blocks,
            [
                shaped(TOKENS, D, dtype=F32),
                shaped(TOKENS, D, dtype=F32),
                shaped(TOKENS, D),
                shaped(TOKENS, D),
                shaped(TOKENS, FF),
                shaped(TOKENS, FF),
            ],
            MLP_SCRATCH,
            flops=11 * UNIT,
            any_count=24,
        )
        records.append((hidden, a1p, gains, turned, mixed, sums, h1, a2, op, act, slope))
        hidden = following

    def leave(values):
        values = jnp.dot(
            values, p2.astype(F32).T, precision=lax.Precision.HIGHEST, preferred_element_type=F32
        )
        own = values[:128]
        came = fetch(values[128:], y=2)
        return jnp.stack(
            [jnp.where(high == 0, own, came), jnp.where(high == 0, came, own)]
        )[:, None]

    outputs = leave(hidden)

    keeps, sends = [None, None], [None, None]
    for layer in (1, 0):
        hidden, a1p, gains, turned, mixed, sums, h1, a2, op, act, slope = records[layer]
        dpre, g1, g1b, norm2, *pieces = run_kernel(
            functools.partial(mlp_back_kernel, layer),
            [place, grad, slope, h1, gains, p2, po] + a_blocks + b_blocks + c_blocks,
            [
                shaped(TOKENS, FF),
                shaped(TOKENS, D, dtype=F32),
                shaped(TOKENS, D),
                shaped(8, D, dtype=F32),
            ]
            + [shaped(GROUP, TOKENS)] * 4,
            MLP_SCRATCH,
            flops=11 * UNIT,
            any_count=24,
        )
        grad_mixed = exchange_four(pieces)
        first_keep, first_send, second_keep, second_send = run_kernel(
            mlp_grad_kernel,
            [grad, act, a2, dpre],
            [shaped(D, 1536), shaped(D, 1536), shaped(1536, D), shaped(1536, D)],
            flops=8 * UNIT,
            scalars=False,
        )
        pieces = run_kernel(
            attend_back_kernel,
            [place] + turned + grad_mixed + mixed + [sums],
            [shaped(576, TOKENS)] * 4,
            (pltpu.VMEM((1024, TOKENS), F32),),
            flops=3 * ATTEND,
        )
        grad_pieces = exchange_four(pieces)
        grad, dqkv, norm1 = run_kernel(
            functools.partial(qkv_back_kernel, layer),
            [place] + grad_pieces + [hidden, g1, gains, pa] + a_blocks,
            [shaped(TOKENS, D, dtype=F32), shaped(3 * D, TOKENS), shaped(8, D, dtype=F32)],
            (pltpu.VMEM((D, 3 * D), BF), pltpu.SemaphoreType.DMA((8,))),
            flops=5 * UNIT,
            any_count=8,
        )
        attn_keep, attn_send = run_kernel(
            attn_grad_kernel,
            [a1p, dqkv, op, g1b, norm1, norm2, pa],
            [shaped(384, ROW_A)] * 2,
            flops=4 * UNIT,
            scalars=False,
        )
        keeps[layer] = (attn_keep, first_keep, second_keep)
        sends[layer] = (attn_send, first_send, second_send)
    grad_inputs = leave(grad)
    return (outputs, grad_inputs) + gradients_home(keeps, sends, low)


def solution(mesh):
    in_specs = (
        P(None, "wide", "narrow", None),
        P(None, "wide"),
        P(None, None, ("wide", "narrow")),
        P(None, ("wide", "narrow"), None),
        P(None, ("wide", "narrow"), None),
        P(None, "narrow", "wide"),
        P(None, "wide", "narrow"),
        P(None, "wide", "narrow", None),
    )
    out_specs = (
        P(None, "wide", "narrow", None),
        P(None, "wide", "narrow", None),
        P(None, None, ("wide", "narrow")),
        P(None, ("wide", "narrow"), None),
        P(None, ("wide", "narrow"), None),
        P(None, "narrow", "wide"),
        P(None, "wide", "narrow"),
    )
    return jax.shard_map(body, mesh=mesh, in_specs=in_specs, out_specs=out_specs, check_vma=False)
```

time: 2200 us -> 630 us (0.29)
  waiting for transfers between devices: 969 us -> 257 us
  blocking collectives: 454 us -> 0 us
  local copies, waits for them, and re-layouts: 466 us -> 64.4 us
  matrix products: 172 us -> 5.65 us
  Pallas kernels: 0 us -> 142 us
  starting transfers between devices: 3.45 us -> 109 us
  other arithmetic: 95.7 us -> 39.5 us
    unnamed x25 -> x0, waiting for transfers between devices: 561 us -> none
    all_gather x8 -> x0, waiting for transfers between devices: 408 us -> none  [the longest x1 175 us: body(): lax.all_gather(attn_out, ('wide', 'narrow'), axis=1, tiled=True)]
    all_gather x3 -> x0, blocking collectives: 389 us -> none  [the longest x1 316 us: body(): lax.all_gather(norm_params, ('wide', 'narrow'), axis=2, tiled=True)]
    ppermute x0 -> x99, waiting for transfers between devices: none -> 257 us  [fetch(): return lax.ppermute(value, AXES, pairs)]
    unnamed x611 -> x138, local copies, waits for them, and re-layouts: 261 us -> 14.8 us
    dot_general x120 -> x3, matrix products: 172 us -> 5.65 us  [the longest x2 3.81 us: leave(): jnp.dot(values, p2.astype(F32).T, precision=lax.Precision.HIGHEST, prefer...]
    pallas_call x0 -> x16, Pallas kernels: none -> 142 us  [run_kernel(): pl.pallas_call(kernel, out_shape=tuple(outs), in_specs=specs, out_specs=t...]
    ppermute x0 -> x99, starting transfers between devices: none -> 109 us  [fetch(): return lax.ppermute(value, AXES, pairs)]
  transfers between devices with their start and end apart: 17 -> 99, of which waited for: 13 -> 39; matrix products, arithmetic and copies ran while one was open for 26% -> 15% of each run, Pallas kernels for 0% -> 13%
where the time goes in v1:
time: 630 us; the launch traced here: 620 us
  waiting for transfers between devices  257 us (41%)
  Pallas kernels  142 us (23%)
  starting transfers between devices  109 us (17%)
  local copies, waits for them, and re-layouts  64.4 us (10%)
  other arithmetic  39.5 us (6%)
    ppermute x99, waiting for transfers between devices, fetch(): return lax.ppermute(value, AXES, pairs)  257 us
    pallas_call x16, Pallas kernels, run_kernel(): pl.pallas_call(kernel, out_shape=tuple(outs), in_specs=specs, out_specs=t...  142 us
    ppermute x99, starting transfers between devices, fetch(): return lax.ppermute(value, AXES, pairs)  109 us
    unnamed x138, local copies, waits for them, and re-layouts  14.8 us
  transfers between devices with their start and end apart: 99, of which 39 were waited for; matrix products, arithmetic and copies ran while one was open for 15% of the time, Pallas kernels for 13%

profile of v1, /device:TPU:0, one launch (start us, length us, event | category | flops | bytes accessed | tf_op | source)
XLA Modules:
  0.0 619.9 jit_solution(738753857606869106)
XLA Ops:
  48.5 10.8 %collective-permute-done.6 = bf16[4,300,128]{2,1,0:T(8,128)(2,1)S(1)} collective-permute-done((bf16[4,300,128]{2,1,0:T(8,128)(2,1)S(1)}, bf16[4,300,128]{2,1,0:T(8,128)(2,1)S(1)}, u32[]{:S(2)}, u32[]{:S(2)}) %collective-permute-start.6) | collective-permute-done | bytes 307232 | tf_op jit(solution)/shard_map/ppermute | solution.py:37
  79.7 11.9 %collective-permute-done.28.refs_18_.refs_11_ = bf16[2,192,1536]{2,1,0:T(8,128)(2,1)S(1)} collective-permute-done((bf16[2,192,1536]{2,1,0:T(8,128)(2,1)}, bf16[2,192,1536]{2,1,0:T(8,128)(2,1)S(1)}, u32[]{:S(2)}, u32[]{:S(2)}) %collective-permute-start.28) | collective-permute-done | bytes 1179680 | tf_op jit(solution)/shard_map/ppermute | solution.py:37
  93.5 23.2 %collective-permute-done.27.refs_17_.refs_10_ = bf16[2,192,1536]{2,1,0:T(8,128)(2,1)S(1)} collective-permute-done((bf16[2,192,1536]{2,1,0:T(8,128)(2,1)}, bf16[2,192,1536]{2,1,0:T(8,128)(2,1)S(1)}, u32[]{:S(2)}, u32[]{:S(2)}) %collective-permute-start.27) | collective-permute-done | bytes 1179680 | tf_op jit(solution)/shard_map/ppermute | solution.py:37
  117.2 7.8 %collective-permute-done.8.refs_2_.refs_9_ = bf16[2,96,3200]{2,1,0:T(8,128)(2,1)} collective-permute-done((bf16[2,96,3200]{2,1,0:T(8,128)(2,1)S(1)}, bf16[2,96,3200]{2,1,0:T(8,128)(2,1)}, u32[]{:S(2)}, u32[]{:S(2)}) %collective-permute-start.8) | collective-permute-done | bytes 1228832 | tf_op jit(solution)/shard_map/ppermute | solution.py:37
  168.0 35.6 %collective-permute-done.41.refs_26_.refs_19_ = bf16[2,384,768]{2,1,0:T(8,128)(2,1)S(1)} collective-permute-done((bf16[2,384,768]{2,1,0:T(8,128)(2,1)}, bf16[2,384,768]{2,1,0:T(8,128)(2,1)S(1)}, u32[]{:S(2)}, u32[]{:S(2)}) %collective-permute-start.41) | collective-permute-done | bytes 1179680 | tf_op jit(solution)/shard_map/ppermute | solution.py:37
  216.6 9.9 %shard_map.136 = (bf16[192,256]{1,0:T(8,128)(2,1)}, bf16[192,256]{1,0:T(8,128)(2,1)}, bf16[192,256]{1,0:T(8,128)(2,1)}, bf16[192,256]{1,0:T(8,128)(2,1)}, f32[3,1024]{1,0:T(4,128)}) custom-call(s32[4]{0:T(128)} %pad_add_fusion.place_ref, bf16[576,256]{1,0:T(8,128)(2,1)} %get-tuple-element.83.t0.refs_0_, bf16[576,256]{1,0:T(8,128)(2,1)} %copy-done.54, ...), custom_call_target="tpu_custom_call" | custom-call | flops 1610612736 | bytes 1585168 | tf_op jit(solution)/shard_map/pallas_call | solution.py:372
  235.7 10.2 %shard_map.137 = (f32[256,768]{1,0:T(8,128)}, f32[256,768]{1,0:T(8,128)}, bf16[256,768]{1,0:T(8,128)(2,1)}, bf16[256,768]{1,0:T(8,128)(2,1)}, bf16[256,3072]{1,0:T(8,128)(2,1)}, /*index=5*/bf16[256,3072]{1,0:T(8,128)(2,1)}) custom-call(s32[4]{0:T(128)} %pad_add_fusion.place_ref, f32[256,768]{1,0:T(8,128)} %get-tuple-element.217.h_ref, ...), custom_call_target="tpu_custom_call" | custom-call | flops 3321888768 | bytes 37773328 | tf_op jit(solution)/shard_map/pallas_call | solution.py:372
  254.7 7.5 %collective-permute-done.46.t1.refs_1_ = bf16[576,256]{1,0:T(8,128)(2,1)S(1)} collective-permute-done((bf16[576,256]{1,0:T(8,128)(2,1)}, bf16[576,256]{1,0:T(8,128)(2,1)S(1)}, u32[]{:S(2)}, u32[]{:S(2)}) %collective-permute-start.46) | collective-permute-done | bytes 294944 | tf_op jit(solution)/shard_map/ppermute | solution.py:37
  269.5 9.9 %shard_map.139 = (bf16[192,256]{1,0:T(8,128)(2,1)}, bf16[192,256]{1,0:T(8,128)(2,1)}, bf16[192,256]{1,0:T(8,128)(2,1)}, bf16[192,256]{1,0:T(8,128)(2,1)}, f32[3,1024]{1,0:T(4,128)}) custom-call(s32[4]{0:T(128)} %pad_add_fusion.place_ref, bf16[576,256]{1,0:T(8,128)(2,1)} %get-tuple-element.93.t0.refs_0_, bf16[576,256]{1,0:T(8,128)(2,1)} %copy-done.57, ...), custom_call_target="tpu_custom_call" | custom-call | flops 1610612736 | bytes 1585168 | tf_op jit(solution)/shard_map/pallas_call | solution.py:372
  288.9 10.1 %shard_map.140 = (f32[256,768]{1,0:T(8,128)}, f32[256,768]{1,0:T(8,128)}, bf16[256,768]{1,0:T(8,128)(2,1)}, bf16[256,768]{1,0:T(8,128)(2,1)}, bf16[256,3072]{1,0:T(8,128)(2,1)}, /*index=5*/bf16[256,3072]{1,0:T(8,128)(2,1)}) custom-call(s32[4]{0:T(128)} %pad_add_fusion.place_ref, f32[256,768]{1,0:T(8,128)} %get-tuple-element.92.h_ref, ...), custom_call_target="tpu_custom_call" | custom-call | flops 3321888768 | bytes 37773328 | tf_op jit(solution)/shard_map/pallas_call | solution.py:372
  299.0 12.9 %shard_map.141 = (bf16[256,3072]{1,0:T(8,128)(2,1)}, f32[256,768]{1,0:T(8,128)}, bf16[256,768]{1,0:T(8,128)(2,1)}, f32[8,768]{1,0:T(8,128)}, bf16[192,256]{1,0:T...) custom-call(s32[4]{0:T(128)} %pad_add_fusion.place_ref, ...), custom_call_target="tpu_custom_call" | custom-call | flops 3321888768 | bytes 37404688 | tf_op jit(solution)/shard_map/pallas_call | solution.py:372
  321.5 10.4 %shard_map.142 = (bf16[576,256]{1,0:T(8,128)(2,1)}, bf16[576,256]{1,0:T(8,128)(2,1)}, bf16[576,256]{1,0:T(8,128)(2,1)}, bf16[576,256]{1,0:T(8,128)(2,1)}) custom-call(s32[4]{0:T(128)} %pad_add_fusion.place_ref, bf16[576,256]{1,0:T(8,128)(2,1)} %get-tuple-element.93.t0.refs_0_, bf16[576,256]{1,0:T(8,128)(2,1)} %copy-done.57, bf16[576,256]{1,0:T(8,128)(2,1)} %copy-done.58, ...), custom_call_target="tpu_custom_call" | custom-call | flops 4831838208 | bytes 3158032 | tf_op jit(solution)/shard_map/pallas_call | solution.py:372
  334.4 7.6 %shard_map.150 = (bf16[768,1536]{1,0:T(8,128)(2,1)}, bf16[768,1536]{1,0:T(8,128)(2,1)}, bf16[1536,768]{1,0:T(8,128)(2,1)}, bf16[1536,768]{1,0:T(8,128)(2,1)}) custom-call(f32[256,768]{1,0:T(8,128)} %get-tuple-element.216.g_ref, bf16[256,3072]{1,0:T(8,128)(2,1)} %get-tuple-element.150.act_ref, bf16[256,768]{1,0:T(8,128)(2,1)} %get-tuple-element.151.a2_ref, ...), custom_call_target="tpu_custom_call" | custom-call | flops 2415919104 | bytes 13762560 | tf_op jit(solution)/shard_map/pallas_call | solution.py:372
  348.0 8.1 %shard_map.143 = (f32[256,768]{1,0:T(8,128)}, bf16[2304,256]{1,0:T(8,128)(2,1)}, f32[8,768]{1,0:T(8,128)}) custom-call(s32[4]{0:T(128)} %pad_add_fusion.place_ref, bf16[576,256]{1,0:T(8,128)(2,1)} %get-tuple-element.110.d0, bf16[576,256]{1,0:T(8,128)(2,1)} %copy-done.37, bf16[576,256]{1,0:T(8,128)(2,1)} %copy-done.38, bf16[576,256]{1,0:T(8,128)(2,1)} %copy-done.39, ...), custom_call_target="tpu_custom_call" | custom-call | flops 1509949440 | bytes 15777808 | tf_op jit(solution)/shard_map/pallas_call | solution.py:372
  356.1 12.8 %shard_map.144 = (bf16[256,3072]{1,0:T(8,128)(2,1)}, f32[256,768]{1,0:T(8,128)}, bf16[256,768]{1,0:T(8,128)(2,1)}, f32[8,768]{1,0:T(8,128)}, bf16[192,256]{1,0:T...) custom-call(s32[4]{0:T(128)} %pad_add_fusion.place_ref, ...), custom_call_target="tpu_custom_call" | custom-call | flops 3321888768 | bytes 37404688 | tf_op jit(solution)/shard_map/pallas_call | solution.py:372
  378.7 10.3 %shard_map.145 = (bf16[576,256]{1,0:T(8,128)(2,1)}, bf16[576,256]{1,0:T(8,128)(2,1)}, bf16[576,256]{1,0:T(8,128)(2,1)}, bf16[576,256]{1,0:T(8,128)(2,1)}) custom-call(s32[4]{0:T(128)} %pad_add_fusion.place_ref, bf16[576,256]{1,0:T(8,128)(2,1)} %get-tuple-element.83.t0.refs_0_, bf16[576,256]{1,0:T(8,128)(2,1)} %copy-done.54, bf16[576,256]{1,0:T(8,128)(2,1)} %copy-done.55, ...), custom_call_target="tpu_custom_call" | custom-call | flops 4831838208 | bytes 3158032 | tf_op jit(solution)/shard_map/pallas_call | solution.py:372
  397.8 7.5 %shard_map.149 = (bf16[768,1536]{1,0:T(8,128)(2,1)}, bf16[768,1536]{1,0:T(8,128)(2,1)}, bf16[1536,768]{1,0:T(8,128)(2,1)}, bf16[1536,768]{1,0:T(8,128)(2,1)}) custom-call(f32[256,768]{1,0:T(8,128)} %get-tuple-element.115.g_ref, bf16[256,3072]{1,0:T(8,128)(2,1)} %get-tuple-element.145.act_ref, bf16[256,768]{1,0:T(8,128)(2,1)} %get-tuple-element.146.a2_ref, ...), custom_call_target="tpu_custom_call" | custom-call | flops 2415919104 | bytes 13762560 | tf_op jit(solution)/shard_map/pallas_call | solution.py:372
  406.7 8.1 %shard_map.146 = (f32[256,768]{1,0:T(8,128)}, bf16[2304,256]{1,0:T(8,128)(2,1)}, f32[8,768]{1,0:T(8,128)}) custom-call(s32[4]{0:T(128)} %pad_add_fusion.place_ref, bf16[576,256]{1,0:T(8,128)(2,1)} %get-tuple-element.123.d0, bf16[576,256]{1,0:T(8,128)(2,1)} %copy-done.34, bf16[576,256]{1,0:T(8,128)(2,1)} %copy-done.35, bf16[576,256]{1,0:T(8,128)(2,1)} %copy-done.36, ...), custom_call_target="tpu_custom_call" | custom-call | flops 1509949440 | bytes 15777808 | tf_op jit(solution)/shard_map/pallas_call | solution.py:372
  457.6 8.8 %collective-permute-done.79 = bf16[2,192,1536]{2,1,0:T(8,128)(2,1)S(1)} collective-permute-done((bf16[2,192,1536]{2,1,0:T(8,128)(2,1)S(1)}, bf16[2,192,1536]{2,1,0:T(8,128)(2,1)S(1)}, u32[]{:S(2)}, u32[]{:S(2)}) %collective-permute-start.79) | collective-permute-done | bytes 1179680 | tf_op jit(solution)/shard_map/ppermute | solution.py:37
  466.4 25.5 %collective-permute-done.80 = bf16[2,192,1536]{2,1,0:T(8,128)(2,1)S(1)} collective-permute-done((bf16[2,192,1536]{2,1,0:T(8,128)(2,1)S(1)}, bf16[2,192,1536]{2,1,0:T(8,128)(2,1)S(1)}, u32[]{:S(2)}, u32[]{:S(2)}) %collective-permute-start.80) | collective-permute-done | bytes 1179680 | tf_op jit(solution)/shard_map/ppermute | solution.py:37
  506.5 14.6 %collective-permute-done.92 = bf16[2,384,768]{2,1,0:T(8,128)(2,1)} collective-permute-done((bf16[2,384,768]{2,1,0:T(8,128)(2,1)}, bf16[2,384,768]{2,1,0:T(8,128)(2,1)}, u32[]{:S(2)}, u32[]{:S(2)}) %collective-permute-start.92) | collective-permute-done | bytes 1179680 | tf_op jit(solution)/shard_map/ppermute | solution.py:37
  541.5 28.1 %collective-permute-done.95 = bf16[4,288,128]{2,1,0:T(8,128)(2,1)S(1)} collective-permute-done((bf16[4,288,128]{2,1,0:T(8,128)(2,1)}, bf16[4,288,128]{2,1,0:T(8,128)(2,1)S(1)}, u32[]{:S(2)}, u32[]{:S(2)}) %collective-permute-start.95) | collective-permute-done | bytes 294944 | tf_op jit(solution)/shard_map/ppermute | solution.py:37
  573.4 6.8 %collective-permute-done.93 = bf16[4,288,128]{2,1,0:T(8,128)(2,1)S(1)} collective-permute-done((bf16[4,288,128]{2,1,0:T(8,128)(2,1)}, bf16[4,288,128]{2,1,0:T(8,128)(2,1)S(1)}, u32[]{:S(2)}, u32[]{:S(2)}) %collective-permute-start.93) | collective-permute-done | bytes 294944 | tf_op jit(solution)/shard_map/ppermute | solution.py:37
  593.4 9.7 %collective-permute-start.72 = (bf16[4,300,128]{2,1,0:T(8,128)(2,1)}, bf16[4,300,128]{2,1,0:T(8,128)(2,1)S(1)}, u32[]{:S(2)}, u32[]{:S(2)}) collective-permute-start(bf16[4,300,128]{2,1,0:T(8,128)(2,1)} %squeeze.88), channel_id=1, source_target_pairs={{4,0},{6,2},{0,4},{2,6},{12,8},{14,10},{8,12},{10,14},{20,16},{22,... | collective-permute-start | bytes 921608 | tf_op jit(solution)/shard_map/ppermute | solution.py:37
  (454 shorter events, 309.5 us)
Async XLA Ops:
  36.2 43.3 %collective-permute-start.29 = (bf16[2,192,1536]{2,1,0:T(8,128)(2,1)}, bf16[2,192,1536]{2,1,0:T(8,128)(2,1)}, u32[]{:S(2)}, u32[]{:S(2)}) collective-permute-start(bf16[2,192,1536]{2,1,0:T(8,128)(2,1)} %reshape.555.refs_15_.refs_8_), channel_id=1, source_target_pairs={{8,0},{10,2},{12,4},{14,6},{0,8},{2,10},{4,12},{6,14},{24,16},{26,... | collective-permute-start | bytes 3538952 | tf_op jit(solution)/shard_map/ppermute | solution.py:37
  73.2 43.5 %collective-permute-start.9 = (bf16[2,96,3200]{2,1,0:T(8,128)(2,1)S(1)}, bf16[2,96,3200]{2,1,0:T(8,128)(2,1)S(1)}, u32[]{:S(2)}, u32[]{:S(2)}) collective-permute-start(bf16[2,96,3200]{2,1,0:T(8,128)(2,1)S(1)} %copy.69.refs_0_.refs_7_), channel_id=1, source_target_pairs={{17,0},{19,2},{21,4},{23,6},{25,8},{27,10},{29,12},{31,14},{0,16},... | collective-permute-start | bytes 3686408 | tf_op jit(solution)/shard_map/ppermute | solution.py:37
  73.9 42.8 %collective-permute-start.27 = (bf16[2,192,1536]{2,1,0:T(8,128)(2,1)}, bf16[2,192,1536]{2,1,0:T(8,128)(2,1)S(1)}, u32[]{:S(2)}, u32[]{:S(2)}) collective-permute-start(bf16[2,192,1536]{2,1,0:T(8,128)(2,1)} %reshape.555.refs_15_.refs_8_), channel_id=1, source_target_pairs={{4,0},{6,2},{0,4},{2,6},{12,8},{14,10},{8,12},{10,14},{20,16},{22,... | collective-permute-start | bytes 3538952 | tf_op jit(solution)/shard_map/ppermute | solution.py:37
  74.0 50.9 %collective-permute-start.8 = (bf16[2,96,3200]{2,1,0:T(8,128)(2,1)S(1)}, bf16[2,96,3200]{2,1,0:T(8,128)(2,1)}, u32[]{:S(2)}, u32[]{:S(2)}) collective-permute-start(bf16[2,96,3200]{2,1,0:T(8,128)(2,1)S(1)} %copy.69.refs_0_.refs_7_), channel_id=1, source_target_pairs={{1,0},{3,2},{5,4},{7,6},{9,8},{11,10},{13,12},{15,14},{17,16},{19,... | collective-permute-start | bytes 3686408 | tf_op jit(solution)/shard_map/ppermute | solution.py:37
  79.4 51.5 %collective-permute-start.7 = (bf16[2,96,3200]{2,1,0:T(8,128)(2,1)S(1)}, bf16[2,96,3200]{2,1,0:T(8,128)(2,1)}, u32[]{:S(2)}, u32[]{:S(2)}) collective-permute-start(bf16[2,96,3200]{2,1,0:T(8,128)(2,1)S(1)} %copy.69.refs_0_.refs_7_), channel_id=1, source_target_pairs={{16,0},{18,2},{20,4},{22,6},{24,8},{26,10},{28,12},{30,14},{1,16},... | collective-permute-start | bytes 3686408 | tf_op jit(solution)/shard_map/ppermute | solution.py:37
  91.6 56.9 %collective-permute-start.26 = (bf16[2,192,1536]{2,1,0:T(8,128)(2,1)}, bf16[2,192,1536]{2,1,0:T(8,128)(2,1)}, u32[]{:S(2)}, u32[]{:S(2)}) collective-permute-start(bf16[2,192,1536]{2,1,0:T(8,128)(2,1)} %reshape.555.refs_15_.refs_8_), channel_id=1, source_target_pairs={{2,0},{4,2},{6,4},{0,6},{10,8},{12,10},{14,12},{8,14},{18,16},{20,... | collective-permute-start | bytes 3538952 | tf_op jit(solution)/shard_map/ppermute | solution.py:37
  116.7 32.9 %collective-permute-start.13 = (bf16[2,96,3200]{2,1,0:T(8,128)(2,1)S(1)}, bf16[2,96,3200]{2,1,0:T(8,128)(2,1)}, u32[]{:S(2)}, u32[]{:S(2)}) collective-permute-start(bf16[2,96,3200]{2,1,0:T(8,128)(2,1)S(1)} %collective-permute-done.9.refs_3_.refs_10_), channel_id=1, source_target_pairs={{8,0},{10,2},{12,4},{14,6},{0,8},{2,10},{4,12},{6,14},{24,16},{26,... | collective-permute-start | bytes 3686408 | tf_op jit(solution)/shard_map/ppermute | solution.py:37
  149.0 54.7 %collective-permute-start.41 = (bf16[2,384,768]{2,1,0:T(8,128)(2,1)}, bf16[2,384,768]{2,1,0:T(8,128)(2,1)S(1)}, u32[]{:S(2)}, u32[]{:S(2)}) collective-permute-start(bf16[2,384,768]{2,1,0:T(8,128)(2,1)} %reshape.557.refs_23_.refs_16_), channel_id=1, source_target_pairs={{96,0},{98,2},{100,4},{102,6},{104,8},{106,10},{108,12},{110,14},{... | collective-permute-start | bytes 3538952 | tf_op jit(solution)/shard_map/ppermute | solution.py:37
  149.6 54.6 %collective-permute-start.40 = (bf16[2,384,768]{2,1,0:T(8,128)(2,1)}, bf16[2,384,768]{2,1,0:T(8,128)(2,1)S(1)}, u32[]{:S(2)}, u32[]{:S(2)}) collective-permute-start(bf16[2,384,768]{2,1,0:T(8,128)(2,1)} %reshape.557.refs_23_.refs_16_), channel_id=1, source_target_pairs={{64,0},{66,2},{68,4},{70,6},{72,8},{74,10},{76,12},{78,14},{80,16}... | collective-permute-start | bytes 3538952 | tf_op jit(solution)/shard_map/ppermute | solution.py:37
  153.0 52.9 %collective-permute-start.39 = (bf16[2,384,768]{2,1,0:T(8,128)(2,1)}, bf16[2,384,768]{2,1,0:T(8,128)(2,1)S(1)}, u32[]{:S(2)}, u32[]{:S(2)}) collective-permute-start(bf16[2,384,768]{2,1,0:T(8,128)(2,1)} %reshape.557.refs_23_.refs_16_), channel_id=1, source_target_pairs={{32,0},{34,2},{36,4},{38,6},{40,8},{42,10},{44,12},{46,14},{48,16}... | collective-permute-start | bytes 3538952 | tf_op jit(solution)/shard_map/ppermute | solution.py:37
  154.9 51.1 %collective-permute-start.32 = (bf16[2,192,1536]{2,1,0:T(8,128)(2,1)}, bf16[2,192,1536]{2,1,0:T(8,128)(2,1)S(1)}, u32[]{:S(2)}, u32[]{:S(2)}) collective-permute-start(bf16[2,192,1536]{2,1,0:T(8,128)(2,1)} %copy-done.4), channel_id=1, source_target_pairs={{8,0},{10,2},{12,4},{14,6},{0,8},{2,10},{4,12},{6,14},{24,16},{26,... | collective-permute-start | bytes 3538952 | tf_op jit(solution)/shard_map/ppermute | solution.py:37
  166.8 39.7 %collective-permute-start.14 = (bf16[576,256]{1,0:T(8,128)(2,1)}, bf16[576,256]{1,0:T(8,128)(2,1)S(1)}, u32[]{:S(2)}, u32[]{:S(2)}) collective-permute-start(bf16[576,256]{1,0:T(8,128)(2,1)} %get-tuple-element.84), channel_id=1, source_target_pairs={{2,0},{4,2},{6,4},{0,6},{10,8},{12,10},{14,12},{8,14},{18,16},{20,... | collective-permute-start | bytes 884744 | tf_op jit(solution)/shard_map/ppermute | solution.py:37
  342.0 82.5 %collective-permute-start.78 = (bf16[768,1536]{1,0:T(8,128)(2,1)}, bf16[768,1536]{1,0:T(8,128)(2,1)S(1)}, u32[]{:S(2)}, u32[]{:S(2)}) collective-permute-start(bf16[768,1536]{1,0:T(8,128)(2,1)} %get-tuple-element.154), channel_id=1, source_target_pairs={{8,0},{10,2},{12,4},{14,6},{0,8},{2,10},{4,12},{6,14},{24,16},{26,... | collective-permute-start | bytes 7077896 | tf_op jit(solution)/shard_map/ppermute | solution.py:37
  344.6 83.1 %collective-permute-start.89 = (bf16[1536,768]{1,0:T(8,128)(2,1)}, bf16[1536,768]{1,0:T(8,128)(2,1)}, u32[]{:S(2)}, u32[]{:S(2)}) collective-permute-start(bf16[1536,768]{1,0:T(8,128)(2,1)} %get-tuple-element.158), channel_id=1, source_target_pairs={{8,0},{10,2},{12,4},{14,6},{0,8},{2,10},{4,12},{6,14},{24,16},{26,... | collective-permute-start | bytes 7077896 | tf_op jit(solution)/shard_map/ppermute | solution.py:37
  405.4 42.3 %collective-permute-start.67 = (bf16[384,3200]{1,0:T(8,128)(2,1)}, bf16[384,3200]{1,0:T(8,128)(2,1)S(1)}, u32[]{:S(2)}, u32[]{:S(2)}) collective-permute-start(bf16[384,3200]{1,0:T(8,128)(2,1)} %get-tuple-element.144), channel_id=1, source_target_pairs={{8,0},{10,2},{12,4},{14,6},{0,8},{2,10},{4,12},{6,14},{24,16},{26,... | collective-permute-start | bytes 7372808 | tf_op jit(solution)/shard_map/ppermute | solution.py:37
  424.5 102.1 %collective-permute-start.65 = (f32[128,768]{1,0:T(8,128)}, f32[128,768]{1,0:T(8,128)}, u32[]{:S(2)}, u32[]{:S(2)}) collective-permute-start(f32[128,768]{1,0:T(8,128)} %slice.289), channel_id=1, source_target_pairs={{1,0},{3,2},{5,4},{7,6},{9,8},{11,10},{13,12},{15,14},{17,16},{19,... | collective-permute-start | bytes 1179656 | tf_op jit(solution)/shard_map/ppermute | solution.py:37
  438.0 53.9 %collective-permute-start.80 = (bf16[2,192,1536]{2,1,0:T(8,128)(2,1)S(1)}, bf16[2,192,1536]{2,1,0:T(8,128)(2,1)S(1)}, u32[]{:S(2)}, u32[]{:S(2)}) collective-permute-start(bf16[2,192,1536]{2,1,0:T(8,128)(2,1)S(1)} %pad_maximum_fusion.5), channel_id=1, source_target_pairs={{4,0},{6,2},{0,4},{2,6},{12,8},{14,10},{8,12},{10,14},{20,16},{22,... | collective-permute-start | bytes 3538952 | tf_op jit(solution)/shard_map/ppermute | solution.py:37
  447.7 44.4 %collective-permute-start.81 = (bf16[2,192,1536]{2,1,0:T(8,128)(2,1)S(1)}, bf16[2,192,1536]{2,1,0:T(8,128)(2,1)S(1)}, u32[]{:S(2)}, u32[]{:S(2)}) collective-permute-start(bf16[2,192,1536]{2,1,0:T(8,128)(2,1)S(1)} %pad_maximum_fusion.6), channel_id=1, source_target_pairs={{2,0},{4,2},{6,4},{0,6},{10,8},{12,10},{14,12},{8,14},{18,16},{20,... | collective-permute-start | bytes 3538952 | tf_op jit(solution)/shard_map/ppermute | solution.py:37
  451.4 53.8 %collective-permute-start.90 = (bf16[2,384,768]{2,1,0:T(8,128)(2,1)}, bf16[2,384,768]{2,1,0:T(8,128)(2,1)}, u32[]{:S(2)}, u32[]{:S(2)}) collective-permute-start(bf16[2,384,768]{2,1,0:T(8,128)(2,1)} %pad_maximum_fusion.7), channel_id=1, source_target_pairs={{96,0},{98,2},{100,4},{102,6},{104,8},{106,10},{108,12},{110,14},{... | collective-permute-start | bytes 3538952 | tf_op jit(solution)/shard_map/ppermute | solution.py:37
  466.4 40.1 %collective-permute-start.91 = (bf16[2,384,768]{2,1,0:T(8,128)(2,1)}, bf16[2,384,768]{2,1,0:T(8,128)(2,1)}, u32[]{:S(2)}, u32[]{:S(2)}) collective-permute-start(bf16[2,384,768]{2,1,0:T(8,128)(2,1)} %pad_maximum_fusion.8), channel_id=1, source_target_pairs={{64,0},{66,2},{68,4},{70,6},{72,8},{74,10},{76,12},{78,14},{80,16}... | collective-permute-start | bytes 3538952 | tf_op jit(solution)/shard_map/ppermute | solution.py:37
  492.1 90.0 %collective-permute-start.68 = (bf16[2,96,3200]{2,1,0:T(8,128)(2,1)}, bf16[2,96,3200]{2,1,0:T(8,128)(2,1)}, u32[]{:S(2)}, u32[]{:S(2)}) collective-permute-start(bf16[2,96,3200]{2,1,0:T(8,128)(2,1)} %pad_maximum_fusion.1), channel_id=1, source_target_pairs={{17,0},{19,2},{21,4},{23,6},{25,8},{27,10},{29,12},{31,14},{0,16},... | collective-permute-start | bytes 3686408 | tf_op jit(solution)/shard_map/ppermute | solution.py:37
  505.3 76.9 %collective-permute-start.69 = (bf16[2,96,3200]{2,1,0:T(8,128)(2,1)}, bf16[2,96,3200]{2,1,0:T(8,128)(2,1)}, u32[]{:S(2)}, u32[]{:S(2)}) collective-permute-start(bf16[2,96,3200]{2,1,0:T(8,128)(2,1)} %pad_maximum_fusion.2), channel_id=1, source_target_pairs={{1,0},{3,2},{5,4},{7,6},{9,8},{11,10},{13,12},{15,14},{17,16},{19,... | collective-permute-start | bytes 3686408 | tf_op jit(solution)/shard_map/ppermute | solution.py:37
  526.5 55.7 %collective-permute-start.70 = (bf16[2,96,3200]{2,1,0:T(8,128)(2,1)}, bf16[2,96,3200]{2,1,0:T(8,128)(2,1)}, u32[]{:S(2)}, u32[]{:S(2)}) collective-permute-start(bf16[2,96,3200]{2,1,0:T(8,128)(2,1)} %pad_maximum_fusion.3), channel_id=1, source_target_pairs={{16,0},{18,2},{20,4},{22,6},{24,8},{26,10},{28,12},{30,14},{1,16},... | collective-permute-start | bytes 3686408 | tf_op jit(solution)/shard_map/ppermute | solution.py:37
  534.4 35.2 %collective-permute-start.95 = (bf16[4,288,128]{2,1,0:T(8,128)(2,1)}, bf16[4,288,128]{2,1,0:T(8,128)(2,1)S(1)}, u32[]{:S(2)}, u32[]{:S(2)}) collective-permute-start(bf16[4,288,128]{2,1,0:T(8,128)(2,1)} %select_n.403), channel_id=1, source_target_pairs={{16,0},{18,2},{20,4},{22,6},{24,8},{26,10},{28,12},{30,14},{1,16},... | collective-permute-start | bytes 884744 | tf_op jit(solution)/shard_map/ppermute | solution.py:37
  (141 other events, 2083.0 us)

commit v2 on v1

v2 whole, which is shorter than its diff:
```python
import functools

import jax
import jax.numpy as jnp
from jax import lax
from jax.experimental import pallas as pl
from jax.experimental.pallas import tpu as pltpu
from jax.sharding import PartitionSpec as P

D = 768
FF = 3072
HEAD_DIM = 64
GROUP = 192
TOKENS = 256
EPS = 1e-06
ROOT_HALF = 0.7071067811865476
INV_ROOT_TWO_PI = 0.3989422804014327
ROW_A = 3200
BF = jnp.bfloat16
F32 = jnp.float32
AXES = ("wide", "narrow")
VMEM_LIMIT = 56 * 1024 * 1024


def index_of(z, y, c, x):
    return ((z * 2 + y % 2) * 2 + c) * 8 + x * 2 + y // 2


def everywhere():
    for z in range(4):
        for y in range(4):
            for c in range(2):
                for x in range(4):
                    yield {"z": z, "y": y, "c": c, "x": x}


def fetch(value, axis, step):
    pairs = []
    for here in everywhere():
        there = dict(here)
        there[axis] = (here[axis] + step) % (2 if axis == "c" else 4)
        pairs.append((index_of(**there), index_of(**here)))
    return lax.ppermute(value, AXES, pairs)


def swap(value, axis, side):
    pairs = []
    for here in everywhere():
        step = side if (here[axis] + here["c"]) % 2 == 0 else -side
        there = dict(here)
        there[axis] = (here[axis] + step) % 4
        pairs.append((index_of(**here), index_of(**there)))
    return lax.ppermute(value, AXES, pairs)


def exchange_four(pieces):
    return [pieces[0]] + [fetch(pieces[4 - k], "x", k) for k in (1, 2, 3)]


def dot(left, right, over_left=1, over_right=0):
    return lax.dot_general(
        left, right, (((over_left,), (over_right,)), ((), ())), preferred_element_type=F32
    )


def dot_two(left, right, over_left=1, over_right=0):
    high = left.astype(BF)
    low = (left - high.astype(F32)).astype(BF)
    return dot(high, right, over_left, over_right) + dot(low, right, over_left, over_right)


def normed(values):
    average = jnp.mean(values, -1, keepdims=True)
    centred = values - average
    spread = jnp.mean(centred * centred, -1, keepdims=True)
    scale = lax.rsqrt(spread + EPS)
    return centred * scale, scale


def norm_back(grad, values, gain_row):
    z, scale = normed(values)
    dz = grad * gain_row
    out = (
        dz - jnp.mean(dz, -1, keepdims=True) - z * jnp.mean(dz * z, -1, keepdims=True)
    ) * scale
    gain_grad = jnp.sum(grad * z, 0, keepdims=True)
    offset_grad = jnp.sum(grad, 0, keepdims=True)
    return out, gain_grad, offset_grad


def two_rows(first, second):
    return jnp.concatenate([first, second, jnp.zeros((6, D), F32)], 0)


def group_start(x, k, base=0):
    return pl.multiple_of(base + lax.rem(x + k, 4) * GROUP, GROUP)


def start_copies(pairs, sems):
    copies = [
        pltpu.make_async_copy(source, target, sems.at[i])
        for i, (source, target) in enumerate(pairs)
    ]
    for copy in copies:
        copy.start()
    return copies


def wait_copies(copies):
    for copy in copies:
        copy.wait()


X, HIGH, LENGTH, NEAR_X, NEAR_Y, NEAR_Z, LOW = range(7)


def weight_blocks(refs, near):
    pair, far, core_pair, core_far = refs
    return [
        (pair, 0, 0, 0),
        (pair, 1, 0, near),
        (far, 0, 0, 3 - near),
        (far, 1, 0, 3),
        (core_pair, 0, 1, 0),
        (core_pair, 1, 1, 3 - near),
        (core_far, 0, 1, near),
        (core_far, 1, 1, 3),
    ]


def at_rows(core, spot, rows):
    return pl.ds(pl.multiple_of((core * 4 + spot) * rows, rows), rows)


def qkv_kernel(place_ref, h_ref, pa_ref, *refs):
    blocks = weight_blocks(refs[:4], place_ref[NEAR_Y])
    a1p_keep, a1p_send, gains_ref = refs[4:7]
    out_refs = refs[7:11]
    win, table, turned, sems = refs[11:]
    norm_copies = start_copies(
        [
            (r.at[i, :, pl.ds(FF, 128)], table.at[at_rows(core, spot, 96)])
            for r, i, core, spot in blocks
        ],
        sems.at[pl.ds(0, 8)],
    )
    win_copies = start_copies(
        [
            (r.at[i, :, pl.ds(0, 3 * D)], win.at[at_rows(core, spot, 96)])
            for r, i, core, spot in blocks
        ],
        sems.at[pl.ds(8, 8)],
    )
    z, _ = normed(h_ref[...])
    wait_copies(norm_copies)
    gains = dot(table[...], pa_ref[...], 0, 1)[0:8]
    gains_ref[...] = gains
    a1 = (z * gains[0:1] + gains[1:2]).astype(BF)
    a1p = dot(a1, pa_ref[...]).astype(BF)
    a1p_keep[...] = a1p[:, :384]
    a1p_send[...] = a1p[:, 384:]
    wait_copies(win_copies)
    for c in range(3):
        part = dot(a1p, win[:, c * D : (c + 1) * D])
        if c == 0:
            part = part * HEAD_DIM ** (-0.5)
        turned[c * D : (c + 1) * D, :] = part.astype(BF).T
    x = place_ref[X]
    for k in range(4):
        for c in range(3):
            out_refs[k][c * GROUP : (c + 1) * GROUP, :] = turned[
                pl.ds(group_start(x, k, c * D), GROUP), :
            ]


def key_bias(place_ref, bias):
    x, yh, length = place_ref[0], place_ref[1], place_ref[2]
    for k in range(4):
        for half in range(2):
            start = lax.rem(x + k, 4) * 256 + lax.rem(yh + half, 2) * 128
            slot = start + lax.broadcasted_iota(jnp.int32, (128, TOKENS), 0)
            bias[pl.ds(k * 256 + half * 128, 128), :] = jnp.where(slot < length, 0.0, -1e30)


def side_by_side(refs, start):
    return jnp.concatenate([r[start : start + HEAD_DIM, :] for r in refs], 1)


def attend_kernel(place_ref, t0, t1, t2, t3, u0, u1, u2, u3, sums_ref, bias):
    t_refs, u_refs = (t0, t1, t2, t3), (u0, u1, u2, u3)
    key_bias(place_ref, bias)
    for j in range(3):
        keys = side_by_side(t_refs, GROUP + j * HEAD_DIM).T
        values_t = side_by_side(t_refs, 2 * GROUP + j * HEAD_DIM)
        for b in range(4):
            query_t = t_refs[b][j * HEAD_DIM : (j + 1) * HEAD_DIM, :]
            scores = dot(keys, query_t) + bias[...]
            peak = jnp.max(scores, 0, keepdims=True)
            expont = jnp.exp(scores - peak)
            total = jnp.sum(expont, 0, keepdims=True)
            mixed = dot(values_t, expont.astype(BF)) / total
            u_refs[b][j * HEAD_DIM : (j + 1) * HEAD_DIM, :] = mixed.astype(BF)
            sums_ref[j : j + 1, b * TOKENS : (b + 1) * TOKENS] = peak + jnp.log(total)


def attend_back_kernel(place_ref, *refs):
    t_refs, g_refs, u_refs = refs[0:4], refs[4:8], refs[8:12]
    sums_ref = refs[12]
    out_refs = refs[13:17]
    bias = refs[17]
    key_bias(place_ref, bias)
    for j in range(3):
        keys_t = side_by_side(t_refs, GROUP + j * HEAD_DIM)
        keys = keys_t.T
        values = side_by_side(t_refs, 2 * GROUP + j * HEAD_DIM).T
        grad_keys = jnp.zeros((4 * TOKENS, HEAD_DIM), F32)
        grad_values = jnp.zeros((4 * TOKENS, HEAD_DIM), F32)
        rows = slice(j * HEAD_DIM, (j + 1) * HEAD_DIM)
        for b in range(4):
            query_t = t_refs[b][rows, :]
            grad_t = g_refs[b][rows, :]
            scores = dot(keys, query_t) + bias[...]
            probs = jnp.exp(scores - sums_ref[j : j + 1, b * TOKENS : (b + 1) * TOKENS])
            grad_probs = dot(values, grad_t)
            delta = jnp.sum(
                grad_t.astype(F32) * u_refs[b][rows, :].astype(F32), 0, keepdims=True
            )
            grad_scores = (probs * (grad_probs - delta)).astype(BF)
            grad_values = grad_values + dot(probs.astype(BF), grad_t, 1, 1)
            grad_keys = grad_keys + dot(grad_scores, query_t, 1, 1)
            grad_query = dot(keys_t, grad_scores) * HEAD_DIM ** (-0.5)
            out_refs[b][rows, :] = grad_query.astype(BF)
        grad_keys = grad_keys.astype(BF).T
        grad_values = grad_values.astype(BF).T
        for b in range(4):
            columns = slice(b * TOKENS, (b + 1) * TOKENS)
            start = GROUP + j * HEAD_DIM
            out_refs[b][start : start + HEAD_DIM, :] = grad_keys[:, columns]
            start = 2 * GROUP + j * HEAD_DIM
            out_refs[b][start : start + HEAD_DIM, :] = grad_values[:, columns]


def mlp_copies(place_ref, refs, wout, w1, w2, sems):
    out_copies = start_copies(
        [
            (r.at[i, :, pl.ds(3 * D, D)], wout.at[at_rows(core, spot, 96)])
            for r, i, core, spot in weight_blocks(refs[0:4], place_ref[NEAR_Y])
        ],
        sems.at[pl.ds(0, 8)],
    )
    first_copies = start_copies(
        [
            (r.at[i], w1.at[core, at_rows(0, spot, 192)])
            for r, i, core, spot in weight_blocks(refs[4:8], place_ref[NEAR_X])
        ],
        sems.at[pl.ds(8, 8)],
    )
    second_copies = start_copies(
        [
            (r.at[i], w2.at[:, at_rows(core, spot, 384)])
            for r, i, core, spot in weight_blocks(refs[8:12], place_ref[NEAR_Z])
        ],
        sems.at[pl.ds(16, 8)],
    )
    return out_copies, first_copies, second_copies


def mlp_kernel(place_ref, h_ref, u0, u1, u2, u3, a1p_send, po_ref, p2_ref, gains_ref, *refs):
    h1_ref, next_ref, slope_ref, send_ref, op_keep, act_keep = refs[12:18]
    turned, wout, w1, w2, sems = refs[18:]
    out_copies, first_copies, second_copies = mlp_copies(
        place_ref, refs[:12], wout, w1, w2, sems
    )
    send_ref[:, 0:384] = a1p_send[...]
    x = place_ref[X]
    for k, piece in enumerate((u0, u1, u2, u3)):
        turned[pl.ds(group_start(x, k), GROUP), :] = piece[...]
    op = dot(turned[...], po_ref[...], 0, 0).astype(BF)
    op_keep[...] = op[:, :384]
    send_ref[:, 384:768] = op[:, 384:]
    wait_copies(out_copies)
    h1 = h_ref[...] + dot_two(dot(op, wout[...]), p2_ref[...])
    h1_ref[...] = h1
    z, _ = normed(h1)
    a2 = (z * gains_ref[2:3] + gains_ref[3:4]).astype(BF)
    send_ref[:, 768:1536] = a2
    wait_copies(first_copies)
    total = h1
    for half in range(2):
        pre = dot(a2, w1[half])
        below = 0.5 * (1.0 + lax.erf(pre * ROOT_HALF))
        act = (pre * below).astype(BF)
        slope = below + pre * (jnp.exp(-0.5 * pre * pre) * INV_ROOT_TWO_PI)
        columns = slice(half * 1536, (half + 1) * 1536)
        if half == 0:
            act_keep[...] = act
            wait_copies(second_copies)
        else:
            send_ref[:, 1536:] = act
        slope_ref[:, columns] = slope.astype(BF)
        total = total + dot(act, w2[:, columns], 1, 1)
    next_ref[...] = total


def mlp_back_kernel(place_ref, g_ref, slope_ref, h1_ref, gains_ref, p2_ref, po_ref, *refs):
    g1_ref, send_ref, dpre_keep, norm_ref = refs[12:16]
    out_refs = refs[16:20]
    turned, wout, w1, w2, sems = refs[20:]
    out_copies, first_copies, second_copies = mlp_copies(
        place_ref, refs[:12], wout, w1, w2, sems
    )
    grad = g_ref[...]
    grad_low = grad.astype(BF)
    send_ref[:, 1536:2304] = grad_low
    wait_copies(second_copies)
    grad_a2 = jnp.zeros((TOKENS, D), F32)
    for half in range(2):
        columns = slice(half * 1536, (half + 1) * 1536)
        grad_act = dot(grad_low, w2[:, columns])
        dpre = (grad_act * slope_ref[:, columns].astype(F32)).astype(BF)
        if half == 0:
            dpre_keep[...] = dpre
            wait_copies(first_copies)
        else:
            send_ref[:, 0:1536] = dpre
        grad_a2 = grad_a2 + dot(dpre, w1[half], 1, 1)
    dv, gain_grad, offset_grad = norm_back(grad_a2, h1_ref[...], gains_ref[2:3])
    norm_ref[...] = two_rows(gain_grad, offset_grad)
    g1 = grad + dv
    g1_ref[...] = g1
    g1b = dot(g1.astype(BF), p2_ref[...], 1, 1).astype(BF)
    send_ref[:, 2304:] = g1b
    wait_copies(out_copies)
    grad_op = dot(g1b, wout[...], 1, 1).astype(BF)
    turned[...] = dot(po_ref[...], grad_op, 1, 1).astype(BF)
    x = place_ref[X]
    for k in range(4):
        out_refs[k][...] = turned[pl.ds(group_start(x, k), GROUP), :]


def both_cores(first_ref, second_ref):
    return jnp.concatenate([first_ref[...], second_ref[...]], 0)


def store_blocks(near, mine, send, columns, blocks):
    mine[0, :, columns] = blocks[0]
    send[1, :, columns] = blocks[3]

    @pl.when(near == 1)
    def _():
        mine[1, :, columns] = blocks[1]
        send[0, :, columns] = blocks[2]

    @pl.when(near == 2)
    def _():
        mine[1, :, columns] = blocks[2]
        send[0, :, columns] = blocks[1]


def mlp_grad_kernel(
    place_ref, a2_0, a2_1, act_0, act_1, dpre_0, dpre_1, gb_0, gb_1,
    first_mine, first_send, second_mine, second_send,
):
    a2 = both_cores(a2_0, a2_1)
    grad_low = both_cores(gb_0, gb_1)
    dpre = both_cores(dpre_0, dpre_1)
    for part in range(2):
        columns = slice(part * 768, part * 768 + 768)
        value = dot(a2, dpre[:, columns], 0, 0).astype(BF)
        blocks = [value[192 * k : 192 * k + 192] for k in range(4)]
        store_blocks(place_ref[NEAR_X], first_mine, first_send, columns, blocks)
    act = both_cores(act_0, act_1)
    blocks = [
        dot(grad_low, act[:, 384 * k : 384 * k + 384], 0, 0).astype(BF) for k in range(4)
    ]
    store_blocks(place_ref[NEAR_Z], second_mine, second_send, slice(0, 384), blocks)


def qkv_back_kernel(
    place_ref, d0, d1, d2, d3, h_ref, g1_ref, gains_ref, pa_ref, norm2_ref, *refs
):
    blocks = weight_blocks(refs[:4], place_ref[NEAR_Y])
    next_ref, dqkv_ref, norm_ref, win, sems = refs[4:]
    win_copies = start_copies(
        [
            (r.at[i, :, pl.ds(0, 3 * D)], win.at[at_rows(core, spot, 96)])
            for r, i, core, spot in blocks
        ],
        sems,
    )
    x = place_ref[X]
    for k, piece in enumerate((d0, d1, d2, d3)):
        for c in range(3):
            dqkv_ref[pl.ds(group_start(x, k, c * D), GROUP), :] = piece[
                c * GROUP : (c + 1) * GROUP, :
            ]
    wait_copies(win_copies)
    turned = dot(win[...], dqkv_ref[...])
    grad_a1 = dot_two(turned, pa_ref[...], 0, 1)
    dv, gain_grad, offset_grad = norm_back(grad_a1, h_ref[...], gains_ref[0:1])
    norm_ref[...] = jnp.concatenate(
        [gain_grad, offset_grad, norm2_ref[0:2], jnp.zeros((4, D), F32)], 0
    )
    next_ref[...] = g1_ref[...] + dv


def attn_grad_kernel(
    place_ref, a1p_0, a1p_1, op_0, op_1, g1b_0, g1b_1, dqkv_0, dqkv_1, norm_0, norm_1, pa_ref,
    mine, send,
):
    near = place_ref[NEAR_Y]
    norms = norm_0[...] + norm_1[...]
    norms = dot_two(norms, pa_ref[:, 0:384])
    norms = jnp.concatenate([norms, jnp.zeros((120, 384), F32)], 0).T.astype(BF)
    a1p = both_cores(a1p_0, a1p_1)
    for c in range(5):
        columns = slice(c * D, min((c + 1) * D, ROW_A))
        if c < 3:
            dqkv = jnp.concatenate(
                [dqkv_0[c * D : (c + 1) * D, :], dqkv_1[c * D : (c + 1) * D, :]], 1
            )
            value = dot(a1p, dqkv, 0, 1).astype(BF)
        elif c == 3:
            value = dot(both_cores(op_0, op_1), both_cores(g1b_0, g1b_1), 0, 0).astype(BF)
        else:
            value = norms
        blocks = [value[96 * k : 96 * k + 96] for k in range(4)]
        store_blocks(near, mine, send, columns, blocks)


def join_kernel(*refs):
    count = (len(refs) - 1) // 3
    pairs = []
    for own, came, out in zip(refs[:count], refs[count : 2 * count], refs[2 * count : -1]):
        pairs += [(own, out.at[0]), (came, out.at[1])]
    wait_copies(start_copies(pairs, refs[-1]))


def order_kernel(spots, place_ref, *refs):
    count = len(spots)
    pairs = []
    for spot, pair, far, out in zip(
        spots, refs[:count], refs[count : 2 * count], refs[2 * count : -1]
    ):
        near = place_ref[spot]
        pairs += [
            (pair.at[0], out.at[0]),
            (pair.at[1], out.at[near]),
            (far.at[0], out.at[3 - near]),
            (far.at[1], out.at[3]),
        ]
    wait_copies(start_copies(pairs, refs[-1]))


def layer_blocks_kernel(layer, place_ref, b_ref, c_ref, first_ref, second_ref):
    middle = 1 + place_ref[LOW]
    part = slice(layer * 192, layer * 192 + 192)
    for high in range(2):
        one, two = (0, middle) if high == 0 else (3, 3 - middle)
        for k in range(4):
            both = [b_ref[k, one][:, part], b_ref[k, two][:, part]]
            first_ref[high * 96 : high * 96 + 96, k * 384 : k * 384 + 384] = jnp.concatenate(
                both, 1
            )
            both = [c_ref[one, k][:, part], c_ref[two, k][:, part]]
            start = (2 * k + high) * 96
            second_ref[start : start + 96, :] = jnp.concatenate(both, 1)


def both_layers_kernel(place_ref, *refs):
    b0, b0_came, c0, c0_came, b1, b1_came, c1, c1_came = refs[:8]
    b_mine, b_send, c_mine, c_send = refs[8:]
    middle = 1 + place_ref[LOW]
    near_z, near_x = place_ref[NEAR_Z], place_ref[NEAR_X]

    def put(mine, send, near, spot, index, value):
        if isinstance(spot, int) and spot == 0:
            mine[0, index] = value
        elif isinstance(spot, int) and spot == 3:
            send[1, index] = value
        else:

            @pl.when(near == spot)
            def _():
                mine[1, index] = value

            @pl.when(near != spot)
            def _():
                send[0, index] = value

    for high in range(2):
        for k in range(4):
            rows, columns = slice(high * 96, high * 96 + 96), slice(k * 384, k * 384 + 384)
            b_parts = [
                total_of(b0[rows, columns], b0_came[rows, columns]),
                total_of(b1[rows, columns], b1_came[rows, columns]),
            ]
            rows = slice((2 * k + high) * 96, (2 * k + high) * 96 + 96)
            c_parts = [
                total_of(c0[rows, :], c0_came[rows, :]),
                total_of(c1[rows, :], c1_came[rows, :]),
            ]
            for part in range(2):
                if part == 0:
                    spot = 0 if high == 0 else 3
                else:
                    spot = middle if high == 0 else 3 - middle
                columns = slice(part * 192, part * 192 + 192)
                value = jnp.concatenate([v[:, columns] for v in b_parts], 1)
                put(b_mine, b_send, near_z, k, spot, value)
                value = jnp.concatenate([v[:, columns] for v in c_parts], 1)
                put(c_mine, c_send, near_x, k, spot, value)


def split_kernel(spots, place_ref, *refs):
    count = len(spots)
    for n, spot in enumerate(spots):
        near = place_ref[spot]
        value, mine, send = refs[n], refs[count + 2 * n], refs[count + 2 * n + 1]
        mine[0] = value[0]
        mine[1] = value[near]
        send[0] = value[3 - near]
        send[1] = value[3]


def total_of(first, second):
    return (first.astype(F32) + second.astype(F32)).astype(BF)


def halve_kernel(*refs):
    count = len(refs) // 4
    for n in range(count):
        mine, came = refs[n], refs[count + n]
        keep, send = refs[2 * count + 2 * n], refs[2 * count + 2 * n + 1]
        keep[...] = total_of(mine[0], came[0])
        send[...] = total_of(mine[1], came[1])


def total_kernel(keep, came, *out_refs):
    for k, out in enumerate(out_refs):
        out[...] = total_of(keep[k], came[k])


def total_split_kernel(spots, place_ref, *refs):
    count = len(spots)
    for n, spot in enumerate(spots):
        near = place_ref[spot]
        keep, came = refs[n], refs[count + n]
        mine, send = refs[2 * count + 2 * n], refs[2 * count + 2 * n + 1]
        mine[0] = total_of(keep[0], came[0])
        mine[1] = total_of(keep[near], came[near])
        send[0] = total_of(keep[3 - near], came[3 - near])
        send[1] = total_of(keep[3], came[3])


def nothing_kernel(*refs):
    pass


def after(values, done):
    anywhere = pl.BlockSpec(memory_space=pl.ANY)
    return pl.pallas_call(
        nothing_kernel,
        out_shape=tuple(jax.ShapeDtypeStruct(v.shape, v.dtype) for v in values),
        in_specs=[anywhere] * (len(values) + len(done)),
        out_specs=tuple(anywhere for _ in values),
        input_output_aliases={i: i for i in range(len(values))},
    )(*values, *done)


def shaped(*shape, dtype=BF):
    return jax.ShapeDtypeStruct(shape, dtype)


def like(value, *lead):
    return jax.ShapeDtypeStruct(tuple(lead) + tuple(value.shape), value.dtype)


def run_kernel(
    kernel, inputs, outs, scratch=(), flops=0, any_count=0, scalars=True, lying=False, done=()
):
    specs, arrays, moved = [], [], 0
    anywhere = pl.BlockSpec(memory_space=pl.ANY)
    for i, value in enumerate(inputs):
        if isinstance(value, tuple):
            value, width, index = value
            specs.append(pl.BlockSpec((value.shape[0], width), lambda _, n=index: (0, n)))
            moved += value.shape[0] * width * value.dtype.itemsize
        elif scalars and i == 0:
            specs.append(pl.BlockSpec(memory_space=pltpu.SMEM))
        else:
            lies = lying or i >= len(inputs) - any_count
            specs.append(anywhere if lies else pl.BlockSpec(memory_space=pltpu.VMEM))
            moved += value.size * value.dtype.itemsize
        arrays.append(value)
    moved += sum(v.size * v.dtype.itemsize for v in outs)
    count, extra = len(inputs), len(done)

    def whole(*refs):
        kernel(*refs[:count], *refs[count + extra :])

    return pl.pallas_call(
        whole,
        grid=(1,),
        out_shape=tuple(outs),
        in_specs=specs + [anywhere] * extra,
        out_specs=tuple(
            pl.BlockSpec(memory_space=pltpu.VMEM) for _ in outs
        ),
        scratch_shapes=list(scratch),
        compiler_params=pltpu.CompilerParams(vmem_limit_bytes=VMEM_LIMIT),
        cost_estimate=pl.CostEstimate(flops=flops, bytes_accessed=moved, transcendentals=0),
    )(*arrays, *done)


MLP_SCRATCH = (
    pltpu.VMEM((D, TOKENS), BF),
    pltpu.VMEM((D, D), BF),
    pltpu.VMEM((2, D, 1536), BF),
    pltpu.VMEM((D, FF), BF),
    pltpu.SemaphoreType.DMA((24,)),
)
UNIT = 2 * TOKENS * D * D
ATTEND = 2 * 3 * 1024 * 1024 * HEAD_DIM * 4


NEAR = {"x": NEAR_X, "y": NEAR_Y, "z": NEAR_Z}


def swaps(values, axes, side):
    return [swap(v, axis, side) for v, axis in zip(values, axes)]


def join(values, came, done=()):
    return list(
        run_kernel(
            join_kernel,
            values + came,
            [like(v, 2) for v in values],
            (pltpu.SemaphoreType.DMA((2 * len(values),)),),
            scalars=False,
            lying=True,
            done=done,
        )
    )


def gather_round(place, values, axes, done=()):
    pairs = join(values, swaps(values, axes, 1))
    far = swaps(pairs, axes, -1)
    return list(
        run_kernel(
            functools.partial(order_kernel, [NEAR[axis] for axis in axes]),
            [place] + pairs + far,
            [like(v, 4) for v in values],
            (pltpu.SemaphoreType.DMA((4 * len(values),)),),
            lying=True,
            done=done,
        )
    )


def padded(value):
    return jnp.pad(value.reshape(300, 128), ((0, 4), (0, 0)))


def weights_around(place, norm_params, attn_in, attn_out, mlp_in, mlp_out, done):
    norm_part = jnp.pad(jnp.swapaxes(norm_params, 1, 2), ((0, 0), (0, 0), (0, 124)))
    a = padded(jnp.concatenate([attn_in, attn_out, norm_part], -1))
    b = mlp_in.transpose(1, 0, 2).reshape(96, 384)
    c = mlp_out.transpose(2, 0, 1).reshape(96, 384)
    values = gather_round(place, [a, b, c], "zyx")
    a, b, c = gather_round(place, values, "xzy", done)
    a = a[:, :, :300].reshape(4, 4, 2, 6, ROW_A)
    layers = []
    for layer in range(2):
        al = a[:, :, layer].transpose(1, 0, 2, 3).reshape(96, ROW_A)
        bl, cl = run_kernel(
            functools.partial(layer_blocks_kernel, layer),
            [place, b, c],
            [shaped(192, 1536), shaped(768, 384)],
        )
        layers.append([al, bl, cl])
    return layers


LAST = "yxz"


def with_core(value):
    return fetch(value, "c", 1)


def halved(mine, came, done=()):
    outs = [like(v[0]) for v in mine for _ in range(2)]
    out = run_kernel(halve_kernel, list(mine) + list(came), outs, scalars=False, done=done)
    return list(out[0::2]), list(out[1::2])


def turn_rings(place, keep, came, later, done=()):
    halves = [like(v[0], 2) for v in keep for _ in range(2)]
    out = run_kernel(
        functools.partial(total_split_kernel, [NEAR[axis] for axis in later]),
        [place] + keep + came,
        halves,
        done=done,
    )
    return list(out[0::2]), list(out[1::2])


def total(keep, came):
    return (keep.astype(F32) + came.astype(F32)).astype(BF)


def gradients_home(place, a_layers, b_layers, c_layers, behind):
    b_mine, b_send, c_mine, c_send = run_kernel(
        both_layers_kernel,
        [place] + b_layers[0] + c_layers[0] + b_layers[1] + c_layers[1],
        [shaped(2, 4, 96, 384)] * 4,
    )
    mine, send = [b_mine, c_mine], [b_send, c_send]
    keep, send = halved(mine, swaps(send, "zx", -1), done=behind)
    came = swaps(send, "zx", 1)

    parts = [v.reshape(4, 4, 6, ROW_A).transpose(1, 0, 2, 3) for v in a_layers]
    a = jnp.stack(parts, 2).reshape(4, 4, 300, 128)
    a = jnp.pad(a, ((0, 0), (0, 0), (0, 4), (0, 0)))
    a_mine, a_send = run_kernel(
        functools.partial(split_kernel, [NEAR_X]), [place, a], [like(a[0], 2)] * 2
    )
    a_came = swap(a_send, "x", -1)
    mine, send = turn_rings(place, keep, came, "yy", done=[a_mine])
    came = swaps(send, "yy", -1)
    (a_keep,), (a_send,) = halved([a_mine], [a_came], done=[mine[0]])
    a_came = swap(a_send, "x", 1)
    keep, send = halved(mine, came, done=[a_keep])
    came = swaps(send, "yy", 1)
    parts = run_kernel(
        total_kernel, [a_keep, a_came], [like(a_keep[0])] * 4, scalars=False, done=[keep[0]]
    )
    b, c = [k.astype(F32) + v.astype(F32) for k, v in zip(keep, came)]
    a = parts[0].astype(F32)
    for part, step in zip(parts[1:], (-1, 1, 2)):
        a = a + fetch(part, "z", step).astype(F32)
    a = a[:300].reshape(2, 6, ROW_A)
    return (
        jnp.swapaxes(a[:, :, 4 * D : 4 * D + 4], 1, 2),
        a[:, :, : 3 * D],
        a[:, :, 3 * D : 4 * D],
        b.reshape(96, 2, 192).transpose(1, 0, 2),
        c.reshape(96, 2, 192).transpose(1, 2, 0),
    )


def body(inputs, lengths, norm_params, attn_in, attn_out, mlp_in, mlp_out, cotangent):
    wide = lax.axis_index("wide")
    narrow = lax.axis_index("narrow")
    core, low, z = wide % 2, (wide // 2) % 2, wide // 4
    x, high = narrow // 2, narrow % 2
    y = high * 2 + low
    length = lax.dynamic_index_in_dim(lengths[:, 0], high, 0, keepdims=False)
    near = [1 + (v + core) % 2 for v in (x, y, z)]
    place = jnp.stack([x, high, length] + near + [low]).astype(jnp.int32)

    def weights_of(pairs, far):
        return [[p, f, with_core(p), with_core(f)] for p, f in zip(pairs, far)]

    def behind(values, done):
        return list(after(values, done))

    slot = jnp.arange(D, dtype=jnp.int32)
    step = jnp.array([0, 1, 3, 2], jnp.int32)
    own_order = ((x + step[slot // 192]) % 4) * 192 + ((high + (slot // 96) % 2) % 2) * 96 + slot % 96
    row_core = (core + slot // 384) % 2
    row_y = (y + step[(slot // 96) % 4]) % 4
    row_z = (z + step[(slot // 24) % 4]) % 4
    row_x = (x + step[(slot // 6) % 4]) % 4
    row_order = 6 * index_of(row_z, row_y, row_core, row_x) + slot % 6
    pa = (own_order[:, None] == row_order[None, :]).astype(BF)
    po = (slot[:, None] == row_order[None, :]).astype(BF)
    p2 = (slot[:, None] == own_order[None, :]).astype(BF)

    def mine_and_other(values):
        mine = lax.dynamic_index_in_dim(values[:, 0], high, 0, keepdims=False)
        return mine, lax.dynamic_index_in_dim(values[:, 0], 1 - high, 0, keepdims=False)

    def in_own_order(mine, came):
        return dot(jnp.concatenate([mine, came], 0), p2)

    mine, other = mine_and_other(inputs)
    other = fetch(other, "y", 2)
    hidden = in_own_order(mine, other)
    around = weights_around(
        place, norm_params, attn_in, attn_out, mlp_in, mlp_out, [other]
    )
    grad_mine, grad_other = mine_and_other(cotangent)
    weights = [None, None]
    pairs = join(around[0], swaps(around[0], LAST, 1), [pa, po, p2, hidden])
    far = behind(swaps(pairs, LAST, -1), [])
    weights[0] = weights_of(pairs[:1] + behind(pairs[1:], far[:1]), far)
    records = []
    for layer in range(2):
        a_weights = weights[layer][0]
        a1p_keep, a1p_send, gains, *pieces = run_kernel(
            qkv_kernel,
            [place, hidden, pa] + a_weights,
            [shaped(TOKENS, 384), shaped(TOKENS, 384), shaped(8, D, dtype=F32)]
            + [shaped(576, TOKENS)] * 4,
            (
                pltpu.VMEM((D, 3 * D), BF),
                pltpu.VMEM((D, 128), BF),
                pltpu.VMEM((3 * D, TOKENS), BF),
                pltpu.SemaphoreType.DMA((16,)),
            ),
            flops=4 * UNIT,
            any_count=4,
            done=[weights[layer][n][1] for n in (1, 2)],
        )
        cores = [v for part in weights[layer][1:] for v in part[2:]]
        pieces = behind(pieces, [cores[0], cores[2]])
        turned = exchange_four(pieces)
        if layer == 0:
            held = list(after(around[1], turned[1:]))
            first = swaps(held, LAST, 1)
        else:
            (grad_other,) = after([grad_other], turned[1:])
            grad_other = fetch(grad_other, "y", 2)
        *mixed, sums = run_kernel(
            attend_kernel,
            [place] + turned,
            [shaped(GROUP, TOKENS)] * 4 + [shaped(3, 1024, dtype=F32)],
            (pltpu.VMEM((1024, TOKENS), F32),),
            flops=ATTEND,
            done=cores,
        )
        if layer == 0:
            mixed = list(after(mixed, first))
        back = exchange_four(mixed)
        if layer == 0:
            pairs = list(after(join(held, first), back[1:]))
            far = behind(swaps(pairs, LAST, -1), [])
        h1, following, slope, forward_send, op_keep, act_keep = run_kernel(
            mlp_kernel,
            [place, hidden] + back + [a1p_send, po, p2, gains] + sum(weights[layer], []),
            [
                shaped(TOKENS, D, dtype=F32),
                shaped(TOKENS, D, dtype=F32),
                shaped(TOKENS, FF),
                shaped(TOKENS, FF),
                shaped(TOKENS, 384),
                shaped(TOKENS, 1536),
            ],
            MLP_SCRATCH,
            flops=11 * UNIT,
            any_count=12,
        )
        records.append(
            (hidden, a1p_keep, gains, turned, mixed, sums, h1, slope, forward_send, op_keep, act_keep)
        )
        if layer == 0:
            far = behind(far, [following])
            weights[1] = weights_of(pairs[:2] + behind(pairs[2:], [following]), far)
        hidden = following

    def leave(values, ahead=()):
        values = jnp.dot(
            values, p2.astype(F32).T, precision=lax.Precision.HIGHEST, preferred_element_type=F32
        )
        far = values[128:]
        if ahead:
            (far,) = after([far], list(ahead))
        else:
            far = far.astype(BF)
        return values[:128], fetch(far, "y", 2)

    def arrange(own, came):
        return jnp.stack(
            [jnp.where(high == 0, own, came), jnp.where(high == 0, came, own)]
        )[:, None]

    def back_to_qkv(layer, grad, done):
        hidden, a1p_keep, gains, turned, mixed, sums, h1, slope = records[layer][:8]
        return run_kernel(
            mlp_back_kernel,
            [place, grad, slope, h1, gains, p2, po] + sum(weights[layer], []),
            [
                shaped(TOKENS, D, dtype=F32),
                shaped(TOKENS, FF),
                shaped(TOKENS, 1536),
                shaped(8, D, dtype=F32),
            ]
            + [shaped(GROUP, TOKENS)] * 4,
            MLP_SCRATCH,
            flops=11 * UNIT,
            any_count=12,
            done=done,
        )

    def mlp_gradients(forward, back, act_keep, dpre_keep):
        return run_kernel(
            mlp_grad_kernel,
            [
                place,
                (forward[0], 768, 1),
                (forward[1], 768, 1),
                act_keep,
                (forward[1], 1536, 1),
                dpre_keep,
                (back[1], 1536, 0),
                (back[0], 768, 2),
                (back[1], 768, 2),
            ],
            [shaped(2, 192, 1536)] * 2 + [shaped(2, 768, 384)] * 2,
            flops=8 * UNIT,
        )

    def attend_back(layer, grad_mixed, done):
        turned, mixed, sums = records[layer][3:6]
        return run_kernel(
            attend_back_kernel,
            [place] + turned + grad_mixed + mixed + [sums],
            [shaped(576, TOKENS)] * 4,
            (pltpu.VMEM((1024, TOKENS), F32),),
            flops=3 * ATTEND,
            done=done,
        )

    def qkv_back(layer, grad_pieces, g1, norm2, done):
        hidden, gains = records[layer][0], records[layer][2]
        return run_kernel(
            qkv_back_kernel,
            [place] + grad_pieces + [hidden, g1, gains, pa, norm2] + weights[layer][0],
            [shaped(TOKENS, D, dtype=F32), shaped(3 * D, TOKENS), shaped(8, D, dtype=F32)],
            (pltpu.VMEM((D, 3 * D), BF), pltpu.SemaphoreType.DMA((8,))),
            flops=5 * UNIT,
            any_count=4,
            done=done,
        )

    def attn_gradients(forward, back, a1p_keep, op_keep, dqkv, norms, done=()):
        return run_kernel(
            attn_grad_kernel,
            [
                place,
                a1p_keep,
                (forward[1], 384, 0),
                op_keep,
                (forward[1], 384, 1),
                (back[0], 768, 3),
                (back[1], 768, 3),
                dqkv[0],
                dqkv[1],
                norms[0],
                norms[1],
                pa,
            ],
            [shaped(2, 96, ROW_A)] * 2,
            flops=4 * UNIT,
            done=done,
        )

    grad = in_own_order(grad_mine, grad_other)

    forward_send, op_keep, act_keep = records[1][8:]
    a1p_keep = records[1][1]
    forward = forward_send, with_core(forward_send)
    g1, back_send, dpre_keep, norm2, *pieces = back_to_qkv(1, grad, [])
    grad_mixed = exchange_four(pieces)
    back = back_send, with_core(back_send)
    b1_mine, b1_send, c1_mine, c1_send = mlp_gradients(forward, back, act_keep, dpre_keep)
    b1_send, c1_send = after([b1_send, c1_send], grad_mixed[1:])
    b1_came, c1_came = swap(b1_send, "x", -1), swap(c1_send, "z", -1)
    outputs = leave(hidden, grad_mixed[1:])
    pieces = attend_back(1, grad_mixed, [b1_mine])
    pieces = after(pieces, [outputs[1], b1_came, c1_came])
    grad_pieces = exchange_four(pieces)
    (b1_keep, c1_keep), (b1_send, c1_send) = halved([b1_mine, c1_mine], [b1_came, c1_came])
    b1_send, c1_send = after([b1_send, c1_send], grad_pieces[1:])
    b1_came, c1_came = swap(b1_send, "x", 1), swap(c1_send, "z", 1)
    grad, dqkv, norms = qkv_back(1, grad_pieces, g1, norm2, [b1_keep])
    dqkv, norms = (dqkv, with_core(dqkv)), (norms, with_core(norms))

    forward_send0, op_keep0, act_keep0 = records[0][8:]
    a1p_keep0 = records[0][1]
    forward0 = forward_send0, with_core(forward_send0)
    g1, back_send0, dpre_keep0, norm2, *pieces = back_to_qkv(0, grad, [b1_came, c1_came])
    pieces = after(pieces, [dqkv[1], norms[1]])
    grad_mixed = exchange_four(pieces)
    back0 = back_send0, with_core(back_send0)
    b0_mine, b0_send, c0_mine, c0_send = mlp_gradients(forward0, back0, act_keep0, dpre_keep0)
    b0_send, c0_send = after([b0_send, c0_send], grad_mixed[1:])
    b0_came, c0_came = swap(b0_send, "x", -1), swap(c0_send, "z", -1)
    pieces = attend_back(0, grad_mixed, [b0_mine])
    pieces = after(pieces, [b0_came, c0_came])
    (op_keep,) = after([op_keep], pieces[:1])
    grad_pieces = exchange_four(pieces)
    a1_mine, a1_send = attn_gradients(forward, back, a1p_keep, op_keep, dqkv, norms)
    (a1_send,) = after([a1_send], grad_pieces[1:])
    a1_came = swap(a1_send, "y", -1)
    grad, dqkv, norms = qkv_back(0, grad_pieces, g1, norm2, [a1_mine])
    dqkv, norms = (dqkv, with_core(dqkv)), (norms, with_core(norms))
    (b0_keep, c0_keep, a1_keep), (b0_send, c0_send, a1_send) = halved(
        [b0_mine, c0_mine, a1_mine], [b0_came, c0_came, a1_came], [grad]
    )
    b0_came, c0_came = swap(b0_send, "x", 1), swap(c0_send, "z", 1)
    a1_came = swap(a1_send, "y", 1)
    grad_own, grad_far = leave(grad)
    a0_mine, a0_send = attn_gradients(
        forward0, back0, a1p_keep0, op_keep0, dqkv, norms, [b0_keep]
    )
    (a0_send,) = after([a0_send], [b0_came, c0_came, a1_came, grad_far])
    a0_came = swap(a0_send, "y", -1)
    (a0_keep,), (a0_send,) = halved([a0_mine], [a0_came])
    a0_came = swap(a0_send, "y", 1)
    weight_grads = gradients_home(
        place,
        [total(a0_keep, a0_came), total(a1_keep, a1_came)],
        [[b0_keep, b0_came], [b1_keep, b1_came]],
        [[c0_keep, c0_came], [c1_keep, c1_came]],
        [a0_keep],
    )
    grad_inputs = grad_own, grad_far.astype(F32)
    return (arrange(*outputs), arrange(*grad_inputs)) + weight_grads


def solution(mesh):
    in_specs = (
        P(None, "wide", "narrow", None),
        P(None, "wide"),
        P(None, None, ("wide", "narrow")),
        P(None, ("wide", "narrow"), None),
        P(None, ("wide", "narrow"), None),
        P(None, "narrow", "wide"),
        P(None, "wide", "narrow"),
        P(None, "wide", "narrow", None),
    )
    out_specs = (
        P(None, "wide", "narrow", None),
        P(None, "wide", "narrow", None),
        P(None, None, ("wide", "narrow")),
        P(None, ("wide", "narrow"), None),
        P(None, ("wide", "narrow"), None),
        P(None, "narrow", "wide"),
        P(None, "wide", "narrow"),
    )
    return jax.shard_map(body, mesh=mesh, in_specs=in_specs, out_specs=out_specs, check_vma=False)
```

time: 630 us -> 529 us (0.84)
  waiting for transfers between devices: 257 us -> 156 us
  Pallas kernels: 142 us -> 202 us
  other arithmetic: 39.5 us -> 6.46 us
  starting transfers between devices: 109 us -> 95.6 us
  local copies, waits for them, and re-layouts: 64.4 us -> 51.9 us
    ppermute x99 -> x51, waiting for transfers between devices: 257 us -> 71.4 us  [fetch(): return lax.ppermute(value, AXES, pairs)]
    ppermute x0 -> x46, waiting for transfers between devices: none -> 84.5 us  [swap(): return lax.ppermute(value, AXES, pairs)]
    ppermute x99 -> x51, starting transfers between devices: 109 us -> 39.2 us  [fetch(): return lax.ppermute(value, AXES, pairs)]
    pallas_call x16 -> x55, Pallas kernels: 142 us -> 202 us  [the longest x34 202 us: run_kernel(): pl.pallas_call(whole, grid=(1,), out_shape=tuple(outs), in_specs=specs +...]
    ppermute x0 -> x46, starting transfers between devices: none -> 56.4 us  [swap(): return lax.ppermute(value, AXES, pairs)]
    unnamed x138 -> x218, local copies, waits for them, and re-layouts: 14.8 us -> 38 us
    convert_element_type x12 -> x2, other arithmetic: 15.9 us -> 0.29 us  [total(): return (keep.astype(F32) + came.astype(F32)).astype(BF)]
    another operation x21 -> x3, other arithmetic: 13 us -> 0.56 us  [the longest x1 0.45 us: gradients_home(): a = jnp.stack(parts, 2).reshape(4, 4, 300, 128)]
  transfers between devices with their start and end apart: 99 -> 97, of which waited for: 39 -> 47; matrix products, arithmetic and copies ran while one was open for 15% -> 5% of each run, Pallas kernels for 13% -> 33%
where the time goes in v2:
time: 529 us; the launch traced here: 520 us
  Pallas kernels  202 us (38%)
  waiting for transfers between devices  156 us (29%)
  starting transfers between devices  95.6 us (18%)
  local copies, waits for them, and re-layouts  51.9 us (10%)
  other arithmetic  6.46 us (1%)
  matrix products  5.83 us (1%)
    pallas_call x34, Pallas kernels, run_kernel(): pl.pallas_call(whole, grid=(1,), out_shape=tuple(outs), in_specs=specs +...  202 us
    ppermute x46, waiting for transfers between devices, swap(): return lax.ppermute(value, AXES, pairs)  84.5 us
    ppermute x51, waiting for transfers between devices, fetch(): return lax.ppermute(value, AXES, pairs)  71.4 us
    ppermute x46, starting transfers between devices, swap(): return lax.ppermute(value, AXES, pairs)  56.4 us
    ppermute x51, starting transfers between devices, fetch(): return lax.ppermute(value, AXES, pairs)  39.2 us
    unnamed x218, local copies, waits for them, and re-layouts  38 us
  transfers between devices with their start and end apart: 97, of which 47 were waited for; matrix products, arithmetic and copies ran while one was open for 5% of the time, Pallas kernels for 33%

profile of v2, /device:TPU:0, one launch (start us, length us, event | category | flops | bytes accessed | tf_op | source)
XLA Modules:
  0.0 520.3 jit_solution(1606261685066254013)
XLA Ops:
  33.6 5.2 %collective-permute-done.8.refs_4_ = bf16[4,96,384]{2,1,0:T(8,128)(2,1)S(1)} collective-permute-done((bf16[4,96,384]{2,1,0:T(8,128)(2,1)}, bf16[4,96,384]{2,1,0:T(8,128)(2,1)S(1)}, u32[]{:S(2)}, u32[]{:S(2)}) %collective-permute-start.8) | collective-permute-done | bytes 294944 | tf_op jit(solution)/shard_map/ppermute | solution.py:53
  51.0 5.5 %collective-permute-done.refs_7_ = bf16[128,768]{1,0:T(8,128)(2,1)S(1)} collective-permute-done((bf16[128,768]{1,0:T(8,128)(2,1)S(1)}, bf16[128,768]{1,0:T(8,128)(2,1)S(1)}, u32[]{:S(2)}, u32[]{:S(2)}) %collective-permute-start) | collective-permute-done | bytes 196640 | tf_op jit(solution)/shard_map/ppermute | solution.py:43
  95.0 14.4 %collective-permute-done.17.refs_1_ = bf16[2,192,1536]{2,1,0:T(8,128)(2,1)S(1)} collective-permute-done((bf16[2,192,1536]{2,1,0:T(8,128)(2,1)}, bf16[2,192,1536]{2,1,0:T(8,128)(2,1)S(1)}, u32[]{:S(2)}, u32[]{:S(2)}) %collective-permute-start.17) | collective-permute-done | bytes 1179680 | tf_op jit(solution)/shard_map/ppermute | solution.py:53
  118.4 6.1 %shard_map.151 = (bf16[256,384]{1,0:T(8,128)(2,1)}, bf16[256,384]{1,0:T(8,128)(2,1)}, f32[8,768]{1,0:T(8,128)}, bf16[576,256]{1,0:T(8,128)(2,1)}, bf16[576,256]{...) custom-call(s32[7]{0:T(128)} %stack.55.refs_0_, f32[256,768]{1,0:T(8,128)} %fusion.4.refs_9_.refs_1_.refs_5_, ...), custom_call_target="tpu_custom_call" | custom-call | flops 1207959552 | bytes 8478720 | tf_op jit(solution)/shard_map/pallas_call | solution.py:602
  131.8 8.3 %collective-permute-done.23.refs_2_.refs_3_ = bf16[576,256]{1,0:T(8,128)(2,1)S(1)} collective-permute-done((bf16[576,256]{1,0:T(8,128)(2,1)}, bf16[576,256]{1,0:T(8,128)(2,1)S(1)}, u32[]{:S(2)}, u32[]{:S(2)}) %collective-permute-start.23) | collective-permute-done | bytes 294944 | tf_op jit(solution)/shard_map/ppermute | solution.py:43
  145.2 9.9 %shard_map.154 = (bf16[192,256]{1,0:T(8,128)(2,1)}, bf16[192,256]{1,0:T(8,128)(2,1)}, bf16[192,256]{1,0:T(8,128)(2,1)}, bf16[192,256]{1,0:T(8,128)(2,1)}, f32[3,1024]{1,0:T(4,128)}) custom-call(s32[7]{0:T(128)} %stack.55.refs_0_, bf16[576,256]{1,0:T(8,128)(2,1)} %get-tuple-element.216.refs_1_, bf16[576,256]{1,0:T(8,128)(2,1)} %copy-done.76, ...), custom_call_target="tpu_custom_call" | custom-call | flops 1610612736 | bytes 1585152 | tf_op jit(solution)/shard_map/pallas_call | solution.py:602
  174.7 10.4 %shard_map.158 = (f32[256,768]{1,0:T(8,128)}, f32[256,768]{1,0:T(8,128)}, bf16[256,3072]{1,0:T(8,128)(2,1)}, bf16[256,3072]{1,0:T(8,128)(2,1)}, bf16[256,384]{1,0:T(8,128)(2,1)}, /*index=5*/bf16[256,1536]{1,0:T(8,128)(2,1)}) custom-call(s32[7]{0:T(128)} %stack.55.refs_0_, f32[256,768]{1,0:T(8,128)} %fusion.4.refs_9_.refs_1_.refs_5_, ...), custom_call_target="tpu_custom_call" | custom-call | flops 3321888768 | bytes 23814144 | tf_op jit(solution)/shard_map/pallas_call | solution.py:602
  198.3 6.1 %shard_map.163 = (bf16[256,384]{1,0:T(8,128)(2,1)}, bf16[256,384]{1,0:T(8,128)(2,1)}, f32[8,768]{1,0:T(8,128)}, bf16[576,256]{1,0:T(8,128)(2,1)}, bf16[576,256]{...) custom-call(s32[7]{0:T(128)} %stack.55.refs_0_, ...), custom_call_target="tpu_custom_call" | custom-call | flops 1207959552 | bytes 8478720 | tf_op jit(solution)/shard_map/pallas_call | solution.py:602
  207.0 7.6 %collective-permute-done.41.refs_2_.refs_1_ = bf16[576,256]{1,0:T(8,128)(2,1)S(1)} collective-permute-done((bf16[576,256]{1,0:T(8,128)(2,1)}, bf16[576,256]{1,0:T(8,128)(2,1)S(1)}, u32[]{:S(2)}, u32[]{:S(2)}) %collective-permute-start.41) | collective-permute-done | bytes 294944 | tf_op jit(solution)/shard_map/ppermute | solution.py:43
  223.1 10.0 %shard_map.166 = (bf16[192,256]{1,0:T(8,128)(2,1)}, bf16[192,256]{1,0:T(8,128)(2,1)}, bf16[192,256]{1,0:T(8,128)(2,1)}, bf16[192,256]{1,0:T(8,128)(2,1)}, f32[3,1024]{1,0:T(4,128)}) custom-call(s32[7]{0:T(128)} %stack.55.refs_0_, bf16[576,256]{1,0:T(8,128)(2,1)} %get-tuple-element.252.refs_1_, bf16[576,256]{1,0:T(8,128)(2,1)} %copy-done.69, ...), custom_call_target="tpu_custom_call" | custom-call | flops 1610612736 | bytes 1585152 | tf_op jit(solution)/shard_map/pallas_call | solution.py:602
  242.3 10.3 %shard_map.167 = (f32[256,768]{1,0:T(8,128)}, f32[256,768]{1,0:T(8,128)}, bf16[256,3072]{1,0:T(8,128)(2,1)}, bf16[256,3072]{1,0:T(8,128)(2,1)}, bf16[256,384]{1,0:T(8,128)(2,1)}, /*index=5*/bf16[256,1536]{1,0:T(8,128)(2,1)}) custom-call(s32[7]{0:T(128)} %stack.55.refs_0_, f32[256,768]{1,0:T(8,128)} %get-tuple-element.235.refs_3_.refs_1_.refs_5_, ...), custom_call_target="tpu_custom_call" | custom-call | flops 3321888768 | bytes 23814144 | tf_op jit(solution)/shard_map/pallas_call | solution.py:602
  254.3 12.8 %shard_map.169 = (f32[256,768]{1,0:T(8,128)}, bf16[256,3072]{1,0:T(8,128)(2,1)}, bf16[256,1536]{1,0:T(8,128)(2,1)}, f32[8,768]{1,0:T(8,128)}, bf16[192,256]{1,0:...) custom-call(s32[7]{0:T(128)} %stack.55.refs_0_, ...), custom_call_target="tpu_custom_call" | custom-call | flops 3321888768 | bytes 23445504 | tf_op jit(solution)/shard_map/pallas_call | solution.py:602
  272.1 8.8 %shard_map.171 = (bf16[2,192,1536]{2,1,0:T(8,128)(2,1)}, bf16[2,192,1536]{2,1,0:T(8,128)(2,1)}, bf16[2,768,384]{2,1,0:T(8,128)(2,1)}, bf16[2,768,384]{2,1,0:T(8,128)(2,1)}) custom-call(s32[7]{0:T(128)} %stack.55.refs_0_, bf16[256,3072]{1,0:T(8,128)(2,1)} %get-tuple-element.270.refs_1_, bf16[256,3072]{1,0:T(8,128)(2,1)} %copy-done.6, ...), custom_call_target="tpu_custom_call" | custom-call | flops 2415919104 | bytes 9437184 | tf_op jit(solution)/shard_map/pallas_call | solution.py:602
  289.4 10.4 %shard_map.172 = (bf16[576,256]{1,0:T(8,128)(2,1)}, bf16[576,256]{1,0:T(8,128)(2,1)}, bf16[576,256]{1,0:T(8,128)(2,1)}, bf16[576,256]{1,0:T(8,128)(2,1)}) custom-call(s32[7]{0:T(128)} %stack.55.refs_0_, bf16[576,256]{1,0:T(8,128)(2,1)} %get-tuple-element.252.refs_1_, bf16[576,256]{1,0:T(8,128)(2,1)} %copy-done.69, bf16[576,256]{1,0:T(8,128)(2,1)} %copy-done.70, ...), custom_call_target="tpu_custom_call" | custom-call | flops 4831838208 | bytes 3158016 | tf_op jit(solution)/shard_map/pallas_call | solution.py:602
  321.4 8.1 %shard_map.176 = (f32[256,768]{1,0:T(8,128)}, bf16[2304,256]{1,0:T(8,128)(2,1)}, f32[8,768]{1,0:T(8,128)}) custom-call(s32[7]{0:T(128)} %stack.55.refs_0_, bf16[576,256]{1,0:T(8,128)(2,1)} %get-tuple-element.283.refs_1_, bf16[576,256]{1,0:T(8,128)(2,1)} %copy-done.39, bf16[576,256]{1,0:T(8,128)(2,1)} %copy-done.40, bf16[576,256]{1,0:T(8,128)(2,1)} %copy-done.41, ...), custom_call_target="tpu_custom_call" | custom-call | flops 1509949440 | bytes 10887168 | tf_op jit(solution)/shard_map/pallas_call | solution.py:602
  330.5 13.0 %shard_map.178 = (f32[256,768]{1,0:T(8,128)}, bf16[256,3072]{1,0:T(8,128)(2,1)}, bf16[256,1536]{1,0:T(8,128)(2,1)}, f32[8,768]{1,0:T(8,128)}, bf16[192,256]{1,0:...) custom-call(s32[7]{0:T(128)} %stack.55.refs_0_, ...), custom_call_target="tpu_custom_call" | custom-call | flops 3321888768 | bytes 23445504 | tf_op jit(solution)/shard_map/pallas_call | solution.py:602
  354.9 8.8 %shard_map.180 = (bf16[2,192,1536]{2,1,0:T(8,128)(2,1)}, bf16[2,192,1536]{2,1,0:T(8,128)(2,1)}, bf16[2,768,384]{2,1,0:T(8,128)(2,1)}, bf16[2,768,384]{2,1,0:T(8,128)(2,1)}) custom-call(s32[7]{0:T(128)} %stack.55.refs_0_, bf16[256,3072]{1,0:T(8,128)(2,1)} %get-tuple-element.309.refs_1_, bf16[256,3072]{1,0:T(8,128)(2,1)} %copy-done.7, ...), custom_call_target="tpu_custom_call" | custom-call | flops 2415919104 | bytes 9437184 | tf_op jit(solution)/shard_map/pallas_call | solution.py:602
  367.7 10.3 %shard_map.181 = (bf16[576,256]{1,0:T(8,128)(2,1)}, bf16[576,256]{1,0:T(8,128)(2,1)}, bf16[576,256]{1,0:T(8,128)(2,1)}, bf16[576,256]{1,0:T(8,128)(2,1)}) custom-call(s32[7]{0:T(128)} %stack.55.refs_0_, bf16[576,256]{1,0:T(8,128)(2,1)} %get-tuple-element.216.refs_1_, bf16[576,256]{1,0:T(8,128)(2,1)} %copy-done.76, bf16[576,256]{1,0:T(8,128)(2,1)} %copy-done.77, ...), custom_call_target="tpu_custom_call" | custom-call | flops 4831838208 | bytes 3158016 | tf_op jit(solution)/shard_map/pallas_call | solution.py:602
  388.3 6.8 %shard_map.185 = (bf16[2,96,3200]{2,1,0:T(8,128)(2,1)}, bf16[2,96,3200]{2,1,0:T(8,128)(2,1)}) custom-call(s32[7]{0:T(128)} %stack.55.refs_0_, bf16[256,384]{1,0:T(8,128)(2,1)} %get-tuple-element.328.refs_1_, bf16[256,3072]{1,0:T(8,128)(2,1)} %copy-done.6, bf16[256,384]{1,0:T(8,128)(2,1)} %shard_map.184.refs_3_, bf16[256,3072]{1,0:T(8,128)(2,1)} %copy-done.6, ...), custom_call_target="tpu_custom_call" | custom-call | flops 1207959552 | bytes 7618560 | tf_op jit(solution)/shard_map/pallas_call | solution.py:602
  403.0 8.1 %shard_map.186 = (f32[256,768]{1,0:T(8,128)}, bf16[2304,256]{1,0:T(8,128)(2,1)}, f32[8,768]{1,0:T(8,128)}) custom-call(s32[7]{0:T(128)} %stack.55.refs_0_, bf16[576,256]{1,0:T(8,128)(2,1)} %get-tuple-element.322.refs_1_, bf16[576,256]{1,0:T(8,128)(2,1)} %copy-done.36, bf16[576,256]{1,0:T(8,128)(2,1)} %copy-done.37, bf16[576,256]{1,0:T(8,128)(2,1)} %copy-done.38, ...), custom_call_target="tpu_custom_call" | custom-call | flops 1509949440 | bytes 10887168 | tf_op jit(solution)/shard_map/pallas_call | solution.py:602
  411.1 8.6 %collective-permute-done.78.refs_5_ = bf16[2,96,3200]{2,1,0:T(8,128)(2,1)S(1)} collective-permute-done((bf16[2,96,3200]{2,1,0:T(8,128)(2,1)}, bf16[2,96,3200]{2,1,0:T(8,128)(2,1)S(1)}, u32[]{:S(2)}, u32[]{:S(2)}) %collective-permute-start.78) | collective-permute-done | bytes 1228832 | tf_op jit(solution)/shard_map/ppermute | solution.py:53
  432.7 6.6 %shard_map.189 = (bf16[2,96,3200]{2,1,0:T(8,128)(2,1)}, bf16[2,96,3200]{2,1,0:T(8,128)(2,1)}) custom-call(s32[7]{0:T(128)} %stack.55.refs_0_, bf16[256,384]{1,0:T(8,128)(2,1)} %get-tuple-element.332.refs_1_, bf16[256,3072]{1,0:T(8,128)(2,1)} %copy-done.7, bf16[256,384]{1,0:T(8,128)(2,1)} %get-tuple-element.333.refs_3_, bf16[256,3072]{1,0:T(8,128)(2,1)} %copy-done.7, ...), custom_call_target="tpu_custom_call" | custom-call | flops 1207959552 | bytes 7618560 | tf_op jit(solution)/shard_map/pallas_call | solution.py:602
  444.4 5.3 %shard_map.193 = (bf16[2,4,96,384]{3,2,1,0:T(8,128)(2,1)}, bf16[2,4,96,384]{3,2,1,0:T(8,128)(2,1)}, bf16[2,4,96,384]{3,2,1,0:T(8,128)(2,1)}, bf16[2,4,96,384]{3,2,1,0:T(8,128)(2,1)}) custom-call(s32[7]{0:T(128)} %stack.55.refs_0_, bf16[192,1536]{1,0:T(8,128)(2,1)} %get-tuple-element.338.refs_12_.refs_1_, bf16[192,1536]{1,0:T(8,128)(2,1)} %copy-done.26, ...), custom_call_target="tpu_custom_call" | custom-call | bytes 7077888 | tf_op jit(solution)/shard_map/pallas_call | solution.py:602
  450.4 10.3 %collective-permute-done.82.refs_1_ = bf16[2,96,3200]{2,1,0:T(8,128)(2,1)S(1)} collective-permute-done((bf16[2,96,3200]{2,1,0:T(8,128)(2,1)}, bf16[2,96,3200]{2,1,0:T(8,128)(2,1)S(1)}, u32[]{:S(2)}, u32[]{:S(2)}) %collective-permute-start.82) | collective-permute-done | bytes 1228832 | tf_op jit(solution)/shard_map/ppermute | solution.py:53
  (494 shorter events, 306.4 us)
Async XLA Ops:
  44.0 18.7 %collective-permute-start.10 = (bf16[2,4,304,128]{3,2,1,0:T(8,128)(2,1)}, bf16[2,4,304,128]{3,2,1,0:T(8,128)(2,1)S(1)}, u32[]{:S(2)}, u32[]{:S(2)}) collective-permute-start(bf16[2,4,304,128]{3,2,1,0:T(8,128)(2,1)} %get-tuple-element.196.refs_1_), channel_id=1, source_target_pairs={{0,6},{2,4},{4,2},{6,0},{8,10},{10,8},{12,14},{14,12},{16,22},{18,... | collective-permute-start | bytes 1867784 | tf_op jit(solution)/shard_map/ppermute | solution.py:53
  90.6 20.8 %collective-permute-start.16 = (bf16[2,96,3200]{2,1,0:T(8,128)(2,1)}, bf16[2,96,3200]{2,1,0:T(8,128)(2,1)S(1)}, u32[]{:S(2)}, u32[]{:S(2)}) collective-permute-start(bf16[2,96,3200]{2,1,0:T(8,128)(2,1)} %get-tuple-element.204.refs_3_.refs_10_.refs_7_), channel_id=1, source_target_pairs={{0,17},{2,19},{4,21},{6,23},{8,24},{10,26},{12,28},{14,30},{16,1},... | collective-permute-start | bytes 3686408 | tf_op jit(solution)/shard_map/ppermute | solution.py:53
  91.7 17.6 %collective-permute-start.17 = (bf16[2,192,1536]{2,1,0:T(8,128)(2,1)}, bf16[2,192,1536]{2,1,0:T(8,128)(2,1)S(1)}, u32[]{:S(2)}, u32[]{:S(2)}) collective-permute-start(bf16[2,192,1536]{2,1,0:T(8,128)(2,1)} %get-tuple-element.205.refs_0_), channel_id=1, source_target_pairs={{0,6},{2,4},{4,2},{6,0},{8,10},{10,8},{12,14},{14,12},{16,22},{18,... | collective-permute-start | bytes 3538952 | tf_op jit(solution)/shard_map/ppermute | solution.py:53
  92.4 17.9 %collective-permute-start.18 = (bf16[2,768,384]{2,1,0:T(8,128)(2,1)}, bf16[2,768,384]{2,1,0:T(8,128)(2,1)S(1)}, u32[]{:S(2)}, u32[]{:S(2)}) collective-permute-start(bf16[2,768,384]{2,1,0:T(8,128)(2,1)} %get-tuple-element.206.refs_1_), channel_id=1, source_target_pairs={{0,96},{2,98},{4,100},{6,102},{8,40},{10,42},{12,44},{14,46},{16,1... | collective-permute-start | bytes 3538952 | tf_op jit(solution)/shard_map/ppermute | solution.py:53
  95.0 18.5 %collective-permute-start.19 = (bf16[2,96,3200]{2,1,0:T(8,128)(2,1)}, bf16[2,96,3200]{2,1,0:T(8,128)(2,1)S(1)}, u32[]{:S(2)}, u32[]{:S(2)}) collective-permute-start(bf16[2,96,3200]{2,1,0:T(8,128)(2,1)} %get-tuple-element.204.refs_3_.refs_10_.refs_7_), channel_id=1, source_target_pairs={{8,0},{10,2},{12,4},{14,6},{0,8},{2,10},{4,12},{6,14},{24,16},{26,... | collective-permute-start | bytes 3686408 | tf_op jit(solution)/shard_map/ppermute | solution.py:43
  113.0 32.2 %collective-permute-start.26 = (bf16[2,192,1536]{2,1,0:T(8,128)(2,1)}, bf16[2,192,1536]{2,1,0:T(8,128)(2,1)}, u32[]{:S(2)}, u32[]{:S(2)}) collective-permute-start(bf16[2,192,1536]{2,1,0:T(8,128)(2,1)} %get-tuple-element.208.refs_7_.refs_15_.refs_12_), channel_id=1, source_target_pairs={{8,0},{10,2},{12,4},{14,6},{0,8},{2,10},{4,12},{6,14},{24,16},{26,... | collective-permute-start | bytes 3538952 | tf_op jit(solution)/shard_map/ppermute | solution.py:43
  113.5 31.7 %collective-permute-start.27 = (bf16[2,768,384]{2,1,0:T(8,128)(2,1)}, bf16[2,768,384]{2,1,0:T(8,128)(2,1)}, u32[]{:S(2)}, u32[]{:S(2)}) collective-permute-start(bf16[2,768,384]{2,1,0:T(8,128)(2,1)} %get-tuple-element.209.refs_8_.refs_19_.refs_16_), channel_id=1, source_target_pairs={{8,0},{10,2},{12,4},{14,6},{0,8},{2,10},{4,12},{6,14},{24,16},{26,... | collective-permute-start | bytes 3538952 | tf_op jit(solution)/shard_map/ppermute | solution.py:43
  126.8 16.5 %collective-permute-start.25 = (bf16[576,256]{1,0:T(8,128)(2,1)}, bf16[576,256]{1,0:T(8,128)(2,1)S(1)}, u32[]{:S(2)}, u32[]{:S(2)}) collective-permute-start(bf16[576,256]{1,0:T(8,128)(2,1)} %get-tuple-element.219), channel_id=1, source_target_pairs={{6,0},{0,2},{2,4},{4,6},{14,8},{8,10},{10,12},{12,14},{22,16},{16,... | collective-permute-start | bytes 884744 | tf_op jit(solution)/shard_map/ppermute | solution.py:43
  167.4 23.8 %collective-permute-start.34 = (bf16[2,96,3200]{2,1,0:T(8,128)(2,1)}, bf16[2,96,3200]{2,1,0:T(8,128)(2,1)S(1)}, u32[]{:S(2)}, u32[]{:S(2)}) collective-permute-start(bf16[2,96,3200]{2,1,0:T(8,128)(2,1)} %get-tuple-element.239.refs_3_.refs_10_.refs_7_), channel_id=1, source_target_pairs={{0,17},{2,19},{4,21},{6,23},{8,24},{10,26},{12,28},{14,30},{16,1},... | collective-permute-start | bytes 3686408 | tf_op jit(solution)/shard_map/ppermute | solution.py:53
  171.5 17.6 %collective-permute-start.36 = (bf16[2,768,384]{2,1,0:T(8,128)(2,1)}, bf16[2,768,384]{2,1,0:T(8,128)(2,1)S(1)}, u32[]{:S(2)}, u32[]{:S(2)}) collective-permute-start(bf16[2,768,384]{2,1,0:T(8,128)(2,1)} %get-tuple-element.241.refs_0_), channel_id=1, source_target_pairs={{0,96},{2,98},{4,100},{6,102},{8,40},{10,42},{12,44},{14,46},{16,1... | collective-permute-start | bytes 3538952 | tf_op jit(solution)/shard_map/ppermute | solution.py:53
  173.6 17.7 %collective-permute-start.35 = (bf16[2,192,1536]{2,1,0:T(8,128)(2,1)}, bf16[2,192,1536]{2,1,0:T(8,128)(2,1)}, u32[]{:S(2)}, u32[]{:S(2)}) collective-permute-start(bf16[2,192,1536]{2,1,0:T(8,128)(2,1)} %get-tuple-element.240.refs_14_.refs_11_), channel_id=1, source_target_pairs={{0,6},{2,4},{4,2},{6,0},{8,10},{10,8},{12,14},{14,12},{16,22},{18,... | collective-permute-start | bytes 3538952 | tf_op jit(solution)/shard_map/ppermute | solution.py:53
  174.7 18.7 %collective-permute-start.37 = (bf16[2,96,3200]{2,1,0:T(8,128)(2,1)}, bf16[2,96,3200]{2,1,0:T(8,128)(2,1)}, u32[]{:S(2)}, u32[]{:S(2)}) collective-permute-start(bf16[2,96,3200]{2,1,0:T(8,128)(2,1)} %get-tuple-element.239.refs_3_.refs_10_.refs_7_), channel_id=1, source_target_pairs={{8,0},{10,2},{12,4},{14,6},{0,8},{2,10},{4,12},{6,14},{24,16},{26,... | collective-permute-start | bytes 3686408 | tf_op jit(solution)/shard_map/ppermute | solution.py:43
  205.6 16.8 %collective-permute-start.43 = (bf16[576,256]{1,0:T(8,128)(2,1)}, bf16[576,256]{1,0:T(8,128)(2,1)S(1)}, u32[]{:S(2)}, u32[]{:S(2)}) collective-permute-start(bf16[576,256]{1,0:T(8,128)(2,1)} %get-tuple-element.255), channel_id=1, source_target_pairs={{6,0},{0,2},{2,4},{4,6},{14,8},{8,10},{10,12},{12,14},{22,16},{16,... | collective-permute-start | bytes 884744 | tf_op jit(solution)/shard_map/ppermute | solution.py:43
  235.8 16.9 %collective-permute-start.49 = (bf16[128,768]{1,0:T(8,128)(2,1)}, bf16[128,768]{1,0:T(8,128)(2,1)S(1)}, u32[]{:S(2)}, u32[]{:S(2)}) collective-permute-start(bf16[128,768]{1,0:T(8,128)(2,1)} %shard_map.168), channel_id=1, source_target_pairs={{1,0},{3,2},{5,4},{7,6},{9,8},{11,10},{13,12},{15,14},{17,16},{19,... | collective-permute-start | bytes 589832 | tf_op jit(solution)/shard_map/ppermute | solution.py:43
  252.6 17.2 %collective-permute-start.54 = (bf16[256,3072]{1,0:T(8,128)(2,1)}, bf16[256,3072]{1,0:T(8,128)(2,1)S(1)}, u32[]{:S(2)}, u32[]{:S(2)}) collective-permute-start(bf16[256,3072]{1,0:T(8,128)(2,1)} %get-tuple-element.270.refs_1_), channel_id=1, source_target_pairs={{8,0},{10,2},{12,4},{14,6},{0,8},{2,10},{4,12},{6,14},{24,16},{26,... | collective-permute-start | bytes 4718600 | tf_op jit(solution)/shard_map/ppermute | solution.py:43
  281.6 18.3 %collective-permute-start.56 = (bf16[2,192,1536]{2,1,0:T(8,128)(2,1)}, bf16[2,192,1536]{2,1,0:T(8,128)(2,1)S(1)}, u32[]{:S(2)}, u32[]{:S(2)}) collective-permute-start(bf16[2,192,1536]{2,1,0:T(8,128)(2,1)} %get-tuple-element.281), channel_id=1, source_target_pairs={{0,6},{2,4},{4,2},{6,0},{8,10},{10,8},{12,14},{14,12},{16,22},{18,... | collective-permute-start | bytes 3538952 | tf_op jit(solution)/shard_map/ppermute | solution.py:53
  284.0 17.6 %collective-permute-start.57 = (bf16[2,768,384]{2,1,0:T(8,128)(2,1)}, bf16[2,768,384]{2,1,0:T(8,128)(2,1)S(1)}, u32[]{:S(2)}, u32[]{:S(2)}) collective-permute-start(bf16[2,768,384]{2,1,0:T(8,128)(2,1)} %get-tuple-element.282), channel_id=1, source_target_pairs={{0,96},{2,98},{4,100},{6,102},{8,40},{10,42},{12,44},{14,46},{16,1... | collective-permute-start | bytes 3538952 | tf_op jit(solution)/shard_map/ppermute | solution.py:53
  321.4 31.8 %collective-permute-start.68 = (bf16[256,3072]{1,0:T(8,128)(2,1)}, bf16[256,3072]{1,0:T(8,128)(2,1)S(1)}, u32[]{:S(2)}, u32[]{:S(2)}) collective-permute-start(bf16[256,3072]{1,0:T(8,128)(2,1)} %get-tuple-element.309.refs_1_), channel_id=1, source_target_pairs={{8,0},{10,2},{12,4},{14,6},{0,8},{2,10},{4,12},{6,14},{24,16},{26,... | collective-permute-start | bytes 4718600 | tf_op jit(solution)/shard_map/ppermute | solution.py:43
  364.4 17.6 %collective-permute-start.70 = (bf16[2,192,1536]{2,1,0:T(8,128)(2,1)}, bf16[2,192,1536]{2,1,0:T(8,128)(2,1)S(1)}, u32[]{:S(2)}, u32[]{:S(2)}) collective-permute-start(bf16[2,192,1536]{2,1,0:T(8,128)(2,1)} %get-tuple-element.320), channel_id=1, source_target_pairs={{0,6},{2,4},{4,2},{6,0},{8,10},{10,8},{12,14},{14,12},{16,22},{18,... | collective-permute-start | bytes 3538952 | tf_op jit(solution)/shard_map/ppermute | solution.py:53
  367.6 17.6 %collective-permute-start.71 = (bf16[2,768,384]{2,1,0:T(8,128)(2,1)}, bf16[2,768,384]{2,1,0:T(8,128)(2,1)S(1)}, u32[]{:S(2)}, u32[]{:S(2)}) collective-permute-start(bf16[2,768,384]{2,1,0:T(8,128)(2,1)} %get-tuple-element.321), channel_id=1, source_target_pairs={{0,96},{2,98},{4,100},{6,102},{8,40},{10,42},{12,44},{14,46},{16,1... | collective-permute-start | bytes 3538952 | tf_op jit(solution)/shard_map/ppermute | solution.py:53
  401.6 18.2 %collective-permute-start.78 = (bf16[2,96,3200]{2,1,0:T(8,128)(2,1)}, bf16[2,96,3200]{2,1,0:T(8,128)(2,1)S(1)}, u32[]{:S(2)}, u32[]{:S(2)}) collective-permute-start(bf16[2,96,3200]{2,1,0:T(8,128)(2,1)} %shard_map.187), channel_id=1, source_target_pairs={{0,17},{2,19},{4,21},{6,23},{8,24},{10,26},{12,28},{14,30},{16,1},... | collective-permute-start | bytes 3686408 | tf_op jit(solution)/shard_map/ppermute | solution.py:53
  411.0 20.6 %collective-permute-start.76 = (bf16[2304,256]{1,0:T(8,128)(2,1)}, bf16[2304,256]{1,0:T(8,128)(2,1)S(1)}, u32[]{:S(2)}, u32[]{:S(2)}) collective-permute-start(bf16[2304,256]{1,0:T(8,128)(2,1)} %get-tuple-element.334.refs_7_), channel_id=1, source_target_pairs={{8,0},{10,2},{12,4},{14,6},{0,8},{2,10},{4,12},{6,14},{24,16},{26,... | collective-permute-start | bytes 3538952 | tf_op jit(solution)/shard_map/ppermute | solution.py:43
  442.6 18.2 %collective-permute-start.82 = (bf16[2,96,3200]{2,1,0:T(8,128)(2,1)}, bf16[2,96,3200]{2,1,0:T(8,128)(2,1)S(1)}, u32[]{:S(2)}, u32[]{:S(2)}) collective-permute-start(bf16[2,96,3200]{2,1,0:T(8,128)(2,1)} %shard_map.190), channel_id=1, source_target_pairs={{0,17},{2,19},{4,21},{6,23},{8,24},{10,26},{12,28},{14,30},{16,1},... | collective-permute-start | bytes 3686408 | tf_op jit(solution)/shard_map/ppermute | solution.py:53
  449.7 15.7 %collective-permute-start.86 = (bf16[2,4,96,384]{3,2,1,0:T(8,128)(2,1)}, bf16[2,4,96,384]{3,2,1,0:T(8,128)(2,1)S(1)}, u32[]{:S(2)}, u32[]{:S(2)}) collective-permute-start(bf16[2,4,96,384]{3,2,1,0:T(8,128)(2,1)} %get-tuple-element.354), channel_id=1, source_target_pairs={{0,6},{2,4},{4,2},{6,0},{8,10},{10,8},{12,14},{14,12},{16,22},{18,... | collective-permute-start | bytes 1769480 | tf_op jit(solution)/shard_map/ppermute | solution.py:53
  (180 other events, 1065.4 us)

commit v3 on v2

--- a/solution.py
+++ b/solution.py
@@ -12,6 +12,8 @@
 HEAD_DIM = 64
 GROUP = 192
 TOKENS = 256
+SPAN = 1024
+SPAN_BACK = 512
 EPS = 1e-06
 ROOT_HALF = 0.7071067811865476
 INV_ROOT_TWO_PI = 0.3989422804014327
@@ -173,63 +175,83 @@
             ]
 
 
-def key_bias(place_ref, bias):
-    x, yh, length = place_ref[0], place_ref[1], place_ref[2]
+def mask_row(place_ref):
+    x, yh, length = place_ref[X], place_ref[HIGH], place_ref[LENGTH]
+    rows = []
     for k in range(4):
         for half in range(2):
             start = lax.rem(x + k, 4) * 256 + lax.rem(yh + half, 2) * 128
-            slot = start + lax.broadcasted_iota(jnp.int32, (128, TOKENS), 0)
-            bias[pl.ds(k * 256 + half * 128, 128), :] = jnp.where(slot < length, 0.0, -1e30)
+            slot = start + lax.broadcasted_iota(jnp.int32, (1, 128), 1)
+            rows.append(jnp.where(slot < length, 0.0, -1e30))
+    return jnp.concatenate(rows, 1)
 
 
 def side_by_side(refs, start):
     return jnp.concatenate([r[start : start + HEAD_DIM, :] for r in refs], 1)
 
 
-def attend_kernel(place_ref, t0, t1, t2, t3, u0, u1, u2, u3, sums_ref, bias):
+def with_rows(block, rows):
+    count, width = len(rows), block.shape[1]
+    tail = jnp.concatenate(rows + [jnp.zeros((16 - count, width), F32)], 0).astype(BF)
+    return jnp.concatenate([block, tail], 0)
+
+
+def in_three(row):
+    high = row.astype(BF).astype(F32)
+    middle = (row - high).astype(BF).astype(F32)
+    return [high, middle, row - high - middle]
+
+
+def attend_kernel(place_ref, t0, t1, t2, t3, u0, u1, u2, u3, sums_ref):
     t_refs, u_refs = (t0, t1, t2, t3), (u0, u1, u2, u3)
-    key_bias(place_ref, bias)
+    mask = mask_row(place_ref)
+    count = SPAN // TOKENS
+    ones = jnp.ones((1, SPAN), F32)
     for j in range(3):
-        keys = side_by_side(t_refs, GROUP + j * HEAD_DIM).T
+        keys = with_rows(side_by_side(t_refs, GROUP + j * HEAD_DIM), [mask]).T
         values_t = side_by_side(t_refs, 2 * GROUP + j * HEAD_DIM)
-        for b in range(4):
-            query_t = t_refs[b][j * HEAD_DIM : (j + 1) * HEAD_DIM, :]
-            scores = dot(keys, query_t) + bias[...]
+        rows = slice(j * HEAD_DIM, (j + 1) * HEAD_DIM)
+        for b in range(0, 4, count):
+            query_t = side_by_side(t_refs[b : b + count], j * HEAD_DIM)
+            scores = dot(keys, with_rows(query_t, [ones]))
             peak = jnp.max(scores, 0, keepdims=True)
             expont = jnp.exp(scores - peak)
             total = jnp.sum(expont, 0, keepdims=True)
-            mixed = dot(values_t, expont.astype(BF)) / total
-            u_refs[b][j * HEAD_DIM : (j + 1) * HEAD_DIM, :] = mixed.astype(BF)
-            sums_ref[j : j + 1, b * TOKENS : (b + 1) * TOKENS] = peak + jnp.log(total)
+            mixed = (dot(values_t, expont.astype(BF)) / total).astype(BF)
+            for n in range(count):
+                u_refs[b + n][rows, :] = mixed[:, n * TOKENS : (n + 1) * TOKENS]
+            sums_ref[j : j + 1, b * TOKENS : (b + count) * TOKENS] = peak + jnp.log(total)
 
 
 def attend_back_kernel(place_ref, *refs):
     t_refs, g_refs, u_refs = refs[0:4], refs[4:8], refs[8:12]
     sums_ref = refs[12]
     out_refs = refs[13:17]
-    bias = refs[17]
-    key_bias(place_ref, bias)
+    mask = mask_row(place_ref)
+    count = SPAN_BACK // TOKENS
+    ones = jnp.ones((1, SPAN_BACK), F32)
+    one_row = jnp.ones((1, 4 * TOKENS), F32)
     for j in range(3):
         keys_t = side_by_side(t_refs, GROUP + j * HEAD_DIM)
-        keys = keys_t.T
-        values = side_by_side(t_refs, 2 * GROUP + j * HEAD_DIM).T
+        keys = with_rows(keys_t, [mask] + [one_row] * 3).T
+        values = with_rows(side_by_side(t_refs, 2 * GROUP + j * HEAD_DIM), [one_row] * 3).T
         grad_keys = jnp.zeros((4 * TOKENS, HEAD_DIM), F32)
         grad_values = jnp.zeros((4 * TOKENS, HEAD_DIM), F32)
         rows = slice(j * HEAD_DIM, (j + 1) * HEAD_DIM)
-        for b in range(4):
-            query_t = t_refs[b][rows, :]
-            grad_t = g_refs[b][rows, :]
-            scores = dot(keys, query_t) + bias[...]
-            probs = jnp.exp(scores - sums_ref[j : j + 1, b * TOKENS : (b + 1) * TOKENS])
-            grad_probs = dot(values, grad_t)
-            delta = jnp.sum(
-                grad_t.astype(F32) * u_refs[b][rows, :].astype(F32), 0, keepdims=True
-            )
-            grad_scores = (probs * (grad_probs - delta)).astype(BF)
+        for b in range(0, 4, count):
+            query_t = side_by_side(t_refs[b : b + count], j * HEAD_DIM)
+            grad_t = side_by_side(g_refs[b : b + count], j * HEAD_DIM)
+            mixed_t = side_by_side(u_refs[b : b + count], j * HEAD_DIM)
+            sums = sums_ref[j : j + 1, b * TOKENS : (b + count) * TOKENS]
+            delta = jnp.sum(grad_t.astype(F32) * mixed_t.astype(F32), 0, keepdims=True)
+            probs = jnp.exp(dot(keys, with_rows(query_t, [ones] + in_three(-sums))))
+            grad_probs = dot(values, with_rows(grad_t, in_three(-delta)))
+            grad_scores = (probs * grad_probs).astype(BF)
             grad_values = grad_values + dot(probs.astype(BF), grad_t, 1, 1)
             grad_keys = grad_keys + dot(grad_scores, query_t, 1, 1)
-            grad_query = dot(keys_t, grad_scores) * HEAD_DIM ** (-0.5)
-            out_refs[b][rows, :] = grad_query.astype(BF)
+            grad_query = (dot(keys_t, grad_scores) * HEAD_DIM ** (-0.5)).astype(BF)
+            for n in range(count):
+                out_refs[b + n][rows, :] = grad_query[:, n * TOKENS : (n + 1) * TOKENS]
         grad_keys = grad_keys.astype(BF).T
         grad_values = grad_values.astype(BF).T
         for b in range(4):
@@ -250,37 +272,35 @@
     )
     first_copies = start_copies(
         [
-            (r.at[i], w1.at[core, at_rows(0, spot, 192)])
-            for r, i, core, spot in weight_blocks(refs[4:8], place_ref[NEAR_X])
+            (ref.at[k], w1.at[core, pl.ds(192 * k, 192)])
+            for core, ref in enumerate(refs[4:6])
+            for k in range(4)
         ],
         sems.at[pl.ds(8, 8)],
     )
     second_copies = start_copies(
         [
-            (r.at[i], w2.at[:, at_rows(core, spot, 384)])
-            for r, i, core, spot in weight_blocks(refs[8:12], place_ref[NEAR_Z])
+            (ref.at[k], w2.at[:, pl.ds((core * 4 + k) * 384, 384)])
+            for core, ref in enumerate(refs[6:8])
+            for k in range(4)
         ],
         sems.at[pl.ds(16, 8)],
     )
     return out_copies, first_copies, second_copies
 
 
-def mlp_kernel(place_ref, h_ref, u0, u1, u2, u3, a1p_send, po_ref, p2_ref, gains_ref, *refs):
-    h1_ref, next_ref, slope_ref, send_ref, op_keep, act_keep = refs[12:18]
-    turned, wout, w1, w2, sems = refs[18:]
-    out_copies, first_copies, second_copies = mlp_copies(
-        place_ref, refs[:12], wout, w1, w2, sems
-    )
+def mlp_forward(place_ref, h, pieces, a1p_send, po_ref, p2_ref, gains_ref, slope_ref, outs, parts):
+    send_ref, op_keep, act_keep = outs
+    turned, wout, w1, w2, out_copies, first_copies, second_copies = parts
     send_ref[:, 0:384] = a1p_send[...]
     x = place_ref[X]
-    for k, piece in enumerate((u0, u1, u2, u3)):
+    for k, piece in enumerate(pieces):
         turned[pl.ds(group_start(x, k), GROUP), :] = piece[...]
     op = dot(turned[...], po_ref[...], 0, 0).astype(BF)
     op_keep[...] = op[:, :384]
     send_ref[:, 384:768] = op[:, 384:]
     wait_copies(out_copies)
-    h1 = h_ref[...] + dot_two(dot(op, wout[...]), p2_ref[...])
-    h1_ref[...] = h1
+    h1 = h + dot_two(dot(op, wout[...]), p2_ref[...])
     z, _ = normed(h1)
     a2 = (z * gains_ref[2:3] + gains_ref[3:4]).astype(BF)
     send_ref[:, 768:1536] = a2
@@ -299,17 +319,12 @@
             send_ref[:, 1536:] = act
         slope_ref[:, columns] = slope.astype(BF)
         total = total + dot(act, w2[:, columns], 1, 1)
-    next_ref[...] = total
-
-
-def mlp_back_kernel(place_ref, g_ref, slope_ref, h1_ref, gains_ref, p2_ref, po_ref, *refs):
-    g1_ref, send_ref, dpre_keep, norm_ref = refs[12:16]
-    out_refs = refs[16:20]
-    turned, wout, w1, w2, sems = refs[20:]
-    out_copies, first_copies, second_copies = mlp_copies(
-        place_ref, refs[:12], wout, w1, w2, sems
-    )
-    grad = g_ref[...]
+    return h1, total
+
+
+def mlp_backward(place_ref, grad, h1, gains_ref, p2_ref, po_ref, slope_ref, outs, parts):
+    send_ref, dpre_keep, norm_ref, out_refs = outs
+    turned, wout, w1, w2, out_copies, first_copies, second_copies = parts
     grad_low = grad.astype(BF)
     send_ref[:, 1536:2304] = grad_low
     wait_copies(second_copies)
@@ -324,10 +339,9 @@
         else:
             send_ref[:, 0:1536] = dpre
         grad_a2 = grad_a2 + dot(dpre, w1[half], 1, 1)
-    dv, gain_grad, offset_grad = norm_back(grad_a2, h1_ref[...], gains_ref[2:3])
+    dv, gain_grad, offset_grad = norm_back(grad_a2, h1, gains_ref[2:3])
     norm_ref[...] = two_rows(gain_grad, offset_grad)
     g1 = grad + dv
-    g1_ref[...] = g1
     g1b = dot(g1.astype(BF), p2_ref[...], 1, 1).astype(BF)
     send_ref[:, 2304:] = g1b
     wait_copies(out_copies)
@@ -336,6 +350,53 @@
     x = place_ref[X]
     for k in range(4):
         out_refs[k][...] = turned[pl.ds(group_start(x, k), GROUP), :]
+    return g1
+
+
+def mlp_kernel(place_ref, h_ref, u0, u1, u2, u3, a1p_send, po_ref, p2_ref, gains_ref, *refs):
+    h1_ref, next_ref, slope_ref, send_ref, op_keep, act_keep = refs[8:14]
+    turned, wout, w1, w2, sems = refs[14:]
+    copies = mlp_copies(place_ref, refs[:8], wout, w1, w2, sems)
+    h1_ref[...], next_ref[...] = mlp_forward(
+        place_ref, h_ref[...], (u0, u1, u2, u3), a1p_send, po_ref, p2_ref, gains_ref, slope_ref,
+        (send_ref, op_keep, act_keep), (turned, wout, w1, w2) + copies,
+    )
+
+
+def mlp_turn_kernel(
+    place_ref, h_ref, u0, u1, u2, u3, a1p_send, po_ref, p2_ref, gains_ref, g_ref, *refs
+):
+    next_ref, forward_send, op_keep, act_keep, g1_ref, back_send, dpre_keep, norm_ref = refs[8:16]
+    out_refs = refs[16:20]
+    turned, wout, w1, w2, sems, slope_ref = refs[20:]
+    copies = mlp_copies(place_ref, refs[:8], wout, w1, w2, sems)
+    h1, next_ref[...] = mlp_forward(
+        place_ref, h_ref[...], (u0, u1, u2, u3), a1p_send, po_ref, p2_ref, gains_ref, slope_ref,
+        (forward_send, op_keep, act_keep), (turned, wout, w1, w2) + copies,
+    )
+    g1_ref[...] = mlp_backward(
+        place_ref, g_ref[...], h1, gains_ref, p2_ref, po_ref, slope_ref,
+        (back_send, dpre_keep, norm_ref, out_refs), (turned, wout, w1, w2, (), (), ()),
+    )
+
+
+def qkv_back_into_mlp_kernel(
+    place_ref, d0, d1, d2, d3, h_ref, g1_ref, gains_ref, pa_ref, norm2_ref,
+    slope_ref, h1_ref, gains0_ref, p2_ref, po_ref, *refs,
+):
+    dqkv_ref, next_ref, back_send, dpre_keep, below_ref = refs[12:17]
+    out_refs = refs[17:21]
+    turned, wout, w1, w2, sems, win, win_sems = refs[21:]
+    win_copies = win_start(place_ref, refs[:4], win, win_sems)
+    copies = mlp_copies(place_ref, refs[4:12], wout, w1, w2, sems)
+    grad = qkv_backward(
+        place_ref, (d0, d1, d2, d3), h_ref, g1_ref, gains_ref, pa_ref, norm2_ref,
+        dqkv_ref, win, win_copies,
+    )
+    next_ref[...] = mlp_backward(
+        place_ref, grad, h1_ref[...], gains0_ref, p2_ref, po_ref, slope_ref,
+        (back_send, dpre_keep, below_ref, out_refs), (turned, wout, w1, w2) + copies,
+    )
 
 
 def both_cores(first_ref, second_ref):
@@ -376,40 +437,57 @@
     store_blocks(place_ref[NEAR_Z], second_mine, second_send, slice(0, 384), blocks)
 
 
-def qkv_back_kernel(
-    place_ref, d0, d1, d2, d3, h_ref, g1_ref, gains_ref, pa_ref, norm2_ref, *refs
-):
-    blocks = weight_blocks(refs[:4], place_ref[NEAR_Y])
-    next_ref, dqkv_ref, norm_ref, win, sems = refs[4:]
-    win_copies = start_copies(
+def win_start(place_ref, refs, win, sems):
+    return start_copies(
         [
             (r.at[i, :, pl.ds(0, 3 * D)], win.at[at_rows(core, spot, 96)])
-            for r, i, core, spot in blocks
+            for r, i, core, spot in weight_blocks(refs, place_ref[NEAR_Y])
         ],
         sems,
     )
+
+
+def qkv_backward(
+    place_ref, pieces, h_ref, g1_ref, gains_ref, pa_ref, norm2_ref, dqkv_ref, win, copies
+):
     x = place_ref[X]
-    for k, piece in enumerate((d0, d1, d2, d3)):
+    for k, piece in enumerate(pieces):
         for c in range(3):
             dqkv_ref[pl.ds(group_start(x, k, c * D), GROUP), :] = piece[
                 c * GROUP : (c + 1) * GROUP, :
             ]
-    wait_copies(win_copies)
-    turned = dot(win[...], dqkv_ref[...])
+    wait_copies(copies)
+    turned = dot(win[...], dqkv_ref[0 : 3 * D, :])
     grad_a1 = dot_two(turned, pa_ref[...], 0, 1)
     dv, gain_grad, offset_grad = norm_back(grad_a1, h_ref[...], gains_ref[0:1])
-    norm_ref[...] = jnp.concatenate(
-        [gain_grad, offset_grad, norm2_ref[0:2], jnp.zeros((4, D), F32)], 0
-    )
-    next_ref[...] = g1_ref[...] + dv
+    norms = jnp.concatenate([gain_grad, offset_grad, norm2_ref[0:2], jnp.zeros((4, D), F32)], 0)
+    high = norms.astype(BF)
+    norms = jnp.concatenate([high, (norms - high.astype(F32)).astype(BF)], 0)
+    for c in range(3):
+        dqkv_ref[3 * D + 16 * c : 3 * D + 16 * c + 16, :] = norms[:, 256 * c : 256 * c + 256]
+    return g1_ref[...] + dv
+
+
+def qkv_back_kernel(
+    place_ref, d0, d1, d2, d3, h_ref, g1_ref, gains_ref, pa_ref, norm2_ref, *refs
+):
+    next_ref, dqkv_ref, win, sems = refs[4:]
+    copies = win_start(place_ref, refs[:4], win, sems)
+    next_ref[...] = qkv_backward(
+        place_ref, (d0, d1, d2, d3), h_ref, g1_ref, gains_ref, pa_ref, norm2_ref,
+        dqkv_ref, win, copies,
+    )
 
 
 def attn_grad_kernel(
-    place_ref, a1p_0, a1p_1, op_0, op_1, g1b_0, g1b_1, dqkv_0, dqkv_1, norm_0, norm_1, pa_ref,
-    mine, send,
+    place_ref, a1p_0, a1p_1, op_0, op_1, g1b_0, g1b_1, dqkv_0, dqkv_1, pa_ref, mine, send
 ):
     near = place_ref[NEAR_Y]
-    norms = norm_0[...] + norm_1[...]
+    norms = jnp.zeros((8, D), F32)
+    for ref in (dqkv_0, dqkv_1):
+        pair = [ref[3 * D + 16 * c : 3 * D + 16 * c + 16, :].astype(F32) for c in range(3)]
+        pair = jnp.concatenate(pair, 1)
+        norms = norms + pair[0:8] + pair[8:16]
     norms = dot_two(norms, pa_ref[:, 0:384])
     norms = jnp.concatenate([norms, jnp.zeros((120, 384), F32)], 0).T.astype(BF)
     a1p = both_cores(a1p_0, a1p_1)
@@ -452,19 +530,32 @@
     wait_copies(start_copies(pairs, refs[-1]))
 
 
-def layer_blocks_kernel(layer, place_ref, b_ref, c_ref, first_ref, second_ref):
+def layer_blocks_kernel(
+    layer, place_ref, b_pair, c_pair, b_far, c_far, first_ref, second_ref
+):
     middle = 1 + place_ref[LOW]
+    near_z = place_ref[NEAR_Z]
+    straight = place_ref[NEAR_Y] == middle
     part = slice(layer * 192, layer * 192 + 192)
+    b_slots = ((b_pair, 0, 0), (b_pair, 1, near_z), (b_far, 0, 3 - near_z), (b_far, 1, 3))
     for high in range(2):
         one, two = (0, middle) if high == 0 else (3, 3 - middle)
+        for ref, i, spot in b_slots:
+            both = [ref[i, one][:, part], ref[i, two][:, part]]
+            first_ref[
+                high * 96 : high * 96 + 96, pl.ds(pl.multiple_of(spot * 384, 384), 384)
+            ] = jnp.concatenate(both, 1)
         for k in range(4):
-            both = [b_ref[k, one][:, part], b_ref[k, two][:, part]]
-            first_ref[high * 96 : high * 96 + 96, k * 384 : k * 384 + 384] = jnp.concatenate(
-                both, 1
+            outer = c_pair[0, k] if high == 0 else c_far[1, k]
+            near, other = c_pair[1, k], c_far[0, k]
+            if high == 0:
+                inner = jnp.where(straight, near, other)
+            else:
+                inner = jnp.where(straight, other, near)
+            start = (2 * k + high) * 96
+            second_ref[start : start + 96, :] = jnp.concatenate(
+                [outer[:, part], inner[:, part]], 1
             )
-            both = [c_ref[one, k][:, part], c_ref[two, k][:, part]]
-            start = (2 * k + high) * 96
-            second_ref[start : start + 96, :] = jnp.concatenate(both, 1)
 
 
 def both_layers_kernel(place_ref, *refs):
@@ -536,21 +627,15 @@
         send[...] = total_of(mine[1], came[1])
 
 
+def total_pair_kernel(b_keep, b_came, c_keep, c_came, *out_refs):
+    for k, out in enumerate(out_refs):
+        out[0] = total_of(b_keep[k], b_came[k])
+        out[1] = total_of(c_keep[k], c_came[k])
+
+
 def total_kernel(keep, came, *out_refs):
     for k, out in enumerate(out_refs):
         out[...] = total_of(keep[k], came[k])
-
-
-def total_split_kernel(spots, place_ref, *refs):
-    count = len(spots)
-    for n, spot in enumerate(spots):
-        near = place_ref[spot]
-        keep, came = refs[n], refs[count + n]
-        mine, send = refs[2 * count + 2 * n], refs[2 * count + 2 * n + 1]
-        mine[0] = total_of(keep[0], came[0])
-        mine[1] = total_of(keep[near], came[near])
-        send[0] = total_of(keep[3 - near], came[3 - near])
-        send[1] = total_of(keep[3], came[3])
 
 
 def nothing_kernel(*refs):
@@ -609,7 +694,9 @@
         ),
         scratch_shapes=list(scratch),
         compiler_params=pltpu.CompilerParams(vmem_limit_bytes=VMEM_LIMIT),
-        cost_estimate=pl.CostEstimate(flops=flops, bytes_accessed=moved, transcendentals=0),
+        cost_estimate=pl.CostEstimate(
+            flops=flops, bytes_accessed=moved if flops else 0, transcendentals=0
+        ),
     )(*arrays, *done)
 
 
@@ -645,15 +732,13 @@
     )
 
 
-def gather_round(place, values, axes, done=()):
-    pairs = join(values, swaps(values, axes, 1))
-    far = swaps(pairs, axes, -1)
+def order(place, pairs, far, axes, done=()):
     return list(
         run_kernel(
             functools.partial(order_kernel, [NEAR[axis] for axis in axes]),
             [place] + pairs + far,
-            [like(v, 4) for v in values],
-            (pltpu.SemaphoreType.DMA((4 * len(values),)),),
+            [like(v[0], 4) for v in pairs],
+            (pltpu.SemaphoreType.DMA((4 * len(pairs),)),),
             lying=True,
             done=done,
         )
@@ -664,21 +749,29 @@
     return jnp.pad(value.reshape(300, 128), ((0, 4), (0, 0)))
 
 
-def weights_around(place, norm_params, attn_in, attn_out, mlp_in, mlp_out, done):
+def weights_around(place, norm_params, attn_in, attn_out, mlp_in, mlp_out, early):
     norm_part = jnp.pad(jnp.swapaxes(norm_params, 1, 2), ((0, 0), (0, 0), (0, 124)))
     a = padded(jnp.concatenate([attn_in, attn_out, norm_part], -1))
-    b = mlp_in.transpose(1, 0, 2).reshape(96, 384)
-    c = mlp_out.transpose(2, 0, 1).reshape(96, 384)
-    values = gather_round(place, [a, b, c], "zyx")
-    a, b, c = gather_round(place, values, "xzy", done)
+    bc = [mlp_in.transpose(1, 0, 2).reshape(96, 384), mlp_out.transpose(2, 0, 1).reshape(96, 384)]
+    for a_axis, bc_axes in (("z", "yx"), ("x", "zy")):
+        bc_near = swaps(bc, bc_axes, 1)
+        a_pair = join([a], [swap(a, a_axis, 1)], done=early + bc_near if early else bc)
+        early = []
+        bc_pair = join(bc, bc_near, done=a_pair)
+        a_far = swap(a_pair[0], a_axis, -1)
+        bc_far = swaps(bc_pair, bc_axes, -1)
+        (a,) = order(place, a_pair, [a_far], a_axis, done=bc_pair)
+        if a_axis == "z":
+            bc = order(place, bc_pair, bc_far, bc_axes, done=[a])
     a = a[:, :, :300].reshape(4, 4, 2, 6, ROW_A)
     layers = []
     for layer in range(2):
         al = a[:, :, layer].transpose(1, 0, 2, 3).reshape(96, ROW_A)
         bl, cl = run_kernel(
             functools.partial(layer_blocks_kernel, layer),
-            [place, b, c],
+            [place] + bc_pair + bc_far,
             [shaped(192, 1536), shaped(768, 384)],
+            done=[al],
         )
         layers.append([al, bl, cl])
     return layers
@@ -697,31 +790,11 @@
     return list(out[0::2]), list(out[1::2])
 
 
-def turn_rings(place, keep, came, later, done=()):
-    halves = [like(v[0], 2) for v in keep for _ in range(2)]
-    out = run_kernel(
-        functools.partial(total_split_kernel, [NEAR[axis] for axis in later]),
-        [place] + keep + came,
-        halves,
-        done=done,
-    )
-    return list(out[0::2]), list(out[1::2])
-
-
 def total(keep, came):
     return (keep.astype(F32) + came.astype(F32)).astype(BF)
 
 
-def gradients_home(place, a_layers, b_layers, c_layers, behind):
-    b_mine, b_send, c_mine, c_send = run_kernel(
-        both_layers_kernel,
-        [place] + b_layers[0] + c_layers[0] + b_layers[1] + c_layers[1],
-        [shaped(2, 4, 96, 384)] * 4,
-    )
-    mine, send = [b_mine, c_mine], [b_send, c_send]
-    keep, send = halved(mine, swaps(send, "zx", -1), done=behind)
-    came = swaps(send, "zx", 1)
-
+def gradients_home(place, a_layers, b_layers, c_layers):
     parts = [v.reshape(4, 4, 6, ROW_A).transpose(1, 0, 2, 3) for v in a_layers]
     a = jnp.stack(parts, 2).reshape(4, 4, 300, 128)
     a = jnp.pad(a, ((0, 0), (0, 0), (0, 4), (0, 0)))
@@ -729,26 +802,37 @@
         functools.partial(split_kernel, [NEAR_X]), [place, a], [like(a[0], 2)] * 2
     )
     a_came = swap(a_send, "x", -1)
-    mine, send = turn_rings(place, keep, came, "yy", done=[a_mine])
-    came = swaps(send, "yy", -1)
-    (a_keep,), (a_send,) = halved([a_mine], [a_came], done=[mine[0]])
-    a_came = swap(a_send, "x", 1)
-    keep, send = halved(mine, came, done=[a_keep])
-    came = swaps(send, "yy", 1)
+    b_mine, b_send, c_mine, c_send = run_kernel(
+        both_layers_kernel,
+        [place] + b_layers[0] + c_layers[0] + b_layers[1] + c_layers[1],
+        [shaped(2, 4, 96, 384)] * 4,
+    )
+    keep, send = halved([b_mine, c_mine], swaps([b_send, c_send], "zx", -1))
+    came = swaps(send, "zx", 1)
+    (a_keep,), (a_send,) = halved([a_mine], [a_came])
     parts = run_kernel(
-        total_kernel, [a_keep, a_came], [like(a_keep[0])] * 4, scalars=False, done=[keep[0]]
-    )
-    b, c = [k.astype(F32) + v.astype(F32) for k, v in zip(keep, came)]
+        total_pair_kernel,
+        [keep[0], came[0], keep[1], came[1]],
+        [shaped(2, 96, 384)] * 4,
+        scalars=False,
+    )
+    bc = parts[0].astype(F32)
+    for part, step in zip(parts[1:], (-1, 1, 2)):
+        bc = bc + fetch(part, "y", step).astype(F32)
+    parts = run_kernel(
+        total_kernel, [a_keep, swap(a_send, "x", 1)], [like(a_keep[0])] * 4, scalars=False
+    )
     a = parts[0].astype(F32)
     for part, step in zip(parts[1:], (-1, 1, 2)):
         a = a + fetch(part, "z", step).astype(F32)
     a = a[:300].reshape(2, 6, ROW_A)
+    bc = bc.reshape(2, 96, 2, 192)
     return (
         jnp.swapaxes(a[:, :, 4 * D : 4 * D + 4], 1, 2),
         a[:, :, : 3 * D],
         a[:, :, 3 * D : 4 * D],
-        b.reshape(96, 2, 192).transpose(1, 0, 2),
-        c.reshape(96, 2, 192).transpose(1, 2, 0),
+        bc[0].transpose(1, 0, 2),
+        bc[1].transpose(1, 2, 0),
     )
 
 
@@ -762,8 +846,8 @@
     near = [1 + (v + core) % 2 for v in (x, y, z)]
     place = jnp.stack([x, high, length] + near + [low]).astype(jnp.int32)
 
-    def weights_of(pairs, far):
-        return [[p, f, with_core(p), with_core(f)] for p, f in zip(pairs, far)]
+    def weights_of(pair, far):
+        return [pair, far, with_core(pair), with_core(far)]
 
     def behind(values, done):
         return list(after(values, done))
@@ -794,16 +878,19 @@
         place, norm_params, attn_in, attn_out, mlp_in, mlp_out, [other]
     )
     grad_mine, grad_other = mine_and_other(cotangent)
+    a_around, *bc_around = around[0]
+    a_pair = join([a_around], [swap(a_around, "y", 1)], [pa, po, p2, hidden] + bc_around)
+    bc_pair = join(bc_around, swaps(bc_around, "xz", 1), a_pair + around[1])
+    a_far = swap(a_pair[0], "y", -1)
+    (a_far,) = after([a_far], bc_pair)
+    a_weights = [weights_of(a_pair[0], a_far)]
+    bc_far = swaps(bc_pair, "xz", -1)
     weights = [None, None]
-    pairs = join(around[0], swaps(around[0], LAST, 1), [pa, po, p2, hidden])
-    far = behind(swaps(pairs, LAST, -1), [])
-    weights[0] = weights_of(pairs[:1] + behind(pairs[1:], far[:1]), far)
     records = []
     for layer in range(2):
-        a_weights = weights[layer][0]
         a1p_keep, a1p_send, gains, *pieces = run_kernel(
             qkv_kernel,
-            [place, hidden, pa] + a_weights,
+            [place, hidden, pa] + a_weights[layer],
             [shaped(TOKENS, 384), shaped(TOKENS, 384), shaped(8, D, dtype=F32)]
             + [shaped(576, TOKENS)] * 4,
             (
@@ -814,13 +901,14 @@
             ),
             flops=4 * UNIT,
             any_count=4,
-            done=[weights[layer][n][1] for n in (1, 2)],
         )
-        cores = [v for part in weights[layer][1:] for v in part[2:]]
-        pieces = behind(pieces, [cores[0], cores[2]])
+        blocks = order(place, bc_pair, bc_far, "xz", done=[a1p_keep])
         turned = exchange_four(pieces)
+        blocks = behind(blocks, turned[1:])
+        cores = [with_core(v) for v in blocks]
+        weights[layer] = a_weights[layer] + [blocks[0], cores[0], blocks[1], cores[1]]
         if layer == 0:
-            held = list(after(around[1], turned[1:]))
+            held = behind(around[1], turned[1:])
             first = swaps(held, LAST, 1)
         else:
             (grad_other,) = after([grad_other], turned[1:])
@@ -829,72 +917,63 @@
             attend_kernel,
             [place] + turned,
             [shaped(GROUP, TOKENS)] * 4 + [shaped(3, 1024, dtype=F32)],
-            (pltpu.VMEM((1024, TOKENS), F32),),
             flops=ATTEND,
-            done=cores,
         )
         if layer == 0:
-            mixed = list(after(mixed, first))
+            mixed = behind(mixed, first)
+        mixed = behind(mixed, cores)
         back = exchange_four(mixed)
         if layer == 0:
-            pairs = list(after(join(held, first), back[1:]))
-            far = behind(swaps(pairs, LAST, -1), [])
-        h1, following, slope, forward_send, op_keep, act_keep = run_kernel(
-            mlp_kernel,
-            [place, hidden] + back + [a1p_send, po, p2, gains] + sum(weights[layer], []),
-            [
-                shaped(TOKENS, D, dtype=F32),
-                shaped(TOKENS, D, dtype=F32),
-                shaped(TOKENS, FF),
-                shaped(TOKENS, FF),
-                shaped(TOKENS, 384),
-                shaped(TOKENS, 1536),
-            ],
-            MLP_SCRATCH,
-            flops=11 * UNIT,
-            any_count=12,
+            a_pair = join(held[:1], first[:1])
+            bc_pair = behind(join(held[1:], first[1:], a_pair), back[1:])
+            (a_pair,) = after(a_pair, back[1:])
+            a_far = swap(a_pair, "y", -1)
+            bc_far = swaps(bc_pair, "xz", -1)
+        inputs = [place, hidden] + back + [a1p_send, po, p2, gains]
+        whole, wide_rows = shaped(TOKENS, D, dtype=F32), shaped(TOKENS, FF)
+        if layer == 0:
+            h1, following, slope, forward_send, op_keep, act_keep = run_kernel(
+                mlp_kernel,
+                inputs + weights[layer],
+                [whole, whole, wide_rows, wide_rows, shaped(TOKENS, 384), shaped(TOKENS, 1536)],
+                MLP_SCRATCH,
+                flops=11 * UNIT,
+                any_count=8,
+            )
+            (a_far,) = after([a_far], [following])
+            forward0 = forward_send, with_core(forward_send)
+            a_weights.append(weights_of(a_pair, a_far))
+        else:
+            grad = in_own_order(grad_mine, grad_other)
+            following, forward_send, op_keep, act_keep, g1, back_send, dpre_keep, norm2, *pieces = (
+                run_kernel(
+                    mlp_turn_kernel,
+                    inputs + [grad] + weights[layer],
+                    [whole, wide_rows, shaped(TOKENS, 384), shaped(TOKENS, 1536)]
+                    + [whole, wide_rows, shaped(TOKENS, 1536), shaped(8, D, dtype=F32)]
+                    + [shaped(GROUP, TOKENS)] * 4,
+                    MLP_SCRATCH + (pltpu.VMEM((TOKENS, FF), BF),),
+                    flops=22 * UNIT,
+                    any_count=8,
+                    done=[forward0[1]],
+                )
+            )
+        records.append(
+            (hidden, a1p_keep, gains, turned, mixed, sums, forward_send, op_keep, act_keep)
         )
-        records.append(
-            (hidden, a1p_keep, gains, turned, mixed, sums, h1, slope, forward_send, op_keep, act_keep)
-        )
-        if layer == 0:
-            far = behind(far, [following])
-            weights[1] = weights_of(pairs[:2] + behind(pairs[2:], [following]), far)
         hidden = following
 
-    def leave(values, ahead=()):
+    def leave(values, ahead, dtype):
         values = jnp.dot(
             values, p2.astype(F32).T, precision=lax.Precision.HIGHEST, preferred_element_type=F32
         )
-        far = values[128:]
-        if ahead:
-            (far,) = after([far], list(ahead))
-        else:
-            far = far.astype(BF)
+        (far,) = after([values[128:].astype(dtype)], list(ahead))
         return values[:128], fetch(far, "y", 2)
 
     def arrange(own, came):
         return jnp.stack(
             [jnp.where(high == 0, own, came), jnp.where(high == 0, came, own)]
         )[:, None]
-
-    def back_to_qkv(layer, grad, done):
-        hidden, a1p_keep, gains, turned, mixed, sums, h1, slope = records[layer][:8]
-        return run_kernel(
-            mlp_back_kernel,
-            [place, grad, slope, h1, gains, p2, po] + sum(weights[layer], []),
-            [
-                shaped(TOKENS, D, dtype=F32),
-                shaped(TOKENS, FF),
-                shaped(TOKENS, 1536),
-                shaped(8, D, dtype=F32),
-            ]
-            + [shaped(GROUP, TOKENS)] * 4,
-            MLP_SCRATCH,
-            flops=11 * UNIT,
-            any_count=12,
-            done=done,
-        )
 
     def mlp_gradients(forward, back, act_keep, dpre_keep):
         return run_kernel(
@@ -920,7 +999,6 @@
             attend_back_kernel,
             [place] + turned + grad_mixed + mixed + [sums],
             [shaped(576, TOKENS)] * 4,
-            (pltpu.VMEM((1024, TOKENS), F32),),
             flops=3 * ATTEND,
             done=done,
         )
@@ -929,15 +1007,15 @@
         hidden, gains = records[layer][0], records[layer][2]
         return run_kernel(
             qkv_back_kernel,
-            [place] + grad_pieces + [hidden, g1, gains, pa, norm2] + weights[layer][0],
-            [shaped(TOKENS, D, dtype=F32), shaped(3 * D, TOKENS), shaped(8, D, dtype=F32)],
+            [place] + grad_pieces + [hidden, g1, gains, pa, norm2] + a_weights[layer],
+            [shaped(TOKENS, D, dtype=F32), shaped(3 * D + 48, TOKENS)],
             (pltpu.VMEM((D, 3 * D), BF), pltpu.SemaphoreType.DMA((8,))),
             flops=5 * UNIT,
             any_count=4,
             done=done,
         )
 
-    def attn_gradients(forward, back, a1p_keep, op_keep, dqkv, norms, done=()):
+    def attn_gradients(forward, back, a1p_keep, op_keep, dqkv, done=()):
         return run_kernel(
             attn_grad_kernel,
             [
@@ -950,8 +1028,6 @@
                 (back[1], 768, 3),
                 dqkv[0],
                 dqkv[1],
-                norms[0],
-                norms[1],
                 pa,
             ],
             [shaped(2, 96, ROW_A)] * 2,
@@ -959,65 +1035,70 @@
             done=done,
         )
 
-    grad = in_own_order(grad_mine, grad_other)
-
-    forward_send, op_keep, act_keep = records[1][8:]
+    forward_send, op_keep, act_keep = records[1][6:]
     a1p_keep = records[1][1]
     forward = forward_send, with_core(forward_send)
-    g1, back_send, dpre_keep, norm2, *pieces = back_to_qkv(1, grad, [])
     grad_mixed = exchange_four(pieces)
     back = back_send, with_core(back_send)
     b1_mine, b1_send, c1_mine, c1_send = mlp_gradients(forward, back, act_keep, dpre_keep)
     b1_send, c1_send = after([b1_send, c1_send], grad_mixed[1:])
     b1_came, c1_came = swap(b1_send, "x", -1), swap(c1_send, "z", -1)
-    outputs = leave(hidden, grad_mixed[1:])
+    outputs = leave(hidden, grad_mixed[1:], F32)
     pieces = attend_back(1, grad_mixed, [b1_mine])
     pieces = after(pieces, [outputs[1], b1_came, c1_came])
     grad_pieces = exchange_four(pieces)
     (b1_keep, c1_keep), (b1_send, c1_send) = halved([b1_mine, c1_mine], [b1_came, c1_came])
-    b1_send, c1_send = after([b1_send, c1_send], grad_pieces[1:])
+    dqkv, g1, back_send0, dpre_keep0, norm2, *pieces = run_kernel(
+        qkv_back_into_mlp_kernel,
+        [place] + grad_pieces + [records[1][0], g1, records[1][2], pa, norm2]
+        + [slope, h1, records[0][2], p2, po] + a_weights[1] + weights[0],
+        [shaped(3 * D + 48, TOKENS), whole, wide_rows]
+        + [shaped(TOKENS, 1536), shaped(8, D, dtype=F32)]
+        + [shaped(GROUP, TOKENS)] * 4,
+        MLP_SCRATCH + (pltpu.VMEM((D, 3 * D), BF), pltpu.SemaphoreType.DMA((8,))),
+        flops=16 * UNIT,
+        any_count=12,
+        done=[b1_keep],
+    )
+    dqkv = dqkv, with_core(dqkv)
+
+    _, op_keep0, act_keep0 = records[0][6:]
+    a1p_keep0 = records[0][1]
+    grad_mixed = exchange_four(pieces)
+    a1_mine, a1_send = attn_gradients(forward, back, a1p_keep, op_keep, dqkv)
+    a1_send, b1_send, c1_send = after([a1_send, b1_send, c1_send], grad_mixed[1:])
+    a1_came = swap(a1_send, "y", -1)
     b1_came, c1_came = swap(b1_send, "x", 1), swap(c1_send, "z", 1)
-    grad, dqkv, norms = qkv_back(1, grad_pieces, g1, norm2, [b1_keep])
-    dqkv, norms = (dqkv, with_core(dqkv)), (norms, with_core(norms))
-
-    forward_send0, op_keep0, act_keep0 = records[0][8:]
-    a1p_keep0 = records[0][1]
-    forward0 = forward_send0, with_core(forward_send0)
-    g1, back_send0, dpre_keep0, norm2, *pieces = back_to_qkv(0, grad, [b1_came, c1_came])
-    pieces = after(pieces, [dqkv[1], norms[1]])
-    grad_mixed = exchange_four(pieces)
+    pieces = attend_back(0, grad_mixed, [a1_mine])
+    pieces = after(pieces, [a1_came, b1_came, c1_came])
+    dpre_keep0, back_send0 = after([dpre_keep0, back_send0], pieces[:1])
     back0 = back_send0, with_core(back_send0)
+    grad_pieces = exchange_four(pieces)
     b0_mine, b0_send, c0_mine, c0_send = mlp_gradients(forward0, back0, act_keep0, dpre_keep0)
-    b0_send, c0_send = after([b0_send, c0_send], grad_mixed[1:])
+    (a1_keep,), (a1_send,) = halved([a1_mine], [a1_came], [b0_mine])
+    a1_send, b0_send, c0_send = after([a1_send, b0_send, c0_send], grad_pieces[1:])
+    a1_came = swap(a1_send, "y", 1)
     b0_came, c0_came = swap(b0_send, "x", -1), swap(c0_send, "z", -1)
-    pieces = attend_back(0, grad_mixed, [b0_mine])
-    pieces = after(pieces, [b0_came, c0_came])
-    (op_keep,) = after([op_keep], pieces[:1])
-    grad_pieces = exchange_four(pieces)
-    a1_mine, a1_send = attn_gradients(forward, back, a1p_keep, op_keep, dqkv, norms)
-    (a1_send,) = after([a1_send], grad_pieces[1:])
-    a1_came = swap(a1_send, "y", -1)
-    grad, dqkv, norms = qkv_back(0, grad_pieces, g1, norm2, [a1_mine])
-    dqkv, norms = (dqkv, with_core(dqkv)), (norms, with_core(norms))
-    (b0_keep, c0_keep, a1_keep), (b0_send, c0_send, a1_send) = halved(
-        [b0_mine, c0_mine, a1_mine], [b0_came, c0_came, a1_came], [grad]
-    )
-    b0_came, c0_came = swap(b0_send, "x", 1), swap(c0_send, "z", 1)
-    a1_came = swap(a1_send, "y", 1)
-    grad_own, grad_far = leave(grad)
+    grad, dqkv = qkv_back(0, grad_pieces, g1, norm2, [b0_mine, a1_keep])
+    grad, dqkv = after([grad, dqkv], [a1_came])
+    dqkv = dqkv, with_core(dqkv)
+    grad_own, grad_far = leave(grad, [], BF)
     a0_mine, a0_send = attn_gradients(
-        forward0, back0, a1p_keep0, op_keep0, dqkv, norms, [b0_keep]
-    )
-    (a0_send,) = after([a0_send], [b0_came, c0_came, a1_came, grad_far])
+        forward0, back0, a1p_keep0, op_keep0, dqkv
+    )
+    (a0_send,) = after([a0_send], [grad_far])
     a0_came = swap(a0_send, "y", -1)
     (a0_keep,), (a0_send,) = halved([a0_mine], [a0_came])
     a0_came = swap(a0_send, "y", 1)
+    (b0_keep, c0_keep), (b0_send, c0_send) = halved(
+        [b0_mine, c0_mine], [b0_came, c0_came], [a0_keep]
+    )
+    b0_came, c0_came = swap(b0_send, "x", 1), swap(c0_send, "z", 1)
     weight_grads = gradients_home(
         place,
         [total(a0_keep, a0_came), total(a1_keep, a1_came)],
         [[b0_keep, b0_came], [b1_keep, b1_came]],
         [[c0_keep, c0_came], [c1_keep, c1_came]],
-        [a0_keep],
     )
     grad_inputs = grad_own, grad_far.astype(F32)
     return (arrange(*outputs), arrange(*grad_inputs)) + weight_grads

time: 529 us -> 502 us (0.949)
  waiting for transfers between devices: 156 us -> 114 us
  starting transfers between devices: 95.6 us -> 105 us
  local copies, waits for them, and re-layouts: 51.9 us -> 58.8 us
    ppermute x51 -> x48, waiting for transfers between devices: 71.4 us -> 28.2 us  [fetch(): return lax.ppermute(value, AXES, pairs)]
    ppermute x51 -> x48, starting transfers between devices: 39.2 us -> 59 us  [fetch(): return lax.ppermute(value, AXES, pairs)]
    ppermute x46 -> x42, starting transfers between devices: 56.4 us -> 46.4 us  [swap(): return lax.ppermute(value, AXES, pairs)]
    unnamed x218 -> x210, local copies, waits for them, and re-layouts: 38 us -> 43 us
    pallas_call x34 -> x39, Pallas kernels: 202 us -> 201 us  [run_kernel(): pl.pallas_call(whole, grid=(1,), out_shape=tuple(outs), in_specs=specs +...]
    ppermute x46 -> x42, waiting for transfers between devices: 84.5 us -> 86 us  [swap(): return lax.ppermute(value, AXES, pairs)]
  transfers between devices with their start and end apart: 97 -> 90, of which waited for: 47 -> 41; matrix products, arithmetic and copies ran while one was open for 5% -> 6% of each run, Pallas kernels for 33% -> 31%
where the time goes in v3:
time: 502 us; the launch traced here: 495 us
  Pallas kernels  201 us (40%)
  waiting for transfers between devices  114 us (23%)
  starting transfers between devices  105 us (21%)
  local copies, waits for them, and re-layouts  58.8 us (12%)
  matrix products  8.09 us (2%)
  other arithmetic  6.49 us (1%)
    pallas_call x39, Pallas kernels, run_kernel(): pl.pallas_call(whole, grid=(1,), out_shape=tuple(outs), in_specs=specs +...  201 us
    ppermute x42, waiting for transfers between devices, swap(): return lax.ppermute(value, AXES, pairs)  86 us
    ppermute x48, starting transfers between devices, fetch(): return lax.ppermute(value, AXES, pairs)  59 us
    ppermute x42, starting transfers between devices, swap(): return lax.ppermute(value, AXES, pairs)  46.4 us
    unnamed x210, local copies, waits for them, and re-layouts  43 us
    ppermute x48, waiting for transfers between devices, fetch(): return lax.ppermute(value, AXES, pairs)  28.2 us
  transfers between devices with their start and end apart: 90, of which 41 were waited for; matrix products, arithmetic and copies ran while one was open for 6% of the time, Pallas kernels for 31%

profile of v3, /device:TPU:0, one launch (start us, length us, event | category | flops | bytes accessed | tf_op | source)
XLA Modules:
  0.0 495.5 jit_solution(3098978932138252333)
XLA Ops:
  46.0 6.0 %collective-permute-done.9.refs_2_ = bf16[4,96,384]{2,1,0:T(8,128)(2,1)S(1)} collective-permute-done((bf16[4,96,384]{2,1,0:T(8,128)(2,1)S(1)}, bf16[4,96,384]{2,1,0:T(8,128)(2,1)S(1)}, u32[]{:S(2)}, u32[]{:S(2)}) %collective-permute-start.9) | collective-permute-done | bytes 294944 | tf_op jit(solution)/shard_map/ppermute | solution.py:55
  88.4 6.0 %collective-permute-done.15.refs_2_ = bf16[192,1536]{1,0:T(8,128)(2,1)} collective-permute-done((bf16[192,1536]{1,0:T(8,128)(2,1)}, bf16[192,1536]{1,0:T(8,128)(2,1)}, u32[]{:S(2)}, u32[]{:S(2)}) %collective-permute-start.15) | collective-permute-done | bytes 589856 | tf_op jit(solution)/shard_map/ppermute | solution.py:55
  104.5 6.1 %shard_map.156 = (bf16[256,384]{1,0:T(8,128)(2,1)}, bf16[256,384]{1,0:T(8,128)(2,1)}, f32[8,768]{1,0:T(8,128)}, bf16[576,256]{1,0:T(8,128)(2,1)}, bf16[576,256]{...) custom-call(s32[7]{0:T(128)} %stack.55.refs_0_, f32[256,768]{1,0:T(8,128)} %fusion.4.refs_5_.refs_1_, ...), custom_call_target="tpu_custom_call" | custom-call | flops 1207959552 | bytes 8478720 | tf_op jit(solution)/shard_map/pallas_call | solution.py:687
  113.1 12.8 %collective-permute-done.25.refs_3_ = bf16[2,192,1536]{2,1,0:T(8,128)(2,1)S(1)} collective-permute-done((bf16[2,192,1536]{2,1,0:T(8,128)(2,1)}, bf16[2,192,1536]{2,1,0:T(8,128)(2,1)S(1)}, u32[]{:S(2)}, u32[]{:S(2)}) %collective-permute-start.25) | collective-permute-done | bytes 1179680 | tf_op jit(solution)/shard_map/ppermute | solution.py:55
  127.3 5.2 %shard_map.160 = (bf16[4,192,1536]{2,1,0:T(8,128)(2,1)}, bf16[4,768,384]{2,1,0:T(8,128)(2,1)}) custom-call(s32[7]{0:T(128)} %stack.55.refs_0_, bf16[2,192,1536]{2,1,0:T(8,128)(2,1)} %get-tuple-element.181.refs_1_, bf16[2,768,384]{2,1,0:T(8,128)(2,1)} %get-tuple-element.182.refs_2_, bf16[2,192,1536]{2,1,0:T(8,128)(2,1)} %copy-done.37, ...), custom_call_target="tpu_custom_call" | custom-call | tf_op jit(solution)/shard_map/pallas_call | solution.py:687
  134.7 6.3 %shard_map.157 = (bf16[192,256]{1,0:T(8,128)(2,1)}, bf16[192,256]{1,0:T(8,128)(2,1)}, bf16[192,256]{1,0:T(8,128)(2,1)}, bf16[192,256]{1,0:T(8,128)(2,1)}, f32[3,1024]{1,0:T(4,128)}) custom-call(s32[7]{0:T(128)} %stack.55.refs_0_, bf16[576,256]{1,0:T(8,128)(2,1)} %get-tuple-element.183.refs_1_, bf16[576,256]{1,0:T(8,128)(2,1)} %copy-done.40, ...), custom_call_target="tpu_custom_call" | custom-call | flops 1610612736 | bytes 1585152 | tf_op jit(solution)/shard_map/pallas_call | solution.py:687
  161.5 10.3 %collective-permute-start.33 = (bf16[2,96,3200]{2,1,0:T(8,128)(2,1)}, bf16[2,96,3200]{2,1,0:T(8,128)(2,1)S(1)}, u32[]{:S(2)}, u32[]{:S(2)}) collective-permute-start(bf16[2,96,3200]{2,1,0:T(8,128)(2,1)} %shard_map.165.refs_3_.refs_11_.refs_15_), channel_id=1, source_target_pairs={{8,0},{10,2},{12,4},{14,6},{0,8},{2,10},{4,12},{6,14},{24,16},{26,... | collective-permute-start | bytes 3686408 | tf_op jit(solution)/shard_map/ppermute | solution.py:45
  171.8 10.9 %shard_map.163 = (f32[256,768]{1,0:T(8,128)}, f32[256,768]{1,0:T(8,128)}, bf16[256,3072]{1,0:T(8,128)(2,1)}, bf16[256,3072]{1,0:T(8,128)(2,1)}, bf16[256,384]{1,0:T(8,128)(2,1)}, /*index=5*/bf16[256,1536]{1,0:T(8,128)(2,1)}) custom-call(s32[7]{0:T(128)} %stack.55.refs_0_, f32[256,768]{1,0:T(8,128)} %fusion.4.refs_5_.refs_1_, ...), custom_call_target="tpu_custom_call" | custom-call | flops 3321888768 | bytes 23814144 | tf_op jit(solution)/shard_map/pallas_call | solution.py:687
  189.5 6.1 %shard_map.167 = (bf16[256,384]{1,0:T(8,128)(2,1)}, bf16[256,384]{1,0:T(8,128)(2,1)}, f32[8,768]{1,0:T(8,128)}, bf16[576,256]{1,0:T(8,128)(2,1)}, bf16[576,256]{...) custom-call(s32[7]{0:T(128)} %stack.55.refs_0_, f32[256,768]{1,0:T(8,128)} %get-tuple-element.209.refs_1_.refs_5_, ...), custom_call_target="tpu_custom_call" | custom-call | flops 1207959552 | bytes 8478720 | tf_op jit(solution)/shard_map/pallas_call | solution.py:687
  198.4 6.3 %collective-permute-done.38.refs_3_ = bf16[2,192,1536]{2,1,0:T(8,128)(2,1)S(1)} collective-permute-done((bf16[2,192,1536]{2,1,0:T(8,128)(2,1)}, bf16[2,192,1536]{2,1,0:T(8,128)(2,1)S(1)}, u32[]{:S(2)}, u32[]{:S(2)}) %collective-permute-start.38) | collective-permute-done | bytes 1179680 | tf_op jit(solution)/shard_map/ppermute | solution.py:55
  206.2 5.2 %shard_map.171 = (bf16[4,192,1536]{2,1,0:T(8,128)(2,1)}, bf16[4,768,384]{2,1,0:T(8,128)(2,1)}) custom-call(s32[7]{0:T(128)} %stack.55.refs_0_, bf16[2,192,1536]{2,1,0:T(8,128)(2,1)} %get-tuple-element.220.refs_1_, bf16[2,768,384]{2,1,0:T(8,128)(2,1)} %get-tuple-element.221.refs_2_, bf16[2,192,1536]{2,1,0:T(8,128)(2,1)} %copy-done.36, ...), custom_call_target="tpu_custom_call" | custom-call | tf_op jit(solution)/shard_map/pallas_call | solution.py:687
  219.8 6.3 %shard_map.168 = (bf16[192,256]{1,0:T(8,128)(2,1)}, bf16[192,256]{1,0:T(8,128)(2,1)}, bf16[192,256]{1,0:T(8,128)(2,1)}, bf16[192,256]{1,0:T(8,128)(2,1)}, f32[3,1024]{1,0:T(4,128)}) custom-call(s32[7]{0:T(128)} %stack.55.refs_0_, bf16[576,256]{1,0:T(8,128)(2,1)} %get-tuple-element.210.refs_1_, bf16[576,256]{1,0:T(8,128)(2,1)} %copy-done.33, ...), custom_call_target="tpu_custom_call" | custom-call | flops 1610612736 | bytes 1585152 | tf_op jit(solution)/shard_map/pallas_call | solution.py:687
  238.8 14.1 %shard_map.175 = (f32[256,768]{1,0:T(8,128)}, bf16[256,3072]{1,0:T(8,128)(2,1)}, bf16[256,384]{1,0:T(8,128)(2,1)}, bf16[256,1536]{1,0:T(8,128)(2,1)}, f32[256,76...) custom-call(s32[7]{0:T(128)} %stack.55.refs_0_, ...), custom_call_target="tpu_custom_call" | custom-call | flops 6643777536 | bytes 25804800 | tf_op jit(solution)/shard_map/pallas_call | solution.py:687
  260.0 8.7 %shard_map.177 = (bf16[2,192,1536]{2,1,0:T(8,128)(2,1)}, bf16[2,192,1536]{2,1,0:T(8,128)(2,1)}, bf16[2,768,384]{2,1,0:T(8,128)(2,1)}, bf16[2,768,384]{2,1,0:T(8,128)(2,1)}) custom-call(s32[7]{0:T(128)} %stack.55.refs_0_, bf16[256,3072]{1,0:T(8,128)(2,1)} %get-tuple-element.240.refs_1_, bf16[256,3072]{1,0:T(8,128)(2,1)} %copy-done.5, ...), custom_call_target="tpu_custom_call" | custom-call | flops 2415919104 | bytes 9437184 | tf_op jit(solution)/shard_map/pallas_call | solution.py:687
  276.3 10.1 %shard_map.178 = (bf16[576,256]{1,0:T(8,128)(2,1)}, bf16[576,256]{1,0:T(8,128)(2,1)}, bf16[576,256]{1,0:T(8,128)(2,1)}, bf16[576,256]{1,0:T(8,128)(2,1)}) custom-call(s32[7]{0:T(128)} %stack.55.refs_0_, bf16[576,256]{1,0:T(8,128)(2,1)} %get-tuple-element.210.refs_1_, bf16[576,256]{1,0:T(8,128)(2,1)} %copy-done.33, bf16[576,256]{1,0:T(8,128)(2,1)} %copy-done.34, ...), custom_call_target="tpu_custom_call" | custom-call | flops 4831838208 | bytes 3158016 | tf_op jit(solution)/shard_map/pallas_call | solution.py:687
  305.8 18.8 %shard_map.182 = (bf16[2352,256]{1,0:T(8,128)(2,1)}, f32[256,768]{1,0:T(8,128)}, bf16[256,3072]{1,0:T(8,128)(2,1)}, bf16[256,1536]{1,0:T(8,128)(2,1)}, f32[8,768...) custom-call(s32[7]{0:T(128)} %stack.55.refs_0_, ...), custom_call_target="tpu_custom_call" | custom-call | flops 4831838208 | bytes 32759808 | tf_op jit(solution)/shard_map/pallas_call | solution.py:687
  329.7 6.6 %shard_map.183 = (bf16[2,96,3200]{2,1,0:T(8,128)(2,1)}, bf16[2,96,3200]{2,1,0:T(8,128)(2,1)}) custom-call(s32[7]{0:T(128)} %stack.55.refs_0_, bf16[256,384]{1,0:T(8,128)(2,1)} %get-tuple-element.222.refs_5_.refs_1_, bf16[256,3072]{1,0:T(8,128)(2,1)} %copy-done.5, bf16[256,384]{1,0:T(8,128)(2,1)} %get-tuple-element.268.refs_3_, bf16[256,3072]{1,0:T(8,128)(2,1)} %copy-done.5, ...), custom_call_target="tpu_custom_call" | custom-call | flops 1207959552 | bytes 7618560 | tf_op jit(solution)/shard_map/pallas_call | solution.py:687
  342.1 10.1 %shard_map.184 = (bf16[576,256]{1,0:T(8,128)(2,1)}, bf16[576,256]{1,0:T(8,128)(2,1)}, bf16[576,256]{1,0:T(8,128)(2,1)}, bf16[576,256]{1,0:T(8,128)(2,1)}) custom-call(s32[7]{0:T(128)} %stack.55.refs_0_, bf16[576,256]{1,0:T(8,128)(2,1)} %get-tuple-element.183.refs_1_, bf16[576,256]{1,0:T(8,128)(2,1)} %copy-done.40, bf16[576,256]{1,0:T(8,128)(2,1)} %copy-done.41, ...), custom_call_target="tpu_custom_call" | custom-call | flops 4831838208 | bytes 3158016 | tf_op jit(solution)/shard_map/pallas_call | solution.py:687
  362.5 8.6 %shard_map.188 = (bf16[2,192,1536]{2,1,0:T(8,128)(2,1)}, bf16[2,192,1536]{2,1,0:T(8,128)(2,1)}, bf16[2,768,384]{2,1,0:T(8,128)(2,1)}, bf16[2,768,384]{2,1,0:T(8,128)(2,1)}) custom-call(s32[7]{0:T(128)} %stack.55.refs_0_, bf16[256,3072]{1,0:T(8,128)(2,1)} %get-tuple-element.233.refs_1_, bf16[256,3072]{1,0:T(8,128)(2,1)} %copy-done.4, ...), custom_call_target="tpu_custom_call" | custom-call | flops 2415919104 | bytes 9437184 | tf_op jit(solution)/shard_map/pallas_call | solution.py:687
  377.1 8.4 %shard_map.190 = (f32[256,768]{1,0:T(8,128)}, bf16[2352,256]{1,0:T(8,128)(2,1)}) custom-call(s32[7]{0:T(128)} %stack.55.refs_0_, bf16[576,256]{1,0:T(8,128)(2,1)} %get-tuple-element.281.refs_2_.refs_1_, bf16[576,256]{1,0:T(8,128)(2,1)} %copy-done.49, bf16[576,256]{1,0:T(8,128)(2,1)} %copy-done.50, bf16[576,256]{1,0:T(8,128)(2,1)} %copy-done.51, ...), custom_call_target="tpu_custom_call" | custom-call | flops 1509949440 | bytes 10887168 | tf_op jit(solution)/shard_map/pallas_call | solution.py:687
  395.7 6.6 %shard_map.194 = (bf16[2,96,3200]{2,1,0:T(8,128)(2,1)}, bf16[2,96,3200]{2,1,0:T(8,128)(2,1)}) custom-call(s32[7]{0:T(128)} %stack.55.refs_0_, bf16[256,384]{1,0:T(8,128)(2,1)} %get-tuple-element.198.refs_5_.refs_1_, bf16[256,3072]{1,0:T(8,128)(2,1)} %copy-done.4, bf16[256,384]{1,0:T(8,128)(2,1)} %get-tuple-element.301.refs_3_, bf16[256,3072]{1,0:T(8,128)(2,1)} %copy-done.4, ...), custom_call_target="tpu_custom_call" | custom-call | flops 1207959552 | bytes 7618560 | tf_op jit(solution)/shard_map/pallas_call | solution.py:687
  405.6 15.5 %collective-permute-done.72.refs_1_ = bf16[2,96,3200]{2,1,0:T(8,128)(2,1)S(1)} collective-permute-done((bf16[2,96,3200]{2,1,0:T(8,128)(2,1)}, bf16[2,96,3200]{2,1,0:T(8,128)(2,1)S(1)}, u32[]{:S(2)}, u32[]{:S(2)}) %collective-permute-start.72) | collective-permute-done | bytes 1228832 | tf_op jit(solution)/shard_map/ppermute | solution.py:55
  431.9 8.6 %collective-permute-done.81.refs_2_ = bf16[192,1536]{1,0:T(8,128)(2,1)S(1)} collective-permute-done((bf16[192,1536]{1,0:T(8,128)(2,1)}, bf16[192,1536]{1,0:T(8,128)(2,1)S(1)}, u32[]{:S(2)}, u32[]{:S(2)}) %collective-permute-start.81) | collective-permute-done | bytes 589856 | tf_op jit(solution)/shard_map/ppermute | solution.py:55
  441.8 5.4 %shard_map.201 = (bf16[2,4,96,384]{3,2,1,0:T(8,128)(2,1)}, bf16[2,4,96,384]{3,2,1,0:T(8,128)(2,1)}, bf16[2,4,96,384]{3,2,1,0:T(8,128)(2,1)}, bf16[2,4,96,384]{3,2,1,0:T(8,128)(2,1)}) custom-call(s32[7]{0:T(128)} %stack.55.refs_0_, bf16[192,1536]{1,0:T(8,128)(2,1)} %get-tuple-element.318.refs_1_, bf16[192,1536]{1,0:T(8,128)(2,1)} %copy-done.62, ...), custom_call_target="tpu_custom_call" | custom-call | tf_op jit(solution)/shard_map/pallas_call | solution.py:687
  (477 shorter events, 284.6 us)
Async XLA Ops:
  43.3 17.2 %collective-permute-start.8 = (bf16[2,4,304,128]{3,2,1,0:T(8,128)(2,1)}, bf16[2,4,304,128]{3,2,1,0:T(8,128)(2,1)S(1)}, u32[]{:S(2)}, u32[]{:S(2)}) collective-permute-start(bf16[2,4,304,128]{3,2,1,0:T(8,128)(2,1)} %shard_map.148.refs_4_.refs_1_), channel_id=1, source_target_pairs={{0,6},{2,4},{4,2},{6,0},{8,10},{10,8},{12,14},{14,12},{16,22},{18,... | collective-permute-start | bytes 1867784 | tf_op jit(solution)/shard_map/ppermute | solution.py:55
  55.8 16.2 %collective-permute-start.12 = (bf16[2,4,96,384]{3,2,1,0:T(8,128)(2,1)}, bf16[2,4,96,384]{3,2,1,0:T(8,128)(2,1)S(1)}, u32[]{:S(2)}, u32[]{:S(2)}) collective-permute-start(bf16[2,4,96,384]{3,2,1,0:T(8,128)(2,1)} %get-tuple-element.175.refs_3_.refs_1_), channel_id=1, source_target_pairs={{0,96},{2,98},{4,100},{6,102},{8,40},{10,42},{12,44},{14,46},{16,1... | collective-permute-start | bytes 1769480 | tf_op jit(solution)/shard_map/ppermute | solution.py:55
  58.4 16.5 %collective-permute-start.13 = (bf16[2,4,96,384]{3,2,1,0:T(8,128)(2,1)}, bf16[2,4,96,384]{3,2,1,0:T(8,128)(2,1)}, u32[]{:S(2)}, u32[]{:S(2)}) collective-permute-start(bf16[2,4,96,384]{3,2,1,0:T(8,128)(2,1)} %get-tuple-element.176.refs_4_.refs_2_), channel_id=1, source_target_pairs={{0,17},{2,19},{4,21},{6,23},{8,24},{10,26},{12,28},{14,30},{16,1},... | collective-permute-start | bytes 1769480 | tf_op jit(solution)/shard_map/ppermute | solution.py:55
  81.1 18.2 %collective-permute-start.14 = (bf16[2,96,3200]{2,1,0:T(8,128)(2,1)}, bf16[2,96,3200]{2,1,0:T(8,128)(2,1)S(1)}, u32[]{:S(2)}, u32[]{:S(2)}) collective-permute-start(bf16[2,96,3200]{2,1,0:T(8,128)(2,1)} %shard_map.152.refs_4_.refs_3_.refs_10_.refs_19_), channel_id=1, source_target_pairs={{0,17},{2,19},{4,21},{6,23},{8,24},{10,26},{12,28},{14,30},{16,1},... | collective-permute-start | bytes 3686408 | tf_op jit(solution)/shard_map/ppermute | solution.py:55
  100.3 25.5 %collective-permute-start.25 = (bf16[2,192,1536]{2,1,0:T(8,128)(2,1)}, bf16[2,192,1536]{2,1,0:T(8,128)(2,1)S(1)}, u32[]{:S(2)}, u32[]{:S(2)}) collective-permute-start(bf16[2,192,1536]{2,1,0:T(8,128)(2,1)} %get-tuple-element.181.refs_1_), channel_id=1, source_target_pairs={{0,6},{2,4},{4,2},{6,0},{8,10},{10,8},{12,14},{14,12},{16,22},{18,... | collective-permute-start | bytes 3538952 | tf_op jit(solution)/shard_map/ppermute | solution.py:55
  100.8 25.1 %collective-permute-start.26 = (bf16[2,768,384]{2,1,0:T(8,128)(2,1)}, bf16[2,768,384]{2,1,0:T(8,128)(2,1)S(1)}, u32[]{:S(2)}, u32[]{:S(2)}) collective-permute-start(bf16[2,768,384]{2,1,0:T(8,128)(2,1)} %get-tuple-element.182.refs_2_), channel_id=1, source_target_pairs={{0,96},{2,98},{4,100},{6,102},{8,40},{10,42},{12,44},{14,46},{16,1... | collective-permute-start | bytes 3538952 | tf_op jit(solution)/shard_map/ppermute | solution.py:55
  110.6 21.9 %collective-permute-start.19 = (bf16[576,256]{1,0:T(8,128)(2,1)}, bf16[576,256]{1,0:T(8,128)(2,1)S(1)}, u32[]{:S(2)}, u32[]{:S(2)}) collective-permute-start(bf16[576,256]{1,0:T(8,128)(2,1)} %get-tuple-element.184), channel_id=1, source_target_pairs={{2,0},{4,2},{6,4},{0,6},{10,8},{12,10},{14,12},{8,14},{18,16},{20,... | collective-permute-start | bytes 884744 | tf_op jit(solution)/shard_map/ppermute | solution.py:45
  111.8 20.7 %collective-permute-start.20 = (bf16[576,256]{1,0:T(8,128)(2,1)}, bf16[576,256]{1,0:T(8,128)(2,1)S(1)}, u32[]{:S(2)}, u32[]{:S(2)}) collective-permute-start(bf16[576,256]{1,0:T(8,128)(2,1)} %get-tuple-element.185), channel_id=1, source_target_pairs={{4,0},{6,2},{0,4},{2,6},{12,8},{14,10},{8,12},{10,14},{20,16},{22,... | collective-permute-start | bytes 884744 | tf_op jit(solution)/shard_map/ppermute | solution.py:45
  113.1 19.5 %collective-permute-start.21 = (bf16[576,256]{1,0:T(8,128)(2,1)}, bf16[576,256]{1,0:T(8,128)(2,1)S(1)}, u32[]{:S(2)}, u32[]{:S(2)}) collective-permute-start(bf16[576,256]{1,0:T(8,128)(2,1)} %get-tuple-element.186), channel_id=1, source_target_pairs={{6,0},{0,2},{2,4},{4,6},{14,8},{8,10},{10,12},{12,14},{22,16},{16,... | collective-permute-start | bytes 884744 | tf_op jit(solution)/shard_map/ppermute | solution.py:45
  157.4 25.3 %collective-permute-start.32 = (bf16[2,96,3200]{2,1,0:T(8,128)(2,1)}, bf16[2,96,3200]{2,1,0:T(8,128)(2,1)S(1)}, u32[]{:S(2)}, u32[]{:S(2)}) collective-permute-start(bf16[2,96,3200]{2,1,0:T(8,128)(2,1)} %shard_map.165.refs_3_.refs_11_.refs_15_), channel_id=1, source_target_pairs={{0,17},{2,19},{4,21},{6,23},{8,24},{10,26},{12,28},{14,30},{16,1},... | collective-permute-start | bytes 3686408 | tf_op jit(solution)/shard_map/ppermute | solution.py:55
  161.5 26.0 %collective-permute-start.33 = (bf16[2,96,3200]{2,1,0:T(8,128)(2,1)}, bf16[2,96,3200]{2,1,0:T(8,128)(2,1)S(1)}, u32[]{:S(2)}, u32[]{:S(2)}) collective-permute-start(bf16[2,96,3200]{2,1,0:T(8,128)(2,1)} %shard_map.165.refs_3_.refs_11_.refs_15_), channel_id=1, source_target_pairs={{8,0},{10,2},{12,4},{14,6},{0,8},{2,10},{4,12},{6,14},{24,16},{26,... | collective-permute-start | bytes 3686408 | tf_op jit(solution)/shard_map/ppermute | solution.py:45
  184.2 20.4 %collective-permute-start.38 = (bf16[2,192,1536]{2,1,0:T(8,128)(2,1)}, bf16[2,192,1536]{2,1,0:T(8,128)(2,1)S(1)}, u32[]{:S(2)}, u32[]{:S(2)}) collective-permute-start(bf16[2,192,1536]{2,1,0:T(8,128)(2,1)} %get-tuple-element.220.refs_1_), channel_id=1, source_target_pairs={{0,6},{2,4},{4,2},{6,0},{8,10},{10,8},{12,14},{14,12},{16,22},{18,... | collective-permute-start | bytes 3538952 | tf_op jit(solution)/shard_map/ppermute | solution.py:55
  187.4 17.6 %collective-permute-start.39 = (bf16[2,768,384]{2,1,0:T(8,128)(2,1)}, bf16[2,768,384]{2,1,0:T(8,128)(2,1)S(1)}, u32[]{:S(2)}, u32[]{:S(2)}) collective-permute-start(bf16[2,768,384]{2,1,0:T(8,128)(2,1)} %get-tuple-element.221.refs_2_), channel_id=1, source_target_pairs={{0,96},{2,98},{4,100},{6,102},{8,40},{10,42},{12,44},{14,46},{16,1... | collective-permute-start | bytes 3538952 | tf_op jit(solution)/shard_map/ppermute | solution.py:55
  195.6 18.5 %collective-permute-start.35 = (bf16[576,256]{1,0:T(8,128)(2,1)}, bf16[576,256]{1,0:T(8,128)(2,1)S(1)}, u32[]{:S(2)}, u32[]{:S(2)}) collective-permute-start(bf16[576,256]{1,0:T(8,128)(2,1)} %get-tuple-element.211), channel_id=1, source_target_pairs={{2,0},{4,2},{6,4},{0,6},{10,8},{12,10},{14,12},{8,14},{18,16},{20,... | collective-permute-start | bytes 884744 | tf_op jit(solution)/shard_map/ppermute | solution.py:45
  197.4 16.7 %collective-permute-start.36 = (bf16[576,256]{1,0:T(8,128)(2,1)}, bf16[576,256]{1,0:T(8,128)(2,1)S(1)}, u32[]{:S(2)}, u32[]{:S(2)}) collective-permute-start(bf16[576,256]{1,0:T(8,128)(2,1)} %get-tuple-element.212), channel_id=1, source_target_pairs={{4,0},{6,2},{0,4},{2,6},{12,8},{14,10},{8,12},{10,14},{20,16},{22,... | collective-permute-start | bytes 884744 | tf_op jit(solution)/shard_map/ppermute | solution.py:45
  197.4 17.1 %collective-permute-start.37 = (bf16[576,256]{1,0:T(8,128)(2,1)}, bf16[576,256]{1,0:T(8,128)(2,1)S(1)}, u32[]{:S(2)}, u32[]{:S(2)}) collective-permute-start(bf16[576,256]{1,0:T(8,128)(2,1)} %get-tuple-element.213), channel_id=1, source_target_pairs={{6,0},{0,2},{2,4},{4,6},{14,8},{8,10},{10,12},{12,14},{22,16},{16,... | collective-permute-start | bytes 884744 | tf_op jit(solution)/shard_map/ppermute | solution.py:45
  269.5 17.6 %collective-permute-start.53 = (bf16[2,192,1536]{2,1,0:T(8,128)(2,1)}, bf16[2,192,1536]{2,1,0:T(8,128)(2,1)S(1)}, u32[]{:S(2)}, u32[]{:S(2)}) collective-permute-start(bf16[2,192,1536]{2,1,0:T(8,128)(2,1)} %get-tuple-element.251), channel_id=1, source_target_pairs={{0,6},{2,4},{4,2},{6,0},{8,10},{10,8},{12,14},{14,12},{16,22},{18,... | collective-permute-start | bytes 3538952 | tf_op jit(solution)/shard_map/ppermute | solution.py:55
  270.1 17.6 %collective-permute-start.54 = (bf16[2,768,384]{2,1,0:T(8,128)(2,1)}, bf16[2,768,384]{2,1,0:T(8,128)(2,1)S(1)}, u32[]{:S(2)}, u32[]{:S(2)}) collective-permute-start(bf16[2,768,384]{2,1,0:T(8,128)(2,1)} %get-tuple-element.252), channel_id=1, source_target_pairs={{0,96},{2,98},{4,100},{6,102},{8,40},{10,42},{12,44},{14,46},{16,1... | collective-permute-start | bytes 3538952 | tf_op jit(solution)/shard_map/ppermute | solution.py:55
  337.0 18.2 %collective-permute-start.62 = (bf16[2,96,3200]{2,1,0:T(8,128)(2,1)}, bf16[2,96,3200]{2,1,0:T(8,128)(2,1)S(1)}, u32[]{:S(2)}, u32[]{:S(2)}) collective-permute-start(bf16[2,96,3200]{2,1,0:T(8,128)(2,1)} %get-tuple-element.278), channel_id=1, source_target_pairs={{0,17},{2,19},{4,21},{6,23},{8,24},{10,26},{12,28},{14,30},{16,1},... | collective-permute-start | bytes 3686408 | tf_op jit(solution)/shard_map/ppermute | solution.py:55
  357.1 16.8 %collective-permute-start.65 = (bf16[576,256]{1,0:T(8,128)(2,1)S(1)}, bf16[576,256]{1,0:T(8,128)(2,1)S(1)}, u32[]{:S(2)}, u32[]{:S(2)}) collective-permute-start(bf16[576,256]{1,0:T(8,128)(2,1)S(1)} %copy-done.75), channel_id=1, source_target_pairs={{2,0},{4,2},{6,4},{0,6},{10,8},{12,10},{14,12},{8,14},{18,16},{20,... | collective-permute-start | bytes 884744 | tf_op jit(solution)/shard_map/ppermute | solution.py:45
  402.9 18.2 %collective-permute-start.72 = (bf16[2,96,3200]{2,1,0:T(8,128)(2,1)}, bf16[2,96,3200]{2,1,0:T(8,128)(2,1)S(1)}, u32[]{:S(2)}, u32[]{:S(2)}) collective-permute-start(bf16[2,96,3200]{2,1,0:T(8,128)(2,1)} %shard_map.195), channel_id=1, source_target_pairs={{0,17},{2,19},{4,21},{6,23},{8,24},{10,26},{12,28},{14,30},{16,1},... | collective-permute-start | bytes 3686408 | tf_op jit(solution)/shard_map/ppermute | solution.py:55
  404.8 20.2 %collective-permute-start.79 = (bf16[2,192,1536]{2,1,0:T(8,128)(2,1)S(1)}, bf16[2,192,1536]{2,1,0:T(8,128)(2,1)S(1)}, u32[]{:S(2)}, u32[]{:S(2)}) collective-permute-start(bf16[2,192,1536]{2,1,0:T(8,128)(2,1)S(1)} %copy-done.46), channel_id=1, source_target_pairs={{0,6},{2,4},{4,2},{6,0},{8,10},{10,8},{12,14},{14,12},{16,22},{18,... | collective-permute-start | bytes 3538952 | tf_op jit(solution)/shard_map/ppermute | solution.py:55
  405.6 19.4 %collective-permute-start.80 = (bf16[2,768,384]{2,1,0:T(8,128)(2,1)S(1)}, bf16[2,768,384]{2,1,0:T(8,128)(2,1)S(1)}, u32[]{:S(2)}, u32[]{:S(2)}) collective-permute-start(bf16[2,768,384]{2,1,0:T(8,128)(2,1)S(1)} %copy-done.47), channel_id=1, source_target_pairs={{0,96},{2,98},{4,100},{6,102},{8,40},{10,42},{12,44},{14,46},{16,1... | collective-permute-start | bytes 3538952 | tf_op jit(solution)/shard_map/ppermute | solution.py:55
  431.3 16.7 %collective-permute-start.73 = (bf16[96,3200]{1,0:T(8,128)(2,1)}, bf16[96,3200]{1,0:T(8,128)(2,1)S(1)}, u32[]{:S(2)}, u32[]{:S(2)}) collective-permute-start(bf16[96,3200]{1,0:T(8,128)(2,1)} %get-tuple-element.306), channel_id=1, source_target_pairs={{0,16},{2,18},{4,20},{6,22},{8,25},{10,27},{12,29},{14,31},{16,0},... | collective-permute-start | bytes 1843208 | tf_op jit(solution)/shard_map/ppermute | solution.py:55
  (169 other events, 930.8 us)

commit v4 on v3

--- a/solution.py
+++ b/solution.py
@@ -117,17 +117,8 @@
 
 
 def weight_blocks(refs, near):
-    pair, far, core_pair, core_far = refs
-    return [
-        (pair, 0, 0, 0),
-        (pair, 1, 0, near),
-        (far, 0, 0, 3 - near),
-        (far, 1, 0, 3),
-        (core_pair, 0, 1, 0),
-        (core_pair, 1, 1, 3 - near),
-        (core_far, 0, 1, near),
-        (core_far, 1, 1, 3),
-    ]
+    spots = [0, near, 3 - near, 3, 0, 3 - near, near, 3]
+    return [(ref, n // 4, spot) for n, (ref, spot) in enumerate(zip(refs, spots))]
 
 
 def at_rows(core, spot, rows):
@@ -135,21 +126,21 @@
 
 
 def qkv_kernel(place_ref, h_ref, pa_ref, *refs):
-    blocks = weight_blocks(refs[:4], place_ref[NEAR_Y])
-    a1p_keep, a1p_send, gains_ref = refs[4:7]
-    out_refs = refs[7:11]
-    win, table, turned, sems = refs[11:]
+    blocks = weight_blocks(refs[:8], place_ref[NEAR_Y])
+    a1p_keep, a1p_send, gains_ref = refs[8:11]
+    out_refs = refs[11:15]
+    win, table, turned, sems = refs[15:]
     norm_copies = start_copies(
         [
-            (r.at[i, :, pl.ds(FF, 128)], table.at[at_rows(core, spot, 96)])
-            for r, i, core, spot in blocks
+            (r.at[:, pl.ds(FF, 128)], table.at[at_rows(core, spot, 96)])
+            for r, core, spot in blocks
         ],
         sems.at[pl.ds(0, 8)],
     )
     win_copies = start_copies(
         [
-            (r.at[i, :, pl.ds(0, 3 * D)], win.at[at_rows(core, spot, 96)])
-            for r, i, core, spot in blocks
+            (r.at[:, pl.ds(0, 3 * D)], win.at[at_rows(core, spot, 96)])
+            for r, core, spot in blocks
         ],
         sems.at[pl.ds(8, 8)],
     )
@@ -265,15 +256,15 @@
 def mlp_copies(place_ref, refs, wout, w1, w2, sems):
     out_copies = start_copies(
         [
-            (r.at[i, :, pl.ds(3 * D, D)], wout.at[at_rows(core, spot, 96)])
-            for r, i, core, spot in weight_blocks(refs[0:4], place_ref[NEAR_Y])
+            (r.at[:, pl.ds(3 * D, D)], wout.at[at_rows(core, spot, 96)])
+            for r, core, spot in weight_blocks(refs[0:8], place_ref[NEAR_Y])
         ],
         sems.at[pl.ds(0, 8)],
     )
     first_copies = start_copies(
         [
             (ref.at[k], w1.at[core, pl.ds(192 * k, 192)])
-            for core, ref in enumerate(refs[4:6])
+            for core, ref in enumerate(refs[8:10])
             for k in range(4)
         ],
         sems.at[pl.ds(8, 8)],
@@ -281,7 +272,7 @@
     second_copies = start_copies(
         [
             (ref.at[k], w2.at[:, pl.ds((core * 4 + k) * 384, 384)])
-            for core, ref in enumerate(refs[6:8])
+            for core, ref in enumerate(refs[10:12])
             for k in range(4)
         ],
         sems.at[pl.ds(16, 8)],
@@ -354,9 +345,9 @@
 
 
 def mlp_kernel(place_ref, h_ref, u0, u1, u2, u3, a1p_send, po_ref, p2_ref, gains_ref, *refs):
-    h1_ref, next_ref, slope_ref, send_ref, op_keep, act_keep = refs[8:14]
-    turned, wout, w1, w2, sems = refs[14:]
-    copies = mlp_copies(place_ref, refs[:8], wout, w1, w2, sems)
+    h1_ref, next_ref, slope_ref, send_ref, op_keep, act_keep = refs[12:18]
+    turned, wout, w1, w2, sems = refs[18:]
+    copies = mlp_copies(place_ref, refs[:12], wout, w1, w2, sems)
     h1_ref[...], next_ref[...] = mlp_forward(
         place_ref, h_ref[...], (u0, u1, u2, u3), a1p_send, po_ref, p2_ref, gains_ref, slope_ref,
         (send_ref, op_keep, act_keep), (turned, wout, w1, w2) + copies,
@@ -366,10 +357,10 @@
 def mlp_turn_kernel(
     place_ref, h_ref, u0, u1, u2, u3, a1p_send, po_ref, p2_ref, gains_ref, g_ref, *refs
 ):
-    next_ref, forward_send, op_keep, act_keep, g1_ref, back_send, dpre_keep, norm_ref = refs[8:16]
-    out_refs = refs[16:20]
-    turned, wout, w1, w2, sems, slope_ref = refs[20:]
-    copies = mlp_copies(place_ref, refs[:8], wout, w1, w2, sems)
+    next_ref, forward_send, op_keep, act_keep, g1_ref, back_send, dpre_keep, norm_ref = refs[12:20]
+    out_refs = refs[20:24]
+    turned, wout, w1, w2, sems, slope_ref = refs[24:]
+    copies = mlp_copies(place_ref, refs[:12], wout, w1, w2, sems)
     h1, next_ref[...] = mlp_forward(
         place_ref, h_ref[...], (u0, u1, u2, u3), a1p_send, po_ref, p2_ref, gains_ref, slope_ref,
         (forward_send, op_keep, act_keep), (turned, wout, w1, w2) + copies,
@@ -384,11 +375,11 @@
     place_ref, d0, d1, d2, d3, h_ref, g1_ref, gains_ref, pa_ref, norm2_ref,
     slope_ref, h1_ref, gains0_ref, p2_ref, po_ref, *refs,
 ):
-    dqkv_ref, next_ref, back_send, dpre_keep, below_ref = refs[12:17]
-    out_refs = refs[17:21]
-    turned, wout, w1, w2, sems, win, win_sems = refs[21:]
-    win_copies = win_start(place_ref, refs[:4], win, win_sems)
-    copies = mlp_copies(place_ref, refs[4:12], wout, w1, w2, sems)
+    dqkv_ref, next_ref, back_send, dpre_keep, below_ref = refs[20:25]
+    out_refs = refs[25:29]
+    turned, wout, w1, w2, sems, win, win_sems = refs[29:]
+    win_copies = win_start(place_ref, refs[:8], win, win_sems)
+    copies = mlp_copies(place_ref, refs[8:20], wout, w1, w2, sems)
     grad = qkv_backward(
         place_ref, (d0, d1, d2, d3), h_ref, g1_ref, gains_ref, pa_ref, norm2_ref,
         dqkv_ref, win, win_copies,
@@ -440,8 +431,8 @@
 def win_start(place_ref, refs, win, sems):
     return start_copies(
         [
-            (r.at[i, :, pl.ds(0, 3 * D)], win.at[at_rows(core, spot, 96)])
-            for r, i, core, spot in weight_blocks(refs, place_ref[NEAR_Y])
+            (r.at[:, pl.ds(0, 3 * D)], win.at[at_rows(core, spot, 96)])
+            for r, core, spot in weight_blocks(refs, place_ref[NEAR_Y])
         ],
         sems,
     )
@@ -471,8 +462,8 @@
 def qkv_back_kernel(
     place_ref, d0, d1, d2, d3, h_ref, g1_ref, gains_ref, pa_ref, norm2_ref, *refs
 ):
-    next_ref, dqkv_ref, win, sems = refs[4:]
-    copies = win_start(place_ref, refs[:4], win, sems)
+    next_ref, dqkv_ref, win, sems = refs[8:]
+    copies = win_start(place_ref, refs[:8], win, sems)
     next_ref[...] = qkv_backward(
         place_ref, (d0, d1, d2, d3), h_ref, g1_ref, gains_ref, pa_ref, norm2_ref,
         dqkv_ref, win, copies,
@@ -755,9 +746,9 @@
     bc = [mlp_in.transpose(1, 0, 2).reshape(96, 384), mlp_out.transpose(2, 0, 1).reshape(96, 384)]
     for a_axis, bc_axes in (("z", "yx"), ("x", "zy")):
         bc_near = swaps(bc, bc_axes, 1)
-        a_pair = join([a], [swap(a, a_axis, 1)], done=early + bc_near if early else bc)
+        a_pair = join([a], [swap(a, a_axis, 1)], done=bc_near if early else bc)
+        bc_pair = join(bc, bc_near, done=a_pair + early)
         early = []
-        bc_pair = join(bc, bc_near, done=a_pair)
         a_far = swap(a_pair[0], a_axis, -1)
         bc_far = swaps(bc_pair, bc_axes, -1)
         (a,) = order(place, a_pair, [a_far], a_axis, done=bc_pair)
@@ -774,7 +765,7 @@
             done=[al],
         )
         layers.append([al, bl, cl])
-    return layers
+    return layers, bc_far
 
 
 LAST = "yxz"
@@ -846,8 +837,8 @@
     near = [1 + (v + core) % 2 for v in (x, y, z)]
     place = jnp.stack([x, high, length] + near + [low]).astype(jnp.int32)
 
-    def weights_of(pair, far):
-        return [pair, far, with_core(pair), with_core(far)]
+    def weights_of(blocks):
+        return blocks + [with_core(v) for v in blocks]
 
     def behind(values, done):
         return list(after(values, done))
@@ -874,16 +865,16 @@
     mine, other = mine_and_other(inputs)
     other = fetch(other, "y", 2)
     hidden = in_own_order(mine, other)
-    around = weights_around(
+    around, beside = weights_around(
         place, norm_params, attn_in, attn_out, mlp_in, mlp_out, [other]
     )
     grad_mine, grad_other = mine_and_other(cotangent)
     a_around, *bc_around = around[0]
-    a_pair = join([a_around], [swap(a_around, "y", 1)], [pa, po, p2, hidden] + bc_around)
-    bc_pair = join(bc_around, swaps(bc_around, "xz", 1), a_pair + around[1])
-    a_far = swap(a_pair[0], "y", -1)
-    (a_far,) = after([a_far], bc_pair)
-    a_weights = [weights_of(a_pair[0], a_far)]
+    a_near, a_far = swap(a_around, "y", 1), swap(a_around, "y", -1)
+    a_near, a_far = after([a_near, a_far], [pa, po, p2, hidden] + beside)
+    bc_pair = join(bc_around, swaps(bc_around, "xz", 1), [a_near] + around[1])
+    (a_last,) = after([swap(a_near, "y", -1)], bc_pair)
+    a_weights = [weights_of([a_around, a_near, a_far, a_last])]
     bc_far = swaps(bc_pair, "xz", -1)
     weights = [None, None]
     records = []
@@ -900,7 +891,7 @@
                 pltpu.SemaphoreType.DMA((16,)),
             ),
             flops=4 * UNIT,
-            any_count=4,
+            any_count=8,
         )
         blocks = order(place, bc_pair, bc_far, "xz", done=[a1p_keep])
         turned = exchange_four(pieces)
@@ -924,10 +915,9 @@
         mixed = behind(mixed, cores)
         back = exchange_four(mixed)
         if layer == 0:
-            a_pair = join(held[:1], first[:1])
-            bc_pair = behind(join(held[1:], first[1:], a_pair), back[1:])
-            (a_pair,) = after(a_pair, back[1:])
-            a_far = swap(a_pair, "y", -1)
+            bc_pair = behind(join(held[1:], first[1:]), back[1:])
+            a_own, a_near = after([held[0], first[0]], back[1:])
+            a_far, a_last = swap(a_own, "y", -1), swap(a_near, "y", -1)
             bc_far = swaps(bc_pair, "xz", -1)
         inputs = [place, hidden] + back + [a1p_send, po, p2, gains]
         whole, wide_rows = shaped(TOKENS, D, dtype=F32), shaped(TOKENS, FF)
@@ -938,11 +928,11 @@
                 [whole, whole, wide_rows, wide_rows, shaped(TOKENS, 384), shaped(TOKENS, 1536)],
                 MLP_SCRATCH,
                 flops=11 * UNIT,
-                any_count=8,
+                any_count=12,
             )
-            (a_far,) = after([a_far], [following])
+            a_far, a_last = after([a_far, a_last], [following])
             forward0 = forward_send, with_core(forward_send)
-            a_weights.append(weights_of(a_pair, a_far))
+            a_weights.append(weights_of([a_own, a_near, a_far, a_last]))
         else:
             grad = in_own_order(grad_mine, grad_other)
             following, forward_send, op_keep, act_keep, g1, back_send, dpre_keep, norm2, *pieces = (
@@ -954,7 +944,7 @@
                     + [shaped(GROUP, TOKENS)] * 4,
                     MLP_SCRATCH + (pltpu.VMEM((TOKENS, FF), BF),),
                     flops=22 * UNIT,
-                    any_count=8,
+                    any_count=12,
                     done=[forward0[1]],
                 )
             )
@@ -1011,7 +1001,7 @@
             [shaped(TOKENS, D, dtype=F32), shaped(3 * D + 48, TOKENS)],
             (pltpu.VMEM((D, 3 * D), BF), pltpu.SemaphoreType.DMA((8,))),
             flops=5 * UNIT,
-            any_count=4,
+            any_count=8,
             done=done,
         )
 
@@ -1057,7 +1047,7 @@
         + [shaped(GROUP, TOKENS)] * 4,
         MLP_SCRATCH + (pltpu.VMEM((D, 3 * D), BF), pltpu.SemaphoreType.DMA((8,))),
         flops=16 * UNIT,
-        any_count=12,
+        any_count=20,
         done=[b1_keep],
     )
     dqkv = dqkv, with_core(dqkv)
@@ -1088,11 +1078,10 @@
     )
     (a0_send,) = after([a0_send], [grad_far])
     a0_came = swap(a0_send, "y", -1)
-    (a0_keep,), (a0_send,) = halved([a0_mine], [a0_came])
+    (a0_keep, b0_keep, c0_keep), (a0_send, b0_send, c0_send) = halved(
+        [a0_mine, b0_mine, c0_mine], [a0_came, b0_came, c0_came]
+    )
     a0_came = swap(a0_send, "y", 1)
-    (b0_keep, c0_keep), (b0_send, c0_send) = halved(
-        [b0_mine, c0_mine], [b0_came, c0_came], [a0_keep]
-    )
     b0_came, c0_came = swap(b0_send, "x", 1), swap(c0_send, "z", 1)
     weight_grads = gradients_home(
         place,

time: 502 us -> 496 us (0.988)
  Pallas kernels: 201 us -> 194 us
    ppermute x48 -> x52, waiting for transfers between devices: 28.2 us -> 55.5 us  [fetch(): return lax.ppermute(value, AXES, pairs)]
    ppermute x42 -> x44, waiting for transfers between devices: 86 us -> 64 us  [swap(): return lax.ppermute(value, AXES, pairs)]
    ppermute x48 -> x52, starting transfers between devices: 59 us -> 43.3 us  [fetch(): return lax.ppermute(value, AXES, pairs)]
    ppermute x42 -> x44, starting transfers between devices: 46.4 us -> 62.1 us  [swap(): return lax.ppermute(value, AXES, pairs)]
    pallas_call x39 -> x36, Pallas kernels: 201 us -> 194 us  [run_kernel(): pl.pallas_call(whole, grid=(1,), out_shape=tuple(outs), in_specs=specs +...]
    unnamed x210 -> x218, local copies, waits for them, and re-layouts: 43 us -> 39.1 us
  transfers between devices with their start and end apart: 90 -> 96, of which waited for: 41 -> 44; matrix products, arithmetic and copies ran while one was open for 6% -> 6% of each run, Pallas kernels for 31% -> 31%
where the time goes in v4:
time: 496 us; the launch traced here: 491 us
  Pallas kernels  194 us (39%)
  waiting for transfers between devices  119 us (24%)
  starting transfers between devices  105 us (21%)
  local copies, waits for them, and re-layouts  56.4 us (11%)
  matrix products  6.92 us (1%)
  other arithmetic  6.46 us (1%)
    pallas_call x36, Pallas kernels, run_kernel(): pl.pallas_call(whole, grid=(1,), out_shape=tuple(outs), in_specs=specs +...  194 us
    ppermute x44, waiting for transfers between devices, swap(): return lax.ppermute(value, AXES, pairs)  64 us
    ppermute x44, starting transfers between devices, swap(): return lax.ppermute(value, AXES, pairs)  62.1 us
    ppermute x52, waiting for transfers between devices, fetch(): return lax.ppermute(value, AXES, pairs)  55.5 us
    ppermute x52, starting transfers between devices, fetch(): return lax.ppermute(value, AXES, pairs)  43.3 us
    unnamed x218, local copies, waits for them, and re-layouts  39.1 us
  transfers between devices with their start and end apart: 96, of which 44 were waited for; matrix products, arithmetic and copies ran while one was open for 6% of the time, Pallas kernels for 31%

profile of v4, /device:TPU:0, one launch (start us, length us, event | category | flops | bytes accessed | tf_op | source)
XLA Modules:
  0.0 491.0 jit_solution(1557942954482222986)
XLA Ops:
  100.6 6.0 %shard_map.156 = (bf16[256,384]{1,0:T(8,128)(2,1)}, bf16[256,384]{1,0:T(8,128)(2,1)}, f32[8,768]{1,0:T(8,128)}, bf16[576,256]{1,0:T(8,128)(2,1)}, bf16[576,256]{...) custom-call(s32[7]{0:T(128)} %stack.55.refs_0_, f32[256,768]{1,0:T(8,128)} %fusion.4.refs_5_.refs_1_, ...), custom_call_target="tpu_custom_call" | custom-call | flops 1207959552 | bytes 8478720 | tf_op jit(solution)/shard_map/pallas_call | solution.py:678
  111.7 5.2 %shard_map.160 = (bf16[4,192,1536]{2,1,0:T(8,128)(2,1)}, bf16[4,768,384]{2,1,0:T(8,128)(2,1)}) custom-call(s32[7]{0:T(128)} %stack.55.refs_0_, bf16[2,192,1536]{2,1,0:T(8,128)(2,1)} %get-tuple-element.189.refs_1_, bf16[2,768,384]{2,1,0:T(8,128)(2,1)} %get-tuple-element.190.refs_2_, bf16[2,192,1536]{2,1,0:T(8,128)(2,1)} %collective-permute-done.28.refs_3_, ...), custom_call_target="tpu_custom_call" | custom-call | tf_op jit(solution)/shard_map/pallas_call | solution.py:678
  120.0 5.2 %collective-permute-done.24.refs_4_.refs_5_ = bf16[576,256]{1,0:T(8,128)(2,1)S(1)} collective-permute-done((bf16[576,256]{1,0:T(8,128)(2,1)}, bf16[576,256]{1,0:T(8,128)(2,1)S(1)}, u32[]{:S(2)}, u32[]{:S(2)}) %collective-permute-start.24) | collective-permute-done | bytes 294944 | tf_op jit(solution)/shard_map/ppermute | solution.py:45
  126.6 6.3 %shard_map.157 = (bf16[192,256]{1,0:T(8,128)(2,1)}, bf16[192,256]{1,0:T(8,128)(2,1)}, bf16[192,256]{1,0:T(8,128)(2,1)}, bf16[192,256]{1,0:T(8,128)(2,1)}, f32[3,1024]{1,0:T(4,128)}) custom-call(s32[7]{0:T(128)} %stack.55.refs_0_, bf16[576,256]{1,0:T(8,128)(2,1)} %get-tuple-element.191.refs_1_, bf16[576,256]{1,0:T(8,128)(2,1)} %copy-done.46, ...), custom_call_target="tpu_custom_call" | custom-call | flops 1610612736 | bytes 1585152 | tf_op jit(solution)/shard_map/pallas_call | solution.py:678
  157.7 12.1 %collective-permute-start.45 = (bf16[2,768,384]{2,1,0:T(8,128)(2,1)}, bf16[2,768,384]{2,1,0:T(8,128)(2,1)}, u32[]{:S(2)}, u32[]{:S(2)}) collective-permute-start(bf16[2,768,384]{2,1,0:T(8,128)(2,1)} %get-tuple-element.233.refs_2_), channel_id=1, source_target_pairs={{0,96},{2,98},{4,100},{6,102},{8,40},{10,42},{12,44},{14,46},{16,1... | collective-permute-start | bytes 3538952 | tf_op jit(solution)/shard_map/ppermute | solution.py:55
  169.8 10.9 %shard_map.163 = (f32[256,768]{1,0:T(8,128)}, f32[256,768]{1,0:T(8,128)}, bf16[256,3072]{1,0:T(8,128)(2,1)}, bf16[256,3072]{1,0:T(8,128)(2,1)}, bf16[256,384]{1,0:T(8,128)(2,1)}, /*index=5*/bf16[256,1536]{1,0:T(8,128)(2,1)}) custom-call(s32[7]{0:T(128)} %stack.55.refs_0_, f32[256,768]{1,0:T(8,128)} %fusion.4.refs_5_.refs_1_, ...), custom_call_target="tpu_custom_call" | custom-call | flops 3321888768 | bytes 23814144 | tf_op jit(solution)/shard_map/pallas_call | solution.py:678
  185.8 6.0 %shard_map.166 = (bf16[256,384]{1,0:T(8,128)(2,1)}, bf16[256,384]{1,0:T(8,128)(2,1)}, f32[8,768]{1,0:T(8,128)}, bf16[576,256]{1,0:T(8,128)(2,1)}, bf16[576,256]{...) custom-call(s32[7]{0:T(128)} %stack.55.refs_0_, ...), custom_call_target="tpu_custom_call" | custom-call | flops 1207959552 | bytes 8478720 | tf_op jit(solution)/shard_map/pallas_call | solution.py:678
  195.8 5.1 %shard_map.170 = (bf16[4,192,1536]{2,1,0:T(8,128)(2,1)}, bf16[4,768,384]{2,1,0:T(8,128)(2,1)}) custom-call(s32[7]{0:T(128)} %stack.55.refs_0_, bf16[2,192,1536]{2,1,0:T(8,128)(2,1)} %get-tuple-element.232.refs_1_, bf16[2,768,384]{2,1,0:T(8,128)(2,1)} %get-tuple-element.233.refs_2_, bf16[2,192,1536]{2,1,0:T(8,128)(2,1)} %collective-permute-done.44.refs_3_, ...), custom_call_target="tpu_custom_call" | custom-call | tf_op jit(solution)/shard_map/pallas_call | solution.py:678
  200.9 7.3 %collective-permute-done.41.refs_2_.refs_1_ = bf16[576,256]{1,0:T(8,128)(2,1)S(1)} collective-permute-done((bf16[576,256]{1,0:T(8,128)(2,1)}, bf16[576,256]{1,0:T(8,128)(2,1)S(1)}, u32[]{:S(2)}, u32[]{:S(2)}) %collective-permute-start.41) | collective-permute-done | bytes 294944 | tf_op jit(solution)/shard_map/ppermute | solution.py:45
  215.8 6.3 %shard_map.167 = (bf16[192,256]{1,0:T(8,128)(2,1)}, bf16[192,256]{1,0:T(8,128)(2,1)}, bf16[192,256]{1,0:T(8,128)(2,1)}, bf16[192,256]{1,0:T(8,128)(2,1)}, f32[3,1024]{1,0:T(4,128)}) custom-call(s32[7]{0:T(128)} %stack.55.refs_0_, bf16[576,256]{1,0:T(8,128)(2,1)} %get-tuple-element.222.refs_1_, bf16[576,256]{1,0:T(8,128)(2,1)} %copy-done.41, ...), custom_call_target="tpu_custom_call" | custom-call | flops 1610612736 | bytes 1585152 | tf_op jit(solution)/shard_map/pallas_call | solution.py:678
  232.7 14.1 %shard_map.174 = (f32[256,768]{1,0:T(8,128)}, bf16[256,3072]{1,0:T(8,128)(2,1)}, bf16[256,384]{1,0:T(8,128)(2,1)}, bf16[256,1536]{1,0:T(8,128)(2,1)}, f32[256,76...) custom-call(s32[7]{0:T(128)} %stack.55.refs_0_, ...), custom_call_target="tpu_custom_call" | custom-call | flops 6643777536 | bytes 25804800 | tf_op jit(solution)/shard_map/pallas_call | solution.py:678
  253.9 8.7 %shard_map.176 = (bf16[2,192,1536]{2,1,0:T(8,128)(2,1)}, bf16[2,192,1536]{2,1,0:T(8,128)(2,1)}, bf16[2,768,384]{2,1,0:T(8,128)(2,1)}, bf16[2,768,384]{2,1,0:T(8,128)(2,1)}) custom-call(s32[7]{0:T(128)} %stack.55.refs_0_, bf16[256,3072]{1,0:T(8,128)(2,1)} %get-tuple-element.252.refs_1_, bf16[256,3072]{1,0:T(8,128)(2,1)} %copy-done.3, ...), custom_call_target="tpu_custom_call" | custom-call | flops 2415919104 | bytes 9437184 | tf_op jit(solution)/shard_map/pallas_call | solution.py:678
  271.4 10.2 %shard_map.177 = (bf16[576,256]{1,0:T(8,128)(2,1)}, bf16[576,256]{1,0:T(8,128)(2,1)}, bf16[576,256]{1,0:T(8,128)(2,1)}, bf16[576,256]{1,0:T(8,128)(2,1)}) custom-call(s32[7]{0:T(128)} %stack.55.refs_0_, bf16[576,256]{1,0:T(8,128)(2,1)} %get-tuple-element.222.refs_1_, bf16[576,256]{1,0:T(8,128)(2,1)} %copy-done.41, bf16[576,256]{1,0:T(8,128)(2,1)} %copy-done.42, ...), custom_call_target="tpu_custom_call" | custom-call | flops 4831838208 | bytes 3158016 | tf_op jit(solution)/shard_map/pallas_call | solution.py:678
  290.9 5.8 %collective-permute-done.61.refs_2_ = bf16[576,256]{1,0:T(8,128)(2,1)S(1)} collective-permute-done((bf16[576,256]{1,0:T(8,128)(2,1)}, bf16[576,256]{1,0:T(8,128)(2,1)S(1)}, u32[]{:S(2)}, u32[]{:S(2)}) %collective-permute-start.61) | collective-permute-done | bytes 294944 | tf_op jit(solution)/shard_map/ppermute | solution.py:45
  299.8 18.9 %shard_map.181 = (bf16[2352,256]{1,0:T(8,128)(2,1)}, f32[256,768]{1,0:T(8,128)}, bf16[256,3072]{1,0:T(8,128)(2,1)}, bf16[256,1536]{1,0:T(8,128)(2,1)}, f32[8,768...) custom-call(s32[7]{0:T(128)} %stack.55.refs_0_, ...), custom_call_target="tpu_custom_call" | custom-call | flops 4831838208 | bytes 32759808 | tf_op jit(solution)/shard_map/pallas_call | solution.py:678
  323.3 6.5 %shard_map.182 = (bf16[2,96,3200]{2,1,0:T(8,128)(2,1)}, bf16[2,96,3200]{2,1,0:T(8,128)(2,1)}) custom-call(s32[7]{0:T(128)} %stack.55.refs_0_, bf16[256,384]{1,0:T(8,128)(2,1)} %get-tuple-element.234.refs_5_.refs_1_, bf16[256,3072]{1,0:T(8,128)(2,1)} %copy-done.3, bf16[256,384]{1,0:T(8,128)(2,1)} %get-tuple-element.280.refs_3_, bf16[256,3072]{1,0:T(8,128)(2,1)} %copy-done.3, ...), custom_call_target="tpu_custom_call" | custom-call | flops 1207959552 | bytes 7618560 | tf_op jit(solution)/shard_map/pallas_call | solution.py:678
  334.1 10.1 %shard_map.183 = (bf16[576,256]{1,0:T(8,128)(2,1)}, bf16[576,256]{1,0:T(8,128)(2,1)}, bf16[576,256]{1,0:T(8,128)(2,1)}, bf16[576,256]{1,0:T(8,128)(2,1)}) custom-call(s32[7]{0:T(128)} %stack.55.refs_0_, bf16[576,256]{1,0:T(8,128)(2,1)} %get-tuple-element.191.refs_1_, bf16[576,256]{1,0:T(8,128)(2,1)} %copy-done.46, bf16[576,256]{1,0:T(8,128)(2,1)} %copy-done.47, ...), custom_call_target="tpu_custom_call" | custom-call | flops 4831838208 | bytes 3158016 | tf_op jit(solution)/shard_map/pallas_call | solution.py:678
  356.2 8.6 %shard_map.187 = (bf16[2,192,1536]{2,1,0:T(8,128)(2,1)}, bf16[2,192,1536]{2,1,0:T(8,128)(2,1)}, bf16[2,768,384]{2,1,0:T(8,128)(2,1)}, bf16[2,768,384]{2,1,0:T(8,128)(2,1)}) custom-call(s32[7]{0:T(128)} %stack.55.refs_0_, bf16[256,3072]{1,0:T(8,128)(2,1)} %get-tuple-element.245.refs_1_, bf16[256,3072]{1,0:T(8,128)(2,1)} %copy-done.2, ...), custom_call_target="tpu_custom_call" | custom-call | flops 2415919104 | bytes 9437184 | tf_op jit(solution)/shard_map/pallas_call | solution.py:678
  370.3 8.4 %shard_map.189 = (f32[256,768]{1,0:T(8,128)}, bf16[2352,256]{1,0:T(8,128)(2,1)}) custom-call(s32[7]{0:T(128)} %stack.55.refs_0_, bf16[576,256]{1,0:T(8,128)(2,1)} %get-tuple-element.293.refs_2_.refs_1_, bf16[576,256]{1,0:T(8,128)(2,1)} %copy-done.53, bf16[576,256]{1,0:T(8,128)(2,1)} %copy-done.54, bf16[576,256]{1,0:T(8,128)(2,1)} %copy-done.55, ...), custom_call_target="tpu_custom_call" | custom-call | flops 1509949440 | bytes 10887168 | tf_op jit(solution)/shard_map/pallas_call | solution.py:678
  387.4 6.5 %shard_map.193 = (bf16[2,96,3200]{2,1,0:T(8,128)(2,1)}, bf16[2,96,3200]{2,1,0:T(8,128)(2,1)}) custom-call(s32[7]{0:T(128)} %stack.55.refs_0_, bf16[256,384]{1,0:T(8,128)(2,1)} %get-tuple-element.206.refs_5_.refs_1_, bf16[256,3072]{1,0:T(8,128)(2,1)} %copy-done.2, bf16[256,384]{1,0:T(8,128)(2,1)} %get-tuple-element.313.refs_3_, bf16[256,3072]{1,0:T(8,128)(2,1)} %copy-done.2, ...), custom_call_target="tpu_custom_call" | custom-call | flops 1207959552 | bytes 7618560 | tf_op jit(solution)/shard_map/pallas_call | solution.py:678
  399.1 14.9 %collective-permute-done.79.refs_4_ = bf16[2,192,1536]{2,1,0:T(8,128)(2,1)S(1)} collective-permute-done((bf16[2,192,1536]{2,1,0:T(8,128)(2,1)S(1)}, bf16[2,192,1536]{2,1,0:T(8,128)(2,1)S(1)}, u32[]{:S(2)}, u32[]{:S(2)}) %collective-permute-start.79) | collective-permute-done | bytes 1179680 | tf_op jit(solution)/shard_map/ppermute | solution.py:55
  423.1 8.5 %collective-permute-done.87.refs_2_ = bf16[192,1536]{1,0:T(8,128)(2,1)S(1)} collective-permute-done((bf16[192,1536]{1,0:T(8,128)(2,1)}, bf16[192,1536]{1,0:T(8,128)(2,1)S(1)}, u32[]{:S(2)}, u32[]{:S(2)}) %collective-permute-start.87) | collective-permute-done | bytes 589856 | tf_op jit(solution)/shard_map/ppermute | solution.py:55
  432.7 5.4 %shard_map.199 = (bf16[2,4,96,384]{3,2,1,0:T(8,128)(2,1)}, bf16[2,4,96,384]{3,2,1,0:T(8,128)(2,1)}, bf16[2,4,96,384]{3,2,1,0:T(8,128)(2,1)}, bf16[2,4,96,384]{3,2,1,0:T(8,128)(2,1)}) custom-call(s32[7]{0:T(128)} %stack.55.refs_0_, bf16[192,1536]{1,0:T(8,128)(2,1)} %get-tuple-element.330.refs_1_, bf16[192,1536]{1,0:T(8,128)(2,1)} %copy-done.66, ...), custom_call_target="tpu_custom_call" | custom-call | tf_op jit(solution)/shard_map/pallas_call | solution.py:678
  456.3 9.2 %collective-permute-done.82.refs_1_ = bf16[2,4,304,128]{3,2,1,0:T(8,128)(2,1)S(1)} collective-permute-done((bf16[2,4,304,128]{3,2,1,0:T(8,128)(2,1)}, bf16[2,4,304,128]{3,2,1,0:T(8,128)(2,1)S(1)}, u32[]{:S(2)}, u32[]{:S(2)}) %collective-permute-start.82) | collective-permute-done | bytes 622624 | tf_op jit(solution)/shard_map/ppermute | solution.py:55
  (495 shorter events, 282.5 us)
Async XLA Ops:
  25.8 15.2 %collective-permute-start.5 = (bf16[4,304,128]{2,1,0:T(8,128)(2,1)}, bf16[4,304,128]{2,1,0:T(8,128)(2,1)S(1)}, u32[]{:S(2)}, u32[]{:S(2)}) collective-permute-start(bf16[4,304,128]{2,1,0:T(8,128)(2,1)} %shard_map.146.refs_5_.refs_0_), channel_id=1, source_target_pairs={{0,2},{2,0},{4,6},{6,4},{8,14},{10,12},{12,10},{14,8},{16,18},{18,... | collective-permute-start | bytes 933896 | tf_op jit(solution)/shard_map/ppermute | solution.py:55
  43.6 16.0 %collective-permute-start.8 = (bf16[2,4,304,128]{3,2,1,0:T(8,128)(2,1)}, bf16[2,4,304,128]{3,2,1,0:T(8,128)(2,1)S(1)}, u32[]{:S(2)}, u32[]{:S(2)}) collective-permute-start(bf16[2,4,304,128]{3,2,1,0:T(8,128)(2,1)} %shard_map.148.refs_4_.refs_1_), channel_id=1, source_target_pairs={{0,6},{2,4},{4,2},{6,0},{8,10},{10,8},{12,14},{14,12},{16,22},{18,... | collective-permute-start | bytes 1867784 | tf_op jit(solution)/shard_map/ppermute | solution.py:55
  56.7 15.5 %collective-permute-start.13 = (bf16[2,4,96,384]{3,2,1,0:T(8,128)(2,1)}, bf16[2,4,96,384]{3,2,1,0:T(8,128)(2,1)S(1)}, u32[]{:S(2)}, u32[]{:S(2)}) collective-permute-start(bf16[2,4,96,384]{3,2,1,0:T(8,128)(2,1)} %get-tuple-element.181.refs_3_.refs_1_), channel_id=1, source_target_pairs={{0,96},{2,98},{4,100},{6,102},{8,40},{10,42},{12,44},{14,46},{16,1... | collective-permute-start | bytes 1769480 | tf_op jit(solution)/shard_map/ppermute | solution.py:55
  92.4 17.8 %collective-permute-start.28 = (bf16[2,192,1536]{2,1,0:T(8,128)(2,1)}, bf16[2,192,1536]{2,1,0:T(8,128)(2,1)}, u32[]{:S(2)}, u32[]{:S(2)}) collective-permute-start(bf16[2,192,1536]{2,1,0:T(8,128)(2,1)} %get-tuple-element.189.refs_1_), channel_id=1, source_target_pairs={{0,6},{2,4},{4,2},{6,0},{8,10},{10,8},{12,14},{14,12},{16,22},{18,... | collective-permute-start | bytes 3538952 | tf_op jit(solution)/shard_map/ppermute | solution.py:55
  94.0 17.7 %collective-permute-start.29 = (bf16[2,768,384]{2,1,0:T(8,128)(2,1)}, bf16[2,768,384]{2,1,0:T(8,128)(2,1)}, u32[]{:S(2)}, u32[]{:S(2)}) collective-permute-start(bf16[2,768,384]{2,1,0:T(8,128)(2,1)} %get-tuple-element.190.refs_2_), channel_id=1, source_target_pairs={{0,96},{2,98},{4,100},{6,102},{8,40},{10,42},{12,44},{14,46},{16,1... | collective-permute-start | bytes 3538952 | tf_op jit(solution)/shard_map/ppermute | solution.py:55
  109.3 15.9 %collective-permute-start.24 = (bf16[576,256]{1,0:T(8,128)(2,1)}, bf16[576,256]{1,0:T(8,128)(2,1)S(1)}, u32[]{:S(2)}, u32[]{:S(2)}) collective-permute-start(bf16[576,256]{1,0:T(8,128)(2,1)} %get-tuple-element.194), channel_id=1, source_target_pairs={{6,0},{0,2},{2,4},{4,6},{14,8},{8,10},{10,12},{12,14},{22,16},{16,... | collective-permute-start | bytes 884744 | tf_op jit(solution)/shard_map/ppermute | solution.py:45
  151.2 29.5 %collective-permute-start.35 = (bf16[96,3200]{1,0:T(8,128)(2,1)}, bf16[96,3200]{1,0:T(8,128)(2,1)S(1)}, u32[]{:S(2)}, u32[]{:S(2)}) collective-permute-start(bf16[96,3200]{1,0:T(8,128)(2,1)} %get-tuple-element.218.refs_3_.refs_11_.refs_15_), channel_id=1, source_target_pairs={{0,17},{2,19},{4,21},{6,23},{8,24},{10,26},{12,28},{14,30},{16,1},... | collective-permute-start | bytes 1843208 | tf_op jit(solution)/shard_map/ppermute | solution.py:55
  152.5 28.3 %collective-permute-start.36 = (bf16[96,3200]{1,0:T(8,128)(2,1)}, bf16[96,3200]{1,0:T(8,128)(2,1)S(1)}, u32[]{:S(2)}, u32[]{:S(2)}) collective-permute-start(bf16[96,3200]{1,0:T(8,128)(2,1)} %get-tuple-element.219.refs_4_.refs_12_.refs_16_), channel_id=1, source_target_pairs={{0,17},{2,19},{4,21},{6,23},{8,24},{10,26},{12,28},{14,30},{16,1},... | collective-permute-start | bytes 1843208 | tf_op jit(solution)/shard_map/ppermute | solution.py:55
  154.5 27.7 %collective-permute-start.37 = (bf16[96,3200]{1,0:T(8,128)(2,1)}, bf16[96,3200]{1,0:T(8,128)(2,1)S(1)}, u32[]{:S(2)}, u32[]{:S(2)}) collective-permute-start(bf16[96,3200]{1,0:T(8,128)(2,1)} %get-tuple-element.218.refs_3_.refs_11_.refs_15_), channel_id=1, source_target_pairs={{8,0},{10,2},{12,4},{14,6},{0,8},{2,10},{4,12},{6,14},{24,16},{26,... | collective-permute-start | bytes 1843208 | tf_op jit(solution)/shard_map/ppermute | solution.py:45
  157.6 38.2 %collective-permute-start.44 = (bf16[2,192,1536]{2,1,0:T(8,128)(2,1)}, bf16[2,192,1536]{2,1,0:T(8,128)(2,1)}, u32[]{:S(2)}, u32[]{:S(2)}) collective-permute-start(bf16[2,192,1536]{2,1,0:T(8,128)(2,1)} %get-tuple-element.232.refs_1_), channel_id=1, source_target_pairs={{0,6},{2,4},{4,2},{6,0},{8,10},{10,8},{12,14},{14,12},{16,22},{18,... | collective-permute-start | bytes 3538952 | tf_op jit(solution)/shard_map/ppermute | solution.py:55
  157.7 38.1 %collective-permute-start.45 = (bf16[2,768,384]{2,1,0:T(8,128)(2,1)}, bf16[2,768,384]{2,1,0:T(8,128)(2,1)}, u32[]{:S(2)}, u32[]{:S(2)}) collective-permute-start(bf16[2,768,384]{2,1,0:T(8,128)(2,1)} %get-tuple-element.233.refs_2_), channel_id=1, source_target_pairs={{0,96},{2,98},{4,100},{6,102},{8,40},{10,42},{12,44},{14,46},{16,1... | collective-permute-start | bytes 3538952 | tf_op jit(solution)/shard_map/ppermute | solution.py:55
  191.8 16.4 %collective-permute-start.41 = (bf16[576,256]{1,0:T(8,128)(2,1)}, bf16[576,256]{1,0:T(8,128)(2,1)S(1)}, u32[]{:S(2)}, u32[]{:S(2)}) collective-permute-start(bf16[576,256]{1,0:T(8,128)(2,1)} %get-tuple-element.223), channel_id=1, source_target_pairs={{2,0},{4,2},{6,4},{0,6},{10,8},{12,10},{14,12},{8,14},{18,16},{20,... | collective-permute-start | bytes 884744 | tf_op jit(solution)/shard_map/ppermute | solution.py:45
  194.8 16.7 %collective-permute-start.43 = (bf16[576,256]{1,0:T(8,128)(2,1)}, bf16[576,256]{1,0:T(8,128)(2,1)S(1)}, u32[]{:S(2)}, u32[]{:S(2)}) collective-permute-start(bf16[576,256]{1,0:T(8,128)(2,1)} %get-tuple-element.225), channel_id=1, source_target_pairs={{6,0},{0,2},{2,4},{4,6},{14,8},{8,10},{10,12},{12,14},{22,16},{16,... | collective-permute-start | bytes 884744 | tf_op jit(solution)/shard_map/ppermute | solution.py:45
  247.4 15.3 %collective-permute-start.53 = (bf16[192,256]{1,0:T(8,128)(2,1)}, bf16[192,256]{1,0:T(8,128)(2,1)S(1)}, u32[]{:S(2)}, u32[]{:S(2)}) collective-permute-start(bf16[192,256]{1,0:T(8,128)(2,1)} %get-tuple-element.247), channel_id=1, source_target_pairs={{2,0},{4,2},{6,4},{0,6},{10,8},{12,10},{14,12},{8,14},{18,16},{20,... | collective-permute-start | bytes 294920 | tf_op jit(solution)/shard_map/ppermute | solution.py:45
  263.4 18.2 %collective-permute-start.59 = (bf16[2,192,1536]{2,1,0:T(8,128)(2,1)}, bf16[2,192,1536]{2,1,0:T(8,128)(2,1)S(1)}, u32[]{:S(2)}, u32[]{:S(2)}) collective-permute-start(bf16[2,192,1536]{2,1,0:T(8,128)(2,1)} %get-tuple-element.263), channel_id=1, source_target_pairs={{0,6},{2,4},{4,2},{6,0},{8,10},{10,8},{12,14},{14,12},{16,22},{18,... | collective-permute-start | bytes 3538952 | tf_op jit(solution)/shard_map/ppermute | solution.py:55
  264.0 17.6 %collective-permute-start.60 = (bf16[2,768,384]{2,1,0:T(8,128)(2,1)}, bf16[2,768,384]{2,1,0:T(8,128)(2,1)S(1)}, u32[]{:S(2)}, u32[]{:S(2)}) collective-permute-start(bf16[2,768,384]{2,1,0:T(8,128)(2,1)} %get-tuple-element.264), channel_id=1, source_target_pairs={{0,96},{2,98},{4,100},{6,102},{8,40},{10,42},{12,44},{14,46},{16,1... | collective-permute-start | bytes 3538952 | tf_op jit(solution)/shard_map/ppermute | solution.py:55
  330.6 18.2 %collective-permute-start.68 = (bf16[2,96,3200]{2,1,0:T(8,128)(2,1)}, bf16[2,96,3200]{2,1,0:T(8,128)(2,1)S(1)}, u32[]{:S(2)}, u32[]{:S(2)}) collective-permute-start(bf16[2,96,3200]{2,1,0:T(8,128)(2,1)} %get-tuple-element.290), channel_id=1, source_target_pairs={{0,17},{2,19},{4,21},{6,23},{8,24},{10,26},{12,28},{14,30},{16,1},... | collective-permute-start | bytes 3686408 | tf_op jit(solution)/shard_map/ppermute | solution.py:55
  350.7 16.9 %collective-permute-start.71 = (bf16[576,256]{1,0:T(8,128)(2,1)S(1)}, bf16[576,256]{1,0:T(8,128)(2,1)S(1)}, u32[]{:S(2)}, u32[]{:S(2)}) collective-permute-start(bf16[576,256]{1,0:T(8,128)(2,1)S(1)} %copy-done.80), channel_id=1, source_target_pairs={{2,0},{4,2},{6,4},{0,6},{10,8},{12,10},{14,12},{8,14},{18,16},{20,... | collective-permute-start | bytes 884744 | tf_op jit(solution)/shard_map/ppermute | solution.py:45
  395.3 19.7 %collective-permute-start.78 = (bf16[2,96,3200]{2,1,0:T(8,128)(2,1)}, bf16[2,96,3200]{2,1,0:T(8,128)(2,1)S(1)}, u32[]{:S(2)}, u32[]{:S(2)}) collective-permute-start(bf16[2,96,3200]{2,1,0:T(8,128)(2,1)} %shard_map.194), channel_id=1, source_target_pairs={{0,17},{2,19},{4,21},{6,23},{8,24},{10,26},{12,28},{14,30},{16,1},... | collective-permute-start | bytes 3686408 | tf_op jit(solution)/shard_map/ppermute | solution.py:55
  396.6 17.4 %collective-permute-start.79 = (bf16[2,192,1536]{2,1,0:T(8,128)(2,1)S(1)}, bf16[2,192,1536]{2,1,0:T(8,128)(2,1)S(1)}, u32[]{:S(2)}, u32[]{:S(2)}) collective-permute-start(bf16[2,192,1536]{2,1,0:T(8,128)(2,1)S(1)} %copy-done.51), channel_id=1, source_target_pairs={{0,6},{2,4},{4,2},{6,0},{8,10},{10,8},{12,14},{14,12},{16,22},{18,... | collective-permute-start | bytes 3538952 | tf_op jit(solution)/shard_map/ppermute | solution.py:55
  397.6 17.4 %collective-permute-start.80 = (bf16[2,768,384]{2,1,0:T(8,128)(2,1)S(1)}, bf16[2,768,384]{2,1,0:T(8,128)(2,1)S(1)}, u32[]{:S(2)}, u32[]{:S(2)}) collective-permute-start(bf16[2,768,384]{2,1,0:T(8,128)(2,1)S(1)} %copy-done.52), channel_id=1, source_target_pairs={{0,96},{2,98},{4,100},{6,102},{8,40},{10,42},{12,44},{14,46},{16,1... | collective-permute-start | bytes 3538952 | tf_op jit(solution)/shard_map/ppermute | solution.py:55
  422.0 20.2 %collective-permute-start.81 = (bf16[96,3200]{1,0:T(8,128)(2,1)}, bf16[96,3200]{1,0:T(8,128)(2,1)S(1)}, u32[]{:S(2)}, u32[]{:S(2)}) collective-permute-start(bf16[96,3200]{1,0:T(8,128)(2,1)} %get-tuple-element.321), channel_id=1, source_target_pairs={{0,16},{2,18},{4,20},{6,22},{8,25},{10,27},{12,29},{14,31},{16,0},... | collective-permute-start | bytes 1843208 | tf_op jit(solution)/shard_map/ppermute | solution.py:55
  448.2 17.3 %collective-permute-start.82 = (bf16[2,4,304,128]{3,2,1,0:T(8,128)(2,1)}, bf16[2,4,304,128]{3,2,1,0:T(8,128)(2,1)S(1)}, u32[]{:S(2)}, u32[]{:S(2)}) collective-permute-start(bf16[2,4,304,128]{3,2,1,0:T(8,128)(2,1)} %get-tuple-element.323), channel_id=1, source_target_pairs={{0,6},{2,4},{4,2},{6,0},{8,10},{10,8},{12,14},{14,12},{16,22},{18,... | collective-permute-start | bytes 1867784 | tf_op jit(solution)/shard_map/ppermute | solution.py:55
  454.0 15.3 %collective-permute-start.91 = (bf16[4,96,384]{2,1,0:T(8,128)(2,1)}, bf16[4,96,384]{2,1,0:T(8,128)(2,1)S(1)}, u32[]{:S(2)}, u32[]{:S(2)}) collective-permute-start(bf16[4,96,384]{2,1,0:T(8,128)(2,1)} %get-tuple-element.340), channel_id=1, source_target_pairs={{0,32},{2,34},{4,36},{6,38},{8,104},{10,106},{12,108},{14,110},{16... | collective-permute-start | bytes 884744 | tf_op jit(solution)/shard_map/ppermute | solution.py:55
  (179 other events, 1005.0 us)

commit v5 on v4

--- a/solution.py
+++ b/solution.py
@@ -409,6 +409,22 @@
         send[0, :, columns] = blocks[1]
 
 
+def store_four(near, out_refs, columns, blocks):
+    own, first, other, opposite = out_refs
+    own[:, columns] = blocks[0]
+    opposite[:, columns] = blocks[3]
+
+    @pl.when(near == 1)
+    def _():
+        first[:, columns] = blocks[1]
+        other[:, columns] = blocks[2]
+
+    @pl.when(near == 2)
+    def _():
+        first[:, columns] = blocks[2]
+        other[:, columns] = blocks[1]
+
+
 def mlp_grad_kernel(
     place_ref, a2_0, a2_1, act_0, act_1, dpre_0, dpre_1, gb_0, gb_1,
     first_mine, first_send, second_mine, second_send,
@@ -471,7 +487,7 @@
 
 
 def attn_grad_kernel(
-    place_ref, a1p_0, a1p_1, op_0, op_1, g1b_0, g1b_1, dqkv_0, dqkv_1, pa_ref, mine, send
+    place_ref, a1p_0, a1p_1, op_0, op_1, g1b_0, g1b_1, dqkv_0, dqkv_1, pa_ref, *out_refs
 ):
     near = place_ref[NEAR_Y]
     norms = jnp.zeros((8, D), F32)
@@ -494,7 +510,7 @@
         else:
             value = norms
         blocks = [value[96 * k : 96 * k + 96] for k in range(4)]
-        store_blocks(near, mine, send, columns, blocks)
+        store_four(near, out_refs, columns, blocks)
 
 
 def join_kernel(*refs):
@@ -629,6 +645,10 @@
         out[...] = total_of(keep[k], came[k])
 
 
+def sum_kernel(first, second, out):
+    out[...] = total_of(first[...], second[...])
+
+
 def nothing_kernel(*refs):
     pass
 
@@ -781,8 +801,13 @@
     return list(out[0::2]), list(out[1::2])
 
 
-def total(keep, came):
-    return (keep.astype(F32) + came.astype(F32)).astype(BF)
+def summed(first, second, done=()):
+    (out,) = run_kernel(sum_kernel, [first, second], [like(first)], scalars=False, done=done)
+    return out
+
+
+def total(*terms):
+    return sum(v.astype(F32) for v in terms).astype(BF)
 
 
 def gradients_home(place, a_layers, b_layers, c_layers):
@@ -1020,7 +1045,7 @@
                 dqkv[1],
                 pa,
             ],
-            [shaped(2, 96, ROW_A)] * 2,
+            [shaped(96, ROW_A)] * 4,
             flops=4 * UNIT,
             done=done,
         )
@@ -1055,37 +1080,41 @@
     _, op_keep0, act_keep0 = records[0][6:]
     a1p_keep0 = records[0][1]
     grad_mixed = exchange_four(pieces)
-    a1_mine, a1_send = attn_gradients(forward, back, a1p_keep, op_keep, dqkv)
-    a1_send, b1_send, c1_send = after([a1_send, b1_send, c1_send], grad_mixed[1:])
-    a1_came = swap(a1_send, "y", -1)
+    a1_own, a1_near, a1_far, a1_last = attn_gradients(forward, back, a1p_keep, op_keep, dqkv)
+    a1_far, a1_last, b1_send, c1_send = after(
+        [a1_far, a1_last, b1_send, c1_send], grad_mixed[1:]
+    )
+    a1_far, a1_last = swap(a1_far, "y", -1), swap(a1_last, "y", -1)
     b1_came, c1_came = swap(b1_send, "x", 1), swap(c1_send, "z", 1)
-    pieces = attend_back(0, grad_mixed, [a1_mine])
-    pieces = after(pieces, [a1_came, b1_came, c1_came])
+    pieces = attend_back(0, grad_mixed, [a1_own])
+    pieces = after(pieces, [a1_far, a1_last, b1_came, c1_came])
     dpre_keep0, back_send0 = after([dpre_keep0, back_send0], pieces[:1])
     back0 = back_send0, with_core(back_send0)
     grad_pieces = exchange_four(pieces)
     b0_mine, b0_send, c0_mine, c0_send = mlp_gradients(forward0, back0, act_keep0, dpre_keep0)
-    (a1_keep,), (a1_send,) = halved([a1_mine], [a1_came], [b0_mine])
-    a1_send, b0_send, c0_send = after([a1_send, b0_send, c0_send], grad_pieces[1:])
-    a1_came = swap(a1_send, "y", 1)
+    a1_near = summed(a1_near, a1_last, [b0_mine])
+    a1_near, b0_send, c0_send = after([a1_near, b0_send, c0_send], grad_pieces[1:])
+    a1_came = swap(a1_near, "y", 1)
     b0_came, c0_came = swap(b0_send, "x", -1), swap(c0_send, "z", -1)
-    grad, dqkv = qkv_back(0, grad_pieces, g1, norm2, [b0_mine, a1_keep])
+    grad, dqkv = qkv_back(0, grad_pieces, g1, norm2, [b0_mine, a1_near])
     grad, dqkv = after([grad, dqkv], [a1_came])
     dqkv = dqkv, with_core(dqkv)
     grad_own, grad_far = leave(grad, [], BF)
-    a0_mine, a0_send = attn_gradients(
+    a0_own, a0_near, a0_far, a0_last = attn_gradients(
         forward0, back0, a1p_keep0, op_keep0, dqkv
     )
-    (a0_send,) = after([a0_send], [grad_far])
-    a0_came = swap(a0_send, "y", -1)
-    (a0_keep, b0_keep, c0_keep), (a0_send, b0_send, c0_send) = halved(
-        [a0_mine, b0_mine, c0_mine], [a0_came, b0_came, c0_came]
-    )
-    a0_came = swap(a0_send, "y", 1)
+    (a0_last,) = after([a0_last], [grad_far])
+    a0_last = swap(a0_last, "y", -1)
+    a0_near = summed(a0_near, a0_last)
+    (a0_far,) = after([a0_far], [a0_near])
+    a0_came, a0_far = swap(a0_near, "y", 1), swap(a0_far, "y", -1)
+    (b0_keep, c0_keep), (b0_send, c0_send) = halved(
+        [b0_mine, c0_mine], [b0_came, c0_came], [a0_near]
+    )
     b0_came, c0_came = swap(b0_send, "x", 1), swap(c0_send, "z", 1)
     weight_grads = gradients_home(
         place,
-        [total(a0_keep, a0_came), total(a1_keep, a1_came)],
+        [total(a0_own, a0_far, a0_came), total(a1_own, a1_far, a1_came)],
         [[b0_keep, b0_came], [b1_keep, b1_came]],
         [[c0_keep, c0_came], [c1_keep, c1_came]],
     )

time: 496 us -> 492 us (level)
  waiting for transfers between devices: 119 us -> 110 us
    ppermute x44 -> x46, waiting for transfers between devices: 64 us -> 54.6 us  [swap(): return lax.ppermute(value, AXES, pairs)]
    ppermute x44 -> x46, starting transfers between devices: 62.1 us -> 64.5 us  [swap(): return lax.ppermute(value, AXES, pairs)]
    pallas_call x36 -> x37, Pallas kernels: 194 us -> 195 us  [run_kernel(): pl.pallas_call(whole, grid=(1,), out_shape=tuple(outs), in_specs=specs +...]
    unnamed x218 -> x214, local copies, waits for them, and re-layouts: 39.1 us -> 38.8 us
  transfers between devices with their start and end apart: 96 -> 98, of which waited for: 44 -> 42; matrix products, arithmetic and copies ran while one was open for 6% -> 7% of each run, Pallas kernels for 31% -> 32%
where the time goes in v5:
time: 492 us; the launch traced here: 486 us
  Pallas kernels  195 us (40%)
  waiting for transfers between devices  110 us (22%)
  starting transfers between devices  108 us (22%)
  local copies, waits for them, and re-layouts  56.2 us (11%)
  other arithmetic  7.92 us (2%)
  matrix products  6.93 us (1%)
    pallas_call x37, Pallas kernels, run_kernel(): pl.pallas_call(whole, grid=(1,), out_shape=tuple(outs), in_specs=specs +...  195 us
    ppermute x46, starting transfers between devices, swap(): return lax.ppermute(value, AXES, pairs)  64.5 us
    ppermute x52, waiting for transfers between devices, fetch(): return lax.ppermute(value, AXES, pairs)  55.3 us
    ppermute x46, waiting for transfers between devices, swap(): return lax.ppermute(value, AXES, pairs)  54.6 us
    ppermute x52, starting transfers between devices, fetch(): return lax.ppermute(value, AXES, pairs)  43.6 us
    unnamed x214, local copies, waits for them, and re-layouts  38.8 us
  transfers between devices with their start and end apart: 98, of which 42 were waited for; matrix products, arithmetic and copies ran while one was open for 7% of the time, Pallas kernels for 32%

profile of v5, /device:TPU:0, one launch (start us, length us, event | category | flops | bytes accessed | tf_op | source)
XLA Modules:
  0.0 486.1 jit_solution(6803732261481473711)
XLA Ops:
  100.7 6.0 %shard_map.156 = (bf16[256,384]{1,0:T(8,128)(2,1)}, bf16[256,384]{1,0:T(8,128)(2,1)}, f32[8,768]{1,0:T(8,128)}, bf16[576,256]{1,0:T(8,128)(2,1)}, bf16[576,256]{...) custom-call(s32[7]{0:T(128)} %stack.55.refs_0_, f32[256,768]{1,0:T(8,128)} %fusion.4.refs_5_.refs_1_, ...), custom_call_target="tpu_custom_call" | custom-call | flops 1207959552 | bytes 8478720 | tf_op jit(solution)/shard_map/pallas_call | solution.py:698
  111.8 5.2 %shard_map.160 = (bf16[4,192,1536]{2,1,0:T(8,128)(2,1)}, bf16[4,768,384]{2,1,0:T(8,128)(2,1)}) custom-call(s32[7]{0:T(128)} %stack.55.refs_0_, bf16[2,192,1536]{2,1,0:T(8,128)(2,1)} %get-tuple-element.190.refs_1_, bf16[2,768,384]{2,1,0:T(8,128)(2,1)} %get-tuple-element.191.refs_2_, bf16[2,192,1536]{2,1,0:T(8,128)(2,1)} %collective-permute-done.28.refs_3_, ...), custom_call_target="tpu_custom_call" | custom-call | tf_op jit(solution)/shard_map/pallas_call | solution.py:698
  120.1 5.1 %collective-permute-done.24.refs_4_.refs_5_ = bf16[576,256]{1,0:T(8,128)(2,1)S(1)} collective-permute-done((bf16[576,256]{1,0:T(8,128)(2,1)}, bf16[576,256]{1,0:T(8,128)(2,1)S(1)}, u32[]{:S(2)}, u32[]{:S(2)}) %collective-permute-start.24) | collective-permute-done | bytes 294944 | tf_op jit(solution)/shard_map/ppermute | solution.py:45
  126.6 6.3 %shard_map.157 = (bf16[192,256]{1,0:T(8,128)(2,1)}, bf16[192,256]{1,0:T(8,128)(2,1)}, bf16[192,256]{1,0:T(8,128)(2,1)}, bf16[192,256]{1,0:T(8,128)(2,1)}, f32[3,1024]{1,0:T(4,128)}) custom-call(s32[7]{0:T(128)} %stack.55.refs_0_, bf16[576,256]{1,0:T(8,128)(2,1)} %get-tuple-element.192.refs_1_, bf16[576,256]{1,0:T(8,128)(2,1)} %copy-done.44, ...), custom_call_target="tpu_custom_call" | custom-call | flops 1610612736 | bytes 1585152 | tf_op jit(solution)/shard_map/pallas_call | solution.py:698
  157.8 12.0 %collective-permute-start.45 = (bf16[2,768,384]{2,1,0:T(8,128)(2,1)}, bf16[2,768,384]{2,1,0:T(8,128)(2,1)}, u32[]{:S(2)}, u32[]{:S(2)}) collective-permute-start(bf16[2,768,384]{2,1,0:T(8,128)(2,1)} %get-tuple-element.234.refs_2_), channel_id=1, source_target_pairs={{0,96},{2,98},{4,100},{6,102},{8,40},{10,42},{12,44},{14,46},{16,1... | collective-permute-start | bytes 3538952 | tf_op jit(solution)/shard_map/ppermute | solution.py:55
  169.8 10.9 %shard_map.163 = (f32[256,768]{1,0:T(8,128)}, f32[256,768]{1,0:T(8,128)}, bf16[256,3072]{1,0:T(8,128)(2,1)}, bf16[256,3072]{1,0:T(8,128)(2,1)}, bf16[256,384]{1,0:T(8,128)(2,1)}, /*index=5*/bf16[256,1536]{1,0:T(8,128)(2,1)}) custom-call(s32[7]{0:T(128)} %stack.55.refs_0_, f32[256,768]{1,0:T(8,128)} %fusion.4.refs_5_.refs_1_, ...), custom_call_target="tpu_custom_call" | custom-call | flops 3321888768 | bytes 23814144 | tf_op jit(solution)/shard_map/pallas_call | solution.py:698
  185.8 6.1 %shard_map.166 = (bf16[256,384]{1,0:T(8,128)(2,1)}, bf16[256,384]{1,0:T(8,128)(2,1)}, f32[8,768]{1,0:T(8,128)}, bf16[576,256]{1,0:T(8,128)(2,1)}, bf16[576,256]{...) custom-call(s32[7]{0:T(128)} %stack.55.refs_0_, ...), custom_call_target="tpu_custom_call" | custom-call | flops 1207959552 | bytes 8478720 | tf_op jit(solution)/shard_map/pallas_call | solution.py:698
  195.7 5.1 %shard_map.170 = (bf16[4,192,1536]{2,1,0:T(8,128)(2,1)}, bf16[4,768,384]{2,1,0:T(8,128)(2,1)}) custom-call(s32[7]{0:T(128)} %stack.55.refs_0_, bf16[2,192,1536]{2,1,0:T(8,128)(2,1)} %get-tuple-element.233.refs_1_, bf16[2,768,384]{2,1,0:T(8,128)(2,1)} %get-tuple-element.234.refs_2_, bf16[2,192,1536]{2,1,0:T(8,128)(2,1)} %collective-permute-done.44.refs_3_, ...), custom_call_target="tpu_custom_call" | custom-call | tf_op jit(solution)/shard_map/pallas_call | solution.py:698
  200.9 7.3 %collective-permute-done.41.refs_2_.refs_1_ = bf16[576,256]{1,0:T(8,128)(2,1)S(1)} collective-permute-done((bf16[576,256]{1,0:T(8,128)(2,1)}, bf16[576,256]{1,0:T(8,128)(2,1)S(1)}, u32[]{:S(2)}, u32[]{:S(2)}) %collective-permute-start.41) | collective-permute-done | bytes 294944 | tf_op jit(solution)/shard_map/ppermute | solution.py:45
  215.8 6.3 %shard_map.167 = (bf16[192,256]{1,0:T(8,128)(2,1)}, bf16[192,256]{1,0:T(8,128)(2,1)}, bf16[192,256]{1,0:T(8,128)(2,1)}, bf16[192,256]{1,0:T(8,128)(2,1)}, f32[3,1024]{1,0:T(4,128)}) custom-call(s32[7]{0:T(128)} %stack.55.refs_0_, bf16[576,256]{1,0:T(8,128)(2,1)} %get-tuple-element.223.refs_1_, bf16[576,256]{1,0:T(8,128)(2,1)} %copy-done.41, ...), custom_call_target="tpu_custom_call" | custom-call | flops 1610612736 | bytes 1585152 | tf_op jit(solution)/shard_map/pallas_call | solution.py:698
  232.6 14.1 %shard_map.174 = (f32[256,768]{1,0:T(8,128)}, bf16[256,3072]{1,0:T(8,128)(2,1)}, bf16[256,384]{1,0:T(8,128)(2,1)}, bf16[256,1536]{1,0:T(8,128)(2,1)}, f32[256,76...) custom-call(s32[7]{0:T(128)} %stack.55.refs_0_, ...), custom_call_target="tpu_custom_call" | custom-call | flops 6643777536 | bytes 25804800 | tf_op jit(solution)/shard_map/pallas_call | solution.py:698
  253.9 8.7 %shard_map.176 = (bf16[2,192,1536]{2,1,0:T(8,128)(2,1)}, bf16[2,192,1536]{2,1,0:T(8,128)(2,1)}, bf16[2,768,384]{2,1,0:T(8,128)(2,1)}, bf16[2,768,384]{2,1,0:T(8,128)(2,1)}) custom-call(s32[7]{0:T(128)} %stack.55.refs_0_, bf16[256,3072]{1,0:T(8,128)(2,1)} %get-tuple-element.253.refs_1_, bf16[256,3072]{1,0:T(8,128)(2,1)} %copy-done.3, ...), custom_call_target="tpu_custom_call" | custom-call | flops 2415919104 | bytes 9437184 | tf_op jit(solution)/shard_map/pallas_call | solution.py:698
  271.4 10.2 %shard_map.177 = (bf16[576,256]{1,0:T(8,128)(2,1)}, bf16[576,256]{1,0:T(8,128)(2,1)}, bf16[576,256]{1,0:T(8,128)(2,1)}, bf16[576,256]{1,0:T(8,128)(2,1)}) custom-call(s32[7]{0:T(128)} %stack.55.refs_0_, bf16[576,256]{1,0:T(8,128)(2,1)} %get-tuple-element.223.refs_1_, bf16[576,256]{1,0:T(8,128)(2,1)} %copy-done.41, bf16[576,256]{1,0:T(8,128)(2,1)} %copy-done.42, ...), custom_call_target="tpu_custom_call" | custom-call | flops 4831838208 | bytes 3158016 | tf_op jit(solution)/shard_map/pallas_call | solution.py:698
  290.9 5.8 %collective-permute-done.61.refs_2_ = bf16[576,256]{1,0:T(8,128)(2,1)S(1)} collective-permute-done((bf16[576,256]{1,0:T(8,128)(2,1)}, bf16[576,256]{1,0:T(8,128)(2,1)S(1)}, u32[]{:S(2)}, u32[]{:S(2)}) %collective-permute-start.61) | collective-permute-done | bytes 294944 | tf_op jit(solution)/shard_map/ppermute | solution.py:45
  299.7 18.9 %shard_map.181 = (bf16[2352,256]{1,0:T(8,128)(2,1)}, f32[256,768]{1,0:T(8,128)}, bf16[256,3072]{1,0:T(8,128)(2,1)}, bf16[256,1536]{1,0:T(8,128)(2,1)}, f32[8,768...) custom-call(s32[7]{0:T(128)} %stack.55.refs_0_, ...), custom_call_target="tpu_custom_call" | custom-call | flops 4831838208 | bytes 32759808 | tf_op jit(solution)/shard_map/pallas_call | solution.py:698
  323.2 6.6 %shard_map.182 = (bf16[96,3200]{1,0:T(8,128)(2,1)}, bf16[96,3200]{1,0:T(8,128)(2,1)}, bf16[96,3200]{1,0:T(8,128)(2,1)}, bf16[96,3200]{1,0:T(8,128)(2,1)}) custom-call(s32[7]{0:T(128)} %stack.55.refs_0_, bf16[256,384]{1,0:T(8,128)(2,1)} %get-tuple-element.235.refs_5_.refs_1_, bf16[256,3072]{1,0:T(8,128)(2,1)} %copy-done.3, ...), custom_call_target="tpu_custom_call" | custom-call | flops 1207959552 | bytes 7618560 | tf_op jit(solution)/shard_map/pallas_call | solution.py:698
  335.9 10.2 %shard_map.183 = (bf16[576,256]{1,0:T(8,128)(2,1)}, bf16[576,256]{1,0:T(8,128)(2,1)}, bf16[576,256]{1,0:T(8,128)(2,1)}, bf16[576,256]{1,0:T(8,128)(2,1)}) custom-call(s32[7]{0:T(128)} %stack.55.refs_0_, bf16[576,256]{1,0:T(8,128)(2,1)} %get-tuple-element.192.refs_1_, bf16[576,256]{1,0:T(8,128)(2,1)} %copy-done.44, bf16[576,256]{1,0:T(8,128)(2,1)} %copy-done.45, ...), custom_call_target="tpu_custom_call" | custom-call | flops 4831838208 | bytes 3158016 | tf_op jit(solution)/shard_map/pallas_call | solution.py:698
  355.8 8.7 %shard_map.187 = (bf16[2,192,1536]{2,1,0:T(8,128)(2,1)}, bf16[2,192,1536]{2,1,0:T(8,128)(2,1)}, bf16[2,768,384]{2,1,0:T(8,128)(2,1)}, bf16[2,768,384]{2,1,0:T(8,128)(2,1)}) custom-call(s32[7]{0:T(128)} %stack.55.refs_0_, bf16[256,3072]{1,0:T(8,128)(2,1)} %get-tuple-element.246.refs_1_, bf16[256,3072]{1,0:T(8,128)(2,1)} %copy-done.2, ...), custom_call_target="tpu_custom_call" | custom-call | flops 2415919104 | bytes 9437184 | tf_op jit(solution)/shard_map/pallas_call | solution.py:698
  370.0 8.4 %shard_map.190 = (f32[256,768]{1,0:T(8,128)}, bf16[2352,256]{1,0:T(8,128)(2,1)}) custom-call(s32[7]{0:T(128)} %stack.55.refs_0_, bf16[576,256]{1,0:T(8,128)(2,1)} %get-tuple-element.296.refs_2_.refs_1_, bf16[576,256]{1,0:T(8,128)(2,1)} %copy-done.50, bf16[576,256]{1,0:T(8,128)(2,1)} %copy-done.51, bf16[576,256]{1,0:T(8,128)(2,1)} %copy-done.52, ...), custom_call_target="tpu_custom_call" | custom-call | flops 1509949440 | bytes 10887168 | tf_op jit(solution)/shard_map/pallas_call | solution.py:698
  389.6 6.6 %shard_map.193 = (bf16[96,3200]{1,0:T(8,128)(2,1)}, bf16[96,3200]{1,0:T(8,128)(2,1)}, bf16[96,3200]{1,0:T(8,128)(2,1)}, bf16[96,3200]{1,0:T(8,128)(2,1)}) custom-call(s32[7]{0:T(128)} %stack.55.refs_0_, bf16[256,384]{1,0:T(8,128)(2,1)} %get-tuple-element.207.refs_5_.refs_1_, bf16[256,3072]{1,0:T(8,128)(2,1)} %copy-done.2, ...), custom_call_target="tpu_custom_call" | custom-call | flops 1207959552 | bytes 7618560 | tf_op jit(solution)/shard_map/pallas_call | solution.py:698
  398.7 9.7 %collective-permute-done.79.refs_1_ = bf16[96,3200]{1,0:T(8,128)(2,1)S(1)} collective-permute-done((bf16[96,3200]{1,0:T(8,128)(2,1)}, bf16[96,3200]{1,0:T(8,128)(2,1)S(1)}, u32[]{:S(2)}, u32[]{:S(2)}) %collective-permute-start.79) | collective-permute-done | bytes 614432 | tf_op jit(solution)/shard_map/ppermute | solution.py:55
  419.8 7.1 %collective-permute-done.89.refs_2_ = bf16[192,1536]{1,0:T(8,128)(2,1)} collective-permute-done((bf16[192,1536]{1,0:T(8,128)(2,1)}, bf16[192,1536]{1,0:T(8,128)(2,1)}, u32[]{:S(2)}, u32[]{:S(2)}) %collective-permute-start.89) | collective-permute-done | bytes 589856 | tf_op jit(solution)/shard_map/ppermute | solution.py:55
  427.4 5.4 %shard_map.201 = (bf16[2,4,96,384]{3,2,1,0:T(8,128)(2,1)}, bf16[2,4,96,384]{3,2,1,0:T(8,128)(2,1)}, bf16[2,4,96,384]{3,2,1,0:T(8,128)(2,1)}, bf16[2,4,96,384]{3,2,1,0:T(8,128)(2,1)}) custom-call(s32[7]{0:T(128)} %stack.55.refs_0_, bf16[192,1536]{1,0:T(8,128)(2,1)} %get-tuple-element.332.refs_1_, bf16[192,1536]{1,0:T(8,128)(2,1)} %collective-permute-done.89.refs_2_, ...), custom_call_target="tpu_custom_call" | custom-call | tf_op jit(solution)/shard_map/pallas_call | solution.py:698
  450.1 11.0 %collective-permute-done.82.refs_1_ = bf16[2,4,304,128]{3,2,1,0:T(8,128)(2,1)S(1)} collective-permute-done((bf16[2,4,304,128]{3,2,1,0:T(8,128)(2,1)}, bf16[2,4,304,128]{3,2,1,0:T(8,128)(2,1)S(1)}, u32[]{:S(2)}, u32[]{:S(2)}) %collective-permute-start.82) | collective-permute-done | bytes 622624 | tf_op jit(solution)/shard_map/ppermute | solution.py:55
  (497 shorter events, 282.3 us)
Async XLA Ops:
  43.8 15.8 %collective-permute-start.8 = (bf16[2,4,304,128]{3,2,1,0:T(8,128)(2,1)}, bf16[2,4,304,128]{3,2,1,0:T(8,128)(2,1)S(1)}, u32[]{:S(2)}, u32[]{:S(2)}) collective-permute-start(bf16[2,4,304,128]{3,2,1,0:T(8,128)(2,1)} %shard_map.148.refs_4_.refs_1_), channel_id=1, source_target_pairs={{0,6},{2,4},{4,2},{6,0},{8,10},{10,8},{12,14},{14,12},{16,22},{18,... | collective-permute-start | bytes 1867784 | tf_op jit(solution)/shard_map/ppermute | solution.py:55
  56.8 15.4 %collective-permute-start.13 = (bf16[2,4,96,384]{3,2,1,0:T(8,128)(2,1)}, bf16[2,4,96,384]{3,2,1,0:T(8,128)(2,1)S(1)}, u32[]{:S(2)}, u32[]{:S(2)}) collective-permute-start(bf16[2,4,96,384]{3,2,1,0:T(8,128)(2,1)} %get-tuple-element.182.refs_3_.refs_1_), channel_id=1, source_target_pairs={{0,96},{2,98},{4,100},{6,102},{8,40},{10,42},{12,44},{14,46},{16,1... | collective-permute-start | bytes 1769480 | tf_op jit(solution)/shard_map/ppermute | solution.py:55
  92.4 17.8 %collective-permute-start.28 = (bf16[2,192,1536]{2,1,0:T(8,128)(2,1)}, bf16[2,192,1536]{2,1,0:T(8,128)(2,1)}, u32[]{:S(2)}, u32[]{:S(2)}) collective-permute-start(bf16[2,192,1536]{2,1,0:T(8,128)(2,1)} %get-tuple-element.190.refs_1_), channel_id=1, source_target_pairs={{0,6},{2,4},{4,2},{6,0},{8,10},{10,8},{12,14},{14,12},{16,22},{18,... | collective-permute-start | bytes 3538952 | tf_op jit(solution)/shard_map/ppermute | solution.py:55
  94.1 17.7 %collective-permute-start.29 = (bf16[2,768,384]{2,1,0:T(8,128)(2,1)}, bf16[2,768,384]{2,1,0:T(8,128)(2,1)}, u32[]{:S(2)}, u32[]{:S(2)}) collective-permute-start(bf16[2,768,384]{2,1,0:T(8,128)(2,1)} %get-tuple-element.191.refs_2_), channel_id=1, source_target_pairs={{0,96},{2,98},{4,100},{6,102},{8,40},{10,42},{12,44},{14,46},{16,1... | collective-permute-start | bytes 3538952 | tf_op jit(solution)/shard_map/ppermute | solution.py:55
  109.3 15.9 %collective-permute-start.24 = (bf16[576,256]{1,0:T(8,128)(2,1)}, bf16[576,256]{1,0:T(8,128)(2,1)S(1)}, u32[]{:S(2)}, u32[]{:S(2)}) collective-permute-start(bf16[576,256]{1,0:T(8,128)(2,1)} %get-tuple-element.195), channel_id=1, source_target_pairs={{6,0},{0,2},{2,4},{4,6},{14,8},{8,10},{10,12},{12,14},{22,16},{16,... | collective-permute-start | bytes 884744 | tf_op jit(solution)/shard_map/ppermute | solution.py:45
  151.3 29.4 %collective-permute-start.35 = (bf16[96,3200]{1,0:T(8,128)(2,1)}, bf16[96,3200]{1,0:T(8,128)(2,1)S(1)}, u32[]{:S(2)}, u32[]{:S(2)}) collective-permute-start(bf16[96,3200]{1,0:T(8,128)(2,1)} %get-tuple-element.219.refs_3_.refs_11_.refs_15_), channel_id=1, source_target_pairs={{0,17},{2,19},{4,21},{6,23},{8,24},{10,26},{12,28},{14,30},{16,1},... | collective-permute-start | bytes 1843208 | tf_op jit(solution)/shard_map/ppermute | solution.py:55
  152.6 28.2 %collective-permute-start.36 = (bf16[96,3200]{1,0:T(8,128)(2,1)}, bf16[96,3200]{1,0:T(8,128)(2,1)S(1)}, u32[]{:S(2)}, u32[]{:S(2)}) collective-permute-start(bf16[96,3200]{1,0:T(8,128)(2,1)} %get-tuple-element.220.refs_4_.refs_12_.refs_16_), channel_id=1, source_target_pairs={{0,17},{2,19},{4,21},{6,23},{8,24},{10,26},{12,28},{14,30},{16,1},... | collective-permute-start | bytes 1843208 | tf_op jit(solution)/shard_map/ppermute | solution.py:55
  154.5 27.6 %collective-permute-start.37 = (bf16[96,3200]{1,0:T(8,128)(2,1)}, bf16[96,3200]{1,0:T(8,128)(2,1)S(1)}, u32[]{:S(2)}, u32[]{:S(2)}) collective-permute-start(bf16[96,3200]{1,0:T(8,128)(2,1)} %get-tuple-element.219.refs_3_.refs_11_.refs_15_), channel_id=1, source_target_pairs={{8,0},{10,2},{12,4},{14,6},{0,8},{2,10},{4,12},{6,14},{24,16},{26,... | collective-permute-start | bytes 1843208 | tf_op jit(solution)/shard_map/ppermute | solution.py:45
  157.6 38.1 %collective-permute-start.44 = (bf16[2,192,1536]{2,1,0:T(8,128)(2,1)}, bf16[2,192,1536]{2,1,0:T(8,128)(2,1)}, u32[]{:S(2)}, u32[]{:S(2)}) collective-permute-start(bf16[2,192,1536]{2,1,0:T(8,128)(2,1)} %get-tuple-element.233.refs_1_), channel_id=1, source_target_pairs={{0,6},{2,4},{4,2},{6,0},{8,10},{10,8},{12,14},{14,12},{16,22},{18,... | collective-permute-start | bytes 3538952 | tf_op jit(solution)/shard_map/ppermute | solution.py:55
  157.8 38.0 %collective-permute-start.45 = (bf16[2,768,384]{2,1,0:T(8,128)(2,1)}, bf16[2,768,384]{2,1,0:T(8,128)(2,1)}, u32[]{:S(2)}, u32[]{:S(2)}) collective-permute-start(bf16[2,768,384]{2,1,0:T(8,128)(2,1)} %get-tuple-element.234.refs_2_), channel_id=1, source_target_pairs={{0,96},{2,98},{4,100},{6,102},{8,40},{10,42},{12,44},{14,46},{16,1... | collective-permute-start | bytes 3538952 | tf_op jit(solution)/shard_map/ppermute | solution.py:55
  191.8 16.4 %collective-permute-start.41 = (bf16[576,256]{1,0:T(8,128)(2,1)}, bf16[576,256]{1,0:T(8,128)(2,1)S(1)}, u32[]{:S(2)}, u32[]{:S(2)}) collective-permute-start(bf16[576,256]{1,0:T(8,128)(2,1)} %get-tuple-element.224), channel_id=1, source_target_pairs={{2,0},{4,2},{6,4},{0,6},{10,8},{12,10},{14,12},{8,14},{18,16},{20,... | collective-permute-start | bytes 884744 | tf_op jit(solution)/shard_map/ppermute | solution.py:45
  194.9 16.7 %collective-permute-start.43 = (bf16[576,256]{1,0:T(8,128)(2,1)}, bf16[576,256]{1,0:T(8,128)(2,1)S(1)}, u32[]{:S(2)}, u32[]{:S(2)}) collective-permute-start(bf16[576,256]{1,0:T(8,128)(2,1)} %get-tuple-element.226), channel_id=1, source_target_pairs={{6,0},{0,2},{2,4},{4,6},{14,8},{8,10},{10,12},{12,14},{22,16},{16,... | collective-permute-start | bytes 884744 | tf_op jit(solution)/shard_map/ppermute | solution.py:45
  263.4 18.2 %collective-permute-start.59 = (bf16[2,192,1536]{2,1,0:T(8,128)(2,1)}, bf16[2,192,1536]{2,1,0:T(8,128)(2,1)S(1)}, u32[]{:S(2)}, u32[]{:S(2)}) collective-permute-start(bf16[2,192,1536]{2,1,0:T(8,128)(2,1)} %get-tuple-element.264), channel_id=1, source_target_pairs={{0,6},{2,4},{4,2},{6,0},{8,10},{10,8},{12,14},{14,12},{16,22},{18,... | collective-permute-start | bytes 3538952 | tf_op jit(solution)/shard_map/ppermute | solution.py:55
  264.0 17.6 %collective-permute-start.60 = (bf16[2,768,384]{2,1,0:T(8,128)(2,1)}, bf16[2,768,384]{2,1,0:T(8,128)(2,1)S(1)}, u32[]{:S(2)}, u32[]{:S(2)}) collective-permute-start(bf16[2,768,384]{2,1,0:T(8,128)(2,1)} %get-tuple-element.265), channel_id=1, source_target_pairs={{0,96},{2,98},{4,100},{6,102},{8,40},{10,42},{12,44},{14,46},{16,1... | collective-permute-start | bytes 3538952 | tf_op jit(solution)/shard_map/ppermute | solution.py:55
  330.4 15.7 %collective-permute-start.68 = (bf16[96,3200]{1,0:T(8,128)(2,1)}, bf16[96,3200]{1,0:T(8,128)(2,1)S(1)}, u32[]{:S(2)}, u32[]{:S(2)}) collective-permute-start(bf16[96,3200]{1,0:T(8,128)(2,1)} %get-tuple-element.292), channel_id=1, source_target_pairs={{0,17},{2,19},{4,21},{6,23},{8,24},{10,26},{12,28},{14,30},{16,1},... | collective-permute-start | bytes 1843208 | tf_op jit(solution)/shard_map/ppermute | solution.py:55
  331.8 16.7 %collective-permute-start.69 = (bf16[96,3200]{1,0:T(8,128)(2,1)}, bf16[96,3200]{1,0:T(8,128)(2,1)S(1)}, u32[]{:S(2)}, u32[]{:S(2)}) collective-permute-start(bf16[96,3200]{1,0:T(8,128)(2,1)} %get-tuple-element.293), channel_id=1, source_target_pairs={{0,17},{2,19},{4,21},{6,23},{8,24},{10,26},{12,28},{14,30},{16,1},... | collective-permute-start | bytes 1843208 | tf_op jit(solution)/shard_map/ppermute | solution.py:55
  350.4 16.4 %collective-permute-start.72 = (bf16[576,256]{1,0:T(8,128)(2,1)S(1)}, bf16[576,256]{1,0:T(8,128)(2,1)S(1)}, u32[]{:S(2)}, u32[]{:S(2)}) collective-permute-start(bf16[576,256]{1,0:T(8,128)(2,1)S(1)} %copy-done.78), channel_id=1, source_target_pairs={{2,0},{4,2},{6,4},{0,6},{10,8},{12,10},{14,12},{8,14},{18,16},{20,... | collective-permute-start | bytes 884744 | tf_op jit(solution)/shard_map/ppermute | solution.py:45
  381.3 30.3 %collective-permute-start.87 = (bf16[2,192,1536]{2,1,0:T(8,128)(2,1)}, bf16[2,192,1536]{2,1,0:T(8,128)(2,1)S(1)}, u32[]{:S(2)}, u32[]{:S(2)}) collective-permute-start(bf16[2,192,1536]{2,1,0:T(8,128)(2,1)} %get-tuple-element.330), channel_id=1, source_target_pairs={{0,6},{2,4},{4,2},{6,0},{8,10},{10,8},{12,14},{14,12},{16,22},{18,... | collective-permute-start | bytes 3538952 | tf_op jit(solution)/shard_map/ppermute | solution.py:55
  381.8 29.8 %collective-permute-start.88 = (bf16[2,768,384]{2,1,0:T(8,128)(2,1)}, bf16[2,768,384]{2,1,0:T(8,128)(2,1)}, u32[]{:S(2)}, u32[]{:S(2)}) collective-permute-start(bf16[2,768,384]{2,1,0:T(8,128)(2,1)} %get-tuple-element.331), channel_id=1, source_target_pairs={{0,96},{2,98},{4,100},{6,102},{8,40},{10,42},{12,44},{14,46},{16,1... | collective-permute-start | bytes 3538952 | tf_op jit(solution)/shard_map/ppermute | solution.py:55
  411.4 25.2 %collective-permute-start.81 = (bf16[96,3200]{1,0:T(8,128)(2,1)}, bf16[96,3200]{1,0:T(8,128)(2,1)}, u32[]{:S(2)}, u32[]{:S(2)}) collective-permute-start(bf16[96,3200]{1,0:T(8,128)(2,1)} %shard_map.195.refs_1_.refs_4_), channel_id=1, source_target_pairs={{0,16},{2,18},{4,20},{6,22},{8,25},{10,27},{12,29},{14,31},{16,0},... | collective-permute-start | bytes 1843208 | tf_op jit(solution)/shard_map/ppermute | solution.py:55
  417.8 18.9 %collective-permute-start.80 = (bf16[96,3200]{1,0:T(8,128)(2,1)S(1)}, bf16[96,3200]{1,0:T(8,128)(2,1)S(1)}, u32[]{:S(2)}, u32[]{:S(2)}) collective-permute-start(bf16[96,3200]{1,0:T(8,128)(2,1)S(1)} %copy-done.62), channel_id=1, source_target_pairs={{0,17},{2,19},{4,21},{6,23},{8,24},{10,26},{12,28},{14,30},{16,1},... | collective-permute-start | bytes 1843208 | tf_op jit(solution)/shard_map/ppermute | solution.py:55
  444.7 16.3 %collective-permute-start.82 = (bf16[2,4,304,128]{3,2,1,0:T(8,128)(2,1)}, bf16[2,4,304,128]{3,2,1,0:T(8,128)(2,1)S(1)}, u32[]{:S(2)}, u32[]{:S(2)}) collective-permute-start(bf16[2,4,304,128]{3,2,1,0:T(8,128)(2,1)} %get-tuple-element.322), channel_id=1, source_target_pairs={{0,6},{2,4},{4,2},{6,0},{8,10},{10,8},{12,14},{14,12},{16,22},{18,... | collective-permute-start | bytes 1867784 | tf_op jit(solution)/shard_map/ppermute | solution.py:55
  449.0 15.3 %collective-permute-start.93 = (bf16[4,96,384]{2,1,0:T(8,128)(2,1)}, bf16[4,96,384]{2,1,0:T(8,128)(2,1)S(1)}, u32[]{:S(2)}, u32[]{:S(2)}) collective-permute-start(bf16[4,96,384]{2,1,0:T(8,128)(2,1)} %get-tuple-element.342), channel_id=1, source_target_pairs={{0,32},{2,34},{4,36},{6,38},{8,104},{10,106},{12,108},{14,110},{16... | collective-permute-start | bytes 884744 | tf_op jit(solution)/shard_map/ppermute | solution.py:55
  449.0 15.3 %collective-permute-start.94 = (bf16[4,96,384]{2,1,0:T(8,128)(2,1)}, bf16[4,96,384]{2,1,0:T(8,128)(2,1)S(1)}, u32[]{:S(2)}, u32[]{:S(2)}) collective-permute-start(bf16[4,96,384]{2,1,0:T(8,128)(2,1)} %get-tuple-element.344), channel_id=1, source_target_pairs={{0,2},{2,0},{4,6},{6,4},{8,14},{10,12},{12,10},{14,8},{16,18},{18,... | collective-permute-start | bytes 884744 | tf_op jit(solution)/shard_map/ppermute | solution.py:55
  (179 other events, 1037.5 us)
